TPU v7x, 256 devices: a whole 4x4x8 slice. The times are simulated.
256 devices in a mesh: ctx: 16 (over z_hi, x), tp: 2 (over core), ep: 8 (over y, z_lo).
Axes of the slice: x: 4, y: 4, z: 8 (z_hi: 4, z_lo: 2; z = z_hi * 2 + z_lo), core: 2. Of those that a mesh axis runs over, the one named last changes fastest.
Arguments:
- hidden: bfloat16 [2048, 3584], P('ctx'), may hold values from -40 to 40
- grad_out: bfloat16 [2048, 3584], P('ctx'), may hold values from -6 to 6
- gain: float32 [3584], replicated, may hold values from 0.5 to 1.5
- dense_gate: bfloat16 [2432, 3584], P(('tp', 'ep')), may hold values from -0.09375 to 0.09375
- dense_up: bfloat16 [2432, 3584], P(('tp', 'ep')), may hold values from -0.09375 to 0.09375
- dense_down: bfloat16 [2432, 3584], P(('tp', 'ep')), may hold values from -0.125 to 0.125
- expert_gate: bfloat16 [16, 3840, 3584], P('ctx', ('tp', 'ep')), may hold values from -0.09375 to 0.09375
- expert_up: bfloat16 [16, 3840, 3584], P('ctx', ('tp', 'ep')), may hold values from -0.09375 to 0.09375
- expert_down: bfloat16 [16, 3840, 3584], P('ctx', ('tp', 'ep')), may hold values from -0.09375 to 0.09375
- out_proj: bfloat16 [4096, 3584], P(('tp', 'ep')), may hold values from -0.09375 to 0.09375
- queries: bfloat16 [2048, 4096], P('ctx', ('tp', 'ep')), may hold values from -12 to 12
- keys: bfloat16 [2048, 4096], P('ctx', ('tp', 'ep')), may hold values from -12 to 12
- values: bfloat16 [2048, 4096], P('ctx', ('tp', 'ep')), may hold values from -6 to 6
- route_ids: int32 [2048, 2], P('ctx'), may hold values from 0 to 15, all different within a row; in each aligned block of 128 rows (0 to 127, 128 to 255, ...) at most 20 rows name the same one
- route_weights: float32 [2048, 2], P('ctx'), may hold values from 0.2 to 1
Outputs:
- grad_hidden: bfloat16 [2048, 3584], P('ctx')
- grad_queries: bfloat16 [2048, 4096], P('ctx', ('tp', 'ep'))
- grad_keys: bfloat16 [2048, 4096], P('ctx', ('tp', 'ep'))
- grad_values: bfloat16 [2048, 4096], P('ctx', ('tp', 'ep'))
Inputs may be any that keep to these rules, and one draw needn't show every extreme that they name: `route_ids`: the two ids of a token differ. In each aligned block of 128 tokens no expert is named by more than 20 routed rows, a bound that some block reaches.
All inputs are finite; a program needn't handle non-finite values.
Results may differ from a plain program's by a relative error of at most 0.03.
Values may be sent and summed in bfloat16 or wider, within the bound.
No kernel may reach another device: no remote copies, remote signals or barrier semaphores. Data moves between devices by JAX's collectives and lax.ppermute only.
A program may use at most 128 MiB of HBM per device.

v0:
```python
import jax
import jax.numpy as jnp
from jax import lax
from jax.sharding import PartitionSpec as P

HEAD_DIM = 128


NEG_FILL = -1e30
EPSILON = 1e-05


def shifted(shard, axis, by):
    devices = lax.axis_size(axis)
    return lax.ppermute(shard, axis, [(i, (i + by) % devices) for i in range(devices)])


def contract_last(left_rows, right_rows):
    return lax.dot_general(
        left_rows, right_rows, (((1,), (1,)), ((), ())), preferred_element_type=jnp.float32
    )


def swiglu_grad(inputs, upstream, w_gate, w_up, w_down):
    gate_pre = contract_last(inputs, w_gate)
    up_pre = contract_last(inputs, w_up)
    back_grad = contract_last(upstream, w_down)
    sigmoid_gate = jax.nn.sigmoid(gate_pre)
    grad_gate = (
        back_grad * up_pre * sigmoid_gate * (1.0 + gate_pre * (1.0 - sigmoid_gate))
    ).astype(jnp.bfloat16)
    grad_upper = (back_grad * gate_pre * sigmoid_gate).astype(jnp.bfloat16)
    return jnp.dot(grad_gate, w_gate, preferred_element_type=jnp.float32) + jnp.dot(
        grad_upper, w_up, preferred_element_type=jnp.float32
    )


def head_scores(left_heads, right_heads):
    return jnp.einsum("qhd,khd->hqk", left_heads, right_heads, preferred_element_type=jnp.float32)


def forward_piece(running, pieces, query_heads, upstream_heads, query_pos):
    run_max, run_sum, run_dot = running
    key_count = pieces[0].shape[0]
    key_heads = pieces[0].reshape(key_count, -1, HEAD_DIM)
    value_heads = pieces[1].reshape(key_count, -1, HEAD_DIM)
    key_pos = lax.iota(jnp.int32, key_count)
    allowed = key_pos[None, None, :] <= query_pos[None, :, None]
    scores = jnp.where(allowed, head_scores(query_heads, key_heads) * HEAD_DIM ** (-0.5), NEG_FILL)
    new_max = jnp.maximum(run_max, jnp.max(scores, axis=2))
    weights = jnp.where(allowed, jnp.exp(scores - new_max[:, :, None]), 0.0)
    grad_probs = head_scores(upstream_heads, value_heads)
    return (new_max, jnp.sum(weights, axis=2), jnp.sum(weights * grad_probs, axis=2))


def backward_terms(
    query_heads, upstream_heads, key_heads, value_heads, log_norm, delta_row, allowed
):
    score_scale = HEAD_DIM ** (-0.5)
    scores = head_scores(query_heads, key_heads) * score_scale
    probs = jnp.where(allowed, jnp.exp(scores - log_norm[:, :, None]), 0.0)
    grad_scores = probs * (head_scores(upstream_heads, value_heads) - delta_row[:, :, None])
    probs_half = probs.astype(jnp.bfloat16)
    grad_half = grad_scores.astype(jnp.bfloat16)
    grad_values = jnp.einsum(
        "hqk,qhd->khd", probs_half, upstream_heads, preferred_element_type=jnp.float32
    )
    grad_keys = (
        jnp.einsum("hqk,qhd->khd", grad_half, query_heads, preferred_element_type=jnp.float32)
        * score_scale
    )
    grad_queries = (
        jnp.einsum("hqk,khd->qhd", grad_half, key_heads, preferred_element_type=jnp.float32)
        * score_scale
    )
    return (grad_queries, grad_keys, grad_values)


def body(
    hidden,
    grad_out,
    gain,
    dense_gate,
    dense_up,
    dense_down,
    expert_gate,
    expert_up,
    expert_down,
    out_proj,
    queries,
    keys,
    values,
    route_ids,
    route_weights,
):
    row_count = hidden.shape[0]
    feat_width = hidden.shape[1]
    pick_count = route_ids.shape[1]
    hidden_f = hidden.astype(jnp.float32)
    inverse = lax.rsqrt(jnp.mean(hidden_f * hidden_f, axis=1, keepdims=True) + EPSILON)
    normed = hidden_f * inverse
    mixed_in = (normed * gain).astype(jnp.bfloat16)
    dense_part = swiglu_grad(mixed_in, grad_out, dense_gate, dense_up, dense_down)
    expert_count = lax.axis_size("ctx")
    capacity = 5 * row_count // (2 * expert_count)
    flat_ids = route_ids.reshape(-1)
    hits = (flat_ids[:, None] == lax.iota(jnp.int32, expert_count)[None, :]).astype(jnp.int32)
    earlier = jnp.cumsum(hits, axis=0) - hits
    slots = jnp.sum(earlier * hits, axis=1)
    places = flat_ids * capacity + slots
    owners = lax.iota(jnp.int32, pick_count * row_count) // pick_count
    token_of = jnp.full((expert_count * capacity,), row_count, jnp.int32).at[places].set(owners)
    weight_of = (
        jnp.zeros((expert_count * capacity,), jnp.float32).at[places].set(route_weights.reshape(-1))
    )
    present = token_of < row_count
    picked = jnp.minimum(token_of, row_count - 1)
    send_in = jnp.where(present[:, None], mixed_in[picked], jnp.zeros((), jnp.bfloat16)).reshape(
        expert_count, capacity, feat_width
    )
    send_grad = (
        (grad_out[picked].astype(jnp.float32) * weight_of[:, None])
        .astype(jnp.bfloat16)
        .reshape(expert_count, capacity, feat_width)
    )
    inputs = lax.all_to_all(send_in, "ctx", split_axis=0, concat_axis=0, tiled=True)
    upstream = lax.all_to_all(send_grad, "ctx", split_axis=0, concat_axis=0, tiled=True)
    slot_count = inputs.shape[1]
    partial_value = swiglu_grad(
        inputs.reshape(-1, feat_width),
        upstream.reshape(-1, feat_width),
        expert_gate[0],
        expert_up[0],
        expert_down[0],
    )
    partial_value = partial_value.reshape(expert_count, slot_count, feat_width)
    partial_value = lax.psum(partial_value, ("tp", "ep"))
    returned = lax.all_to_all(partial_value, "ctx", split_axis=0, concat_axis=0, tiled=True)
    routed = (
        returned.reshape(expert_count * capacity, feat_width)[places]
        .reshape(row_count, pick_count, feat_width)
        .sum(axis=1)
    )
    total_grad = lax.psum(dense_part, ("tp", "ep")) + routed
    scaled_grad = total_grad * gain
    grad_hidden = (
        grad_out.astype(jnp.float32)
        + inverse * (scaled_grad - normed * jnp.mean(scaled_grad * normed, axis=1, keepdims=True))
    ).astype(jnp.bfloat16)
    grad_heads = contract_last(grad_hidden, out_proj).astype(jnp.bfloat16)
    head_width = queries.shape[1]
    query_heads = queries.reshape(row_count, -1, HEAD_DIM)
    upstream_heads = grad_heads.reshape(row_count, -1, HEAD_DIM)
    heads_here = query_heads.shape[1]
    my_block = lax.axis_index("ctx")
    block_count = lax.axis_size("ctx")
    query_pos = my_block * row_count + lax.iota(jnp.int32, row_count)
    start_state = (
        jnp.full((heads_here, row_count), NEG_FILL, jnp.float32),
        jnp.zeros((heads_here, row_count), jnp.float32),
        jnp.zeros((heads_here, row_count), jnp.float32),
    )
    run_max, run_sum, run_dot = forward_piece(
        start_state,
        (
            lax.all_gather(keys, "ctx", axis=0, tiled=True),
            lax.all_gather(values, "ctx", axis=0, tiled=True),
        ),
        query_heads,
        upstream_heads,
        query_pos,
    )
    log_norm = run_max + jnp.log(run_sum)
    delta_row = run_dot / run_sum

    def cycle_visit(cycle_state, hop_index):
        keys_now, values_now, sum_keys, sum_values, sum_queries = cycle_state
        held_block = (my_block + hop_index) % block_count
        key_pos = held_block * row_count + lax.iota(jnp.int32, row_count)
        allowed = key_pos[None, None, :] <= query_pos[None, :, None]
        term_queries, term_keys, term_values = backward_terms(
            query_heads,
            upstream_heads,
            keys_now.reshape(row_count, -1, HEAD_DIM),
            values_now.reshape(row_count, -1, HEAD_DIM),
            log_norm,
            delta_row,
            allowed,
        )
        sum_keys, sum_values = shifted(
            (
                sum_keys + term_keys.reshape(row_count, head_width),
                sum_values + term_values.reshape(row_count, head_width),
            ),
            "ctx",
            -1,
        )
        return (
            keys_now,
            values_now,
            sum_keys,
            sum_values,
            sum_queries + term_queries.reshape(row_count, head_width),
        )

    def cycle_loop(hop_index, cycle_state):
        cycle_state = cycle_visit(cycle_state, hop_index)
        keys_next, values_next = shifted((cycle_state[0], cycle_state[1]), "ctx", -1)
        return (keys_next, values_next, cycle_state[2], cycle_state[3], cycle_state[4])

    zero_heads = jnp.zeros((row_count, head_width), jnp.float32)
    cycle_state = lax.fori_loop(
        0, block_count - 1, cycle_loop, (keys, values, zero_heads, zero_heads, zero_heads)
    )
    cycle_state = cycle_visit(cycle_state, block_count - 1)
    return (
        grad_hidden,
        cycle_state[4].astype(jnp.bfloat16),
        cycle_state[2].astype(jnp.bfloat16),
        cycle_state[3].astype(jnp.bfloat16),
    )


def solution(mesh):
    return jax.shard_map(
        body,
        mesh=mesh,
        in_specs=(
            P("ctx", None),
            P("ctx", None),
            P(),
            P(("tp", "ep"), None),
            P(("tp", "ep"), None),
            P(("tp", "ep"), None),
            P("ctx", ("tp", "ep"), None),
            P("ctx", ("tp", "ep"), None),
            P("ctx", ("tp", "ep"), None),
            P(("tp", "ep"), None),
            P("ctx", ("tp", "ep")),
            P("ctx", ("tp", "ep")),
            P("ctx", ("tp", "ep")),
            P("ctx", None),
            P("ctx", None),
        ),
        out_specs=(
            P("ctx", None),
            P("ctx", ("tp", "ep")),
            P("ctx", ("tp", "ep")),
            P("ctx", ("tp", "ep")),
        ),
        check_vma=False,
    )
```

profile of v0, /device:TPU:32, one launch (start us, length us, event | category | flops | bytes accessed | tf_op | source)
XLA Modules:
  0.0 1087.0 jit_solution(18247166113199774174)
XLA Ops:
  29.0 10.2 all-to-all-start.1
  39.2 8.8 gather_fusion
  59.1 45.9 %all-to-all-done.1 = bf16[16,20,3584]{2,1,0:T(8,128)(2,1)} async-done(((bf16[16,20,3584]{2,1,0:T(8,128)(2,1)}), bf16[16,20,3584]{2,1,0:T(8,128)(2,1)}, u32[]{:S(2)}, u32[]{:S(2)}) %all-to-all-start.1) | async-done | bytes 2293792 | tf_op jit(solution)/shard_map/all_to_all | solution.py:126
  127.8 49.0 %all-to-all-done = bf16[16,20,3584]{2,1,0:T(8,128)(2,1)} async-done(((bf16[16,20,3584]{2,1,0:T(8,128)(2,1)}), bf16[16,20,3584]{2,1,0:T(8,128)(2,1)}, u32[]{:S(2)}, u32[]{:S(2)}) %all-to-all-start) | async-done | bytes 2293792 | tf_op jit(solution)/shard_map/all_to_all | solution.py:127
  184.7 7.0 fusion.25
  202.4 325.3 %all-reduce.3.cloned.1.call-done = (f32[128,3584]{1,0:T(8,128)}, f32[16,20,3584]{2,1,0:T(8,128)}) async-done(((f32[128,3584]{1,0:T(8,128)}, f32[16,20,3584]{2,1,0:T(8,128)}), (f32[128,3584]{1,0:T(8,128)}, f32[16,20,3584]{2,1,0:T(8,128)})) %all-reduce.3.cloned.1.call-update) | async-done | bytes 6422544 | tf_op jit(solution)/shard_map/psum | solution.py:144
  527.8 9.7 all-to-all-start.2
  539.7 140.2 %all-gather.3.cloned.1.call-done = bf16[2048,256]{0,1:T(8,128)(2,1)} async-done(((bf16[128,256]{0,1:T(8,128)(2,1)}), bf16[2048,256]{0,1:T(8,128)(2,1)}) %all-gather.3.cloned.1.call-update) | async-done | bytes 1048592 | tf_op jit(solution)/shard_map/all_gather | solution.py:166
  689.3 7.6 gather_fusion.2
  702.4 7.7 reduce_sum.59
  716.1 20.7 %all-gather.5.cloned.1.call-done = bf16[2048,256]{0,1:T(8,128)(2,1)} async-done(((bf16[128,256]{0,1:T(8,128)(2,1)}), bf16[2048,256]{0,1:T(8,128)(2,1)}) %all-gather.5.cloned.1.call-update) | async-done | bytes 1048592 | tf_op jit(solution)/shard_map/all_gather | solution.py:167
  739.7 328.3 %while.24 = (s32[]{:T(128)}, bf16[128,256]{0,1:T(8,128)(2,1)S(1)}, bf16[128,256]{1,0:T(8,128)(2,1)S(1)}, f32[128,256]{0,1:T(8,128)S(1)}, f32[128,256]{0,1:T(8,12...) while((s32[]{:T(128)}, bf16[128,256]{0,1:T(8,128)(2,1)S(1)}, ...), condition=%wide.region_14.15_spmd.clone, body=%wide.region_13.14_spmd.clone.sunk | while | flops 42385680 | bytes 5018068 | solution.py:212
  751.8 8.0 collective-permute-done.3
  759.7 6.9 collective-permute-start
  771.0 9.1 collective-permute-done.2
  782.9 6.8 collective-permute-start
  799.9 11.1 %collective-permute-done.3 = f32[128,256]{0,1:T(8,128)S(1)} collective-permute-done((f32[128,256]{0,1:T(8,128)S(1)}, f32[128,256]{0,1:T(8,128)S(1)}, u32[]{:S(2)}, u32[]{:S(2)}) %collective-permute-start.3) | collective-permute-done | bytes 131104 | tf_op jit(solution)/shard_map/while/body/eval_jaxpr/ppermute | solution.py:15
  811.0 6.9 collective-permute-start
  820.5 9.6 collective-permute-done.1
  835.2 6.7 collective-permute-start
  851.9 11.2 %collective-permute-done.3 = f32[128,256]{0,1:T(8,128)S(1)} collective-permute-done((f32[128,256]{0,1:T(8,128)S(1)}, f32[128,256]{0,1:T(8,128)S(1)}, u32[]{:S(2)}, u32[]{:S(2)}) %collective-permute-start.3) | collective-permute-done | bytes 131104 | tf_op jit(solution)/shard_map/while/body/eval_jaxpr/ppermute | solution.py:15
  863.1 6.7 collective-permute-start
  881.4 11.1 %collective-permute-done.3 = f32[128,256]{0,1:T(8,128)S(1)} collective-permute-done((f32[128,256]{0,1:T(8,128)S(1)}, f32[128,256]{0,1:T(8,128)S(1)}, u32[]{:S(2)}, u32[]{:S(2)}) %collective-permute-start.3) | collective-permute-done | bytes 131104 | tf_op jit(solution)/shard_map/while/body/eval_jaxpr/ppermute | solution.py:15
  892.6 6.7 collective-permute-start
  901.0 7.3 collective-permute-done
  912.6 11.1 %collective-permute-done.3 = f32[128,256]{0,1:T(8,128)S(1)} collective-permute-done((f32[128,256]{0,1:T(8,128)S(1)}, f32[128,256]{0,1:T(8,128)S(1)}, u32[]{:S(2)}, u32[]{:S(2)}) %collective-permute-start.3) | collective-permute-done | bytes 131104 | tf_op jit(solution)/shard_map/while/body/eval_jaxpr/ppermute | solution.py:15
  923.8 6.7 collective-permute-start
  941.6 8.5 collective-permute-done.3
  950.2 6.7 collective-permute-start
  961.8 10.1 collective-permute-done.2
  974.5 6.7 collective-permute-start
  998.1 6.7 collective-permute-start
  (459 shorter events, 272.8 us)
Async XLA Ops:
  29.0 76.0 %all-to-all-start.1 = ((bf16[16,20,3584]{2,1,0:T(8,128)(2,1)}), bf16[16,20,3584]{2,1,0:T(8,128)(2,1)}, u32[]{:S(2)}, u32[]{:S(2)}) async-start(bf16[16,20,3584]{2,1,0:T(8,128)(2,1)} %broadcast_select_fusion), calls=%async_computation.1 | async-start | bytes 5505024 | tf_op jit(solution)/shard_map/all_to_all | solution.py:126
  105.0 71.8 %all-to-all-start = ((bf16[16,20,3584]{2,1,0:T(8,128)(2,1)}), bf16[16,20,3584]{2,1,0:T(8,128)(2,1)}, u32[]{:S(2)}, u32[]{:S(2)}) async-start(bf16[16,20,3584]{2,1,0:T(8,128)(2,1)} %multiply_convert_fusion), calls=%async_computation | async-start | bytes 5505024 | tf_op jit(solution)/shard_map/all_to_all | solution.py:127
  110.2 417.6 %all-reduce.3.cloned.1.call-start = ((), (), s32[]{:S(2)}) async-start(), calls=%async_computation.5 | async-start | bytes 14680064 | tf_op jit(solution)/shard_map/psum | solution.py:144
  527.8 156.0 %all-to-all-start.2 = ((f32[16,20,3584]{2,1,0:T(8,128)}), f32[16,20,3584]{2,1,0:T(8,128)}, u32[]{:S(2)}, u32[]{:S(2)}) async-start(f32[16,20,3584]{2,1,0:T(8,128)} %get-tuple-element.395), calls=%async_computation.2 | async-start | bytes 11010048 | tf_op jit(solution)/shard_map/all_to_all | solution.py:138
  537.5 142.3 %all-gather.3.cloned.1.call-start = ((), (), s32[]{:S(2)}) async-start(), calls=%async_computation.3 | async-start | bytes 1114112 | tf_op jit(solution)/shard_map/all_gather | solution.py:166
  538.3 198.4 %all-gather.5.cloned.1.call-start = ((), (), s32[]{:S(2)}) async-start(), calls=%async_computation.4 | async-start | bytes 1114112 | tf_op jit(solution)/shard_map/all_gather | solution.py:167
  746.2 13.6 %collective-permute-start.3 = (f32[128,256]{0,1:T(8,128)S(1)}, f32[128,256]{0,1:T(8,128)S(1)}, u32[]{:S(2)}, u32[]{:S(2)}) collective-permute-start(f32[128,256]{0,1:T(8,128)S(1)} %bitcast_add_fusion.8), channel_id=1, source_target_pairs={{0,240},{16,0},{32,16},{48,32},{64,48},{80,64},{96,80},{112,96},{1... | collective-permute-start | bytes 393224 | tf_op jit(solution)/shard_map/while/body/eval_jaxpr/ppermute | solution.py:15
  759.7 9.8 collective-permute-start
  767.7 12.3 %collective-permute-start.2 = (f32[128,256]{0,1:T(8,128)S(1)}, f32[128,256]{0,1:T(8,128)S(1)}, u32[]{:S(2)}, u32[]{:S(2)}) collective-permute-start(f32[128,256]{0,1:T(8,128)S(1)} %bitcast_add_fusion.7), channel_id=1, source_target_pairs={{0,240},{16,0},{32,16},{48,32},{64,48},{80,64},{96,80},{112,96},{1... | collective-permute-start | bytes 393224 | tf_op jit(solution)/shard_map/while/body/eval_jaxpr/ppermute | solution.py:15
  768.0 14.9 %collective-permute-start.3 = (f32[128,256]{0,1:T(8,128)S(1)}, f32[128,256]{0,1:T(8,128)S(1)}, u32[]{:S(2)}, u32[]{:S(2)}) collective-permute-start(f32[128,256]{0,1:T(8,128)S(1)} %bitcast_add_fusion.8), channel_id=1, source_target_pairs={{0,240},{16,0},{32,16},{48,32},{64,48},{80,64},{96,80},{112,96},{1... | collective-permute-start | bytes 393224 | tf_op jit(solution)/shard_map/while/body/eval_jaxpr/ppermute | solution.py:15
  782.9 12.8 %collective-permute-start = (bf16[128,256]{0,1:T(8,128)(2,1)S(1)}, bf16[128,256]{0,1:T(8,128)(2,1)S(1)}, u32[]{:S(2)}, u32[]{:S(2)}) collective-permute-start(bf16[128,256]{0,1:T(8,128)(2,1)S(1)} %copy.125), channel_id=1, source_target_pairs={{0,240},{16,0},{32,16},{48,32},{64,48},{80,64},{96,80},{112,96},{1... | collective-permute-start | bytes 196616 | tf_op jit(solution)/shard_map/while/body/eval_jaxpr/ppermute | solution.py:15
  791.0 20.1 %collective-permute-start.3 = (f32[128,256]{0,1:T(8,128)S(1)}, f32[128,256]{0,1:T(8,128)S(1)}, u32[]{:S(2)}, u32[]{:S(2)}) collective-permute-start(f32[128,256]{0,1:T(8,128)S(1)} %bitcast_add_fusion.8), channel_id=1, source_target_pairs={{0,240},{16,0},{32,16},{48,32},{64,48},{80,64},{96,80},{112,96},{1... | collective-permute-start | bytes 393224 | tf_op jit(solution)/shard_map/while/body/eval_jaxpr/ppermute | solution.py:15
  817.9 12.2 %collective-permute-start.1 = (bf16[128,256]{1,0:T(8,128)(2,1)S(1)}, bf16[128,256]{1,0:T(8,128)(2,1)S(1)}, u32[]{:S(2)}, u32[]{:S(2)}) collective-permute-start(bf16[128,256]{1,0:T(8,128)(2,1)S(1)} %copy.126), channel_id=1, source_target_pairs={{0,240},{16,0},{32,16},{48,32},{64,48},{80,64},{96,80},{112,96},{1... | collective-permute-start | bytes 196616 | tf_op jit(solution)/shard_map/while/body/eval_jaxpr/ppermute | solution.py:15
  818.9 14.0 %collective-permute-start.2 = (f32[128,256]{0,1:T(8,128)S(1)}, f32[128,256]{0,1:T(8,128)S(1)}, u32[]{:S(2)}, u32[]{:S(2)}) collective-permute-start(f32[128,256]{0,1:T(8,128)S(1)} %bitcast_add_fusion.7), channel_id=1, source_target_pairs={{0,240},{16,0},{32,16},{48,32},{64,48},{80,64},{96,80},{112,96},{1... | collective-permute-start | bytes 393224 | tf_op jit(solution)/shard_map/while/body/eval_jaxpr/ppermute | solution.py:15
  819.2 16.0 %collective-permute-start.3 = (f32[128,256]{0,1:T(8,128)S(1)}, f32[128,256]{0,1:T(8,128)S(1)}, u32[]{:S(2)}, u32[]{:S(2)}) collective-permute-start(f32[128,256]{0,1:T(8,128)S(1)} %bitcast_add_fusion.8), channel_id=1, source_target_pairs={{0,240},{16,0},{32,16},{48,32},{64,48},{80,64},{96,80},{112,96},{1... | collective-permute-start | bytes 393224 | tf_op jit(solution)/shard_map/while/body/eval_jaxpr/ppermute | solution.py:15
  835.2 12.4 %collective-permute-start = (bf16[128,256]{0,1:T(8,128)(2,1)S(1)}, bf16[128,256]{0,1:T(8,128)(2,1)S(1)}, u32[]{:S(2)}, u32[]{:S(2)}) collective-permute-start(bf16[128,256]{0,1:T(8,128)(2,1)S(1)} %copy.125), channel_id=1, source_target_pairs={{0,240},{16,0},{32,16},{48,32},{64,48},{80,64},{96,80},{112,96},{1... | collective-permute-start | bytes 196616 | tf_op jit(solution)/shard_map/while/body/eval_jaxpr/ppermute | solution.py:15
  843.2 19.9 %collective-permute-start.3 = (f32[128,256]{0,1:T(8,128)S(1)}, f32[128,256]{0,1:T(8,128)S(1)}, u32[]{:S(2)}, u32[]{:S(2)}) collective-permute-start(f32[128,256]{0,1:T(8,128)S(1)} %bitcast_add_fusion.8), channel_id=1, source_target_pairs={{0,240},{16,0},{32,16},{48,32},{64,48},{80,64},{96,80},{112,96},{1... | collective-permute-start | bytes 393224 | tf_op jit(solution)/shard_map/while/body/eval_jaxpr/ppermute | solution.py:15
  863.1 14.1 %collective-permute-start = (bf16[128,256]{0,1:T(8,128)(2,1)S(1)}, bf16[128,256]{0,1:T(8,128)(2,1)S(1)}, u32[]{:S(2)}, u32[]{:S(2)}) collective-permute-start(bf16[128,256]{0,1:T(8,128)(2,1)S(1)} %copy.125), channel_id=1, source_target_pairs={{0,240},{16,0},{32,16},{48,32},{64,48},{80,64},{96,80},{112,96},{1... | collective-permute-start | bytes 196616 | tf_op jit(solution)/shard_map/while/body/eval_jaxpr/ppermute | solution.py:15
  870.8 10.6 collective-permute-start.2
  871.1 21.4 %collective-permute-start.3 = (f32[128,256]{0,1:T(8,128)S(1)}, f32[128,256]{0,1:T(8,128)S(1)}, u32[]{:S(2)}, u32[]{:S(2)}) collective-permute-start(f32[128,256]{0,1:T(8,128)S(1)} %bitcast_add_fusion.8), channel_id=1, source_target_pairs={{0,240},{16,0},{32,16},{48,32},{64,48},{80,64},{96,80},{112,96},{1... | collective-permute-start | bytes 393224 | tf_op jit(solution)/shard_map/while/body/eval_jaxpr/ppermute | solution.py:15
  892.6 15.8 %collective-permute-start = (bf16[128,256]{0,1:T(8,128)(2,1)S(1)}, bf16[128,256]{0,1:T(8,128)(2,1)S(1)}, u32[]{:S(2)}, u32[]{:S(2)}) collective-permute-start(bf16[128,256]{0,1:T(8,128)(2,1)S(1)} %copy.125), channel_id=1, source_target_pairs={{0,240},{16,0},{32,16},{48,32},{64,48},{80,64},{96,80},{112,96},{1... | collective-permute-start | bytes 196616 | tf_op jit(solution)/shard_map/while/body/eval_jaxpr/ppermute | solution.py:15
  899.3 10.5 collective-permute-start.1
  900.3 12.3 %collective-permute-start.2 = (f32[128,256]{0,1:T(8,128)S(1)}, f32[128,256]{0,1:T(8,128)S(1)}, u32[]{:S(2)}, u32[]{:S(2)}) collective-permute-start(f32[128,256]{0,1:T(8,128)S(1)} %bitcast_add_fusion.7), channel_id=1, source_target_pairs={{0,240},{16,0},{32,16},{48,32},{64,48},{80,64},{96,80},{112,96},{1... | collective-permute-start | bytes 393224 | tf_op jit(solution)/shard_map/while/body/eval_jaxpr/ppermute | solution.py:15
  900.6 23.2 %collective-permute-start.3 = (f32[128,256]{0,1:T(8,128)S(1)}, f32[128,256]{0,1:T(8,128)S(1)}, u32[]{:S(2)}, u32[]{:S(2)}) collective-permute-start(f32[128,256]{0,1:T(8,128)S(1)} %bitcast_add_fusion.8), channel_id=1, source_target_pairs={{0,240},{16,0},{32,16},{48,32},{64,48},{80,64},{96,80},{112,96},{1... | collective-permute-start | bytes 393224 | tf_op jit(solution)/shard_map/while/body/eval_jaxpr/ppermute | solution.py:15
  923.8 13.6 %collective-permute-start = (bf16[128,256]{0,1:T(8,128)(2,1)S(1)}, bf16[128,256]{0,1:T(8,128)(2,1)S(1)}, u32[]{:S(2)}, u32[]{:S(2)}) collective-permute-start(bf16[128,256]{0,1:T(8,128)(2,1)S(1)} %copy.125), channel_id=1, source_target_pairs={{0,240},{16,0},{32,16},{48,32},{64,48},{80,64},{96,80},{112,96},{1... | collective-permute-start | bytes 196616 | tf_op jit(solution)/shard_map/while/body/eval_jaxpr/ppermute | solution.py:15
  931.5 10.2 collective-permute-start.2
  931.8 18.4 %collective-permute-start.3 = (f32[128,256]{0,1:T(8,128)S(1)}, f32[128,256]{0,1:T(8,128)S(1)}, u32[]{:S(2)}, u32[]{:S(2)}) collective-permute-start(f32[128,256]{0,1:T(8,128)S(1)} %bitcast_add_fusion.8), channel_id=1, source_target_pairs={{0,240},{16,0},{32,16},{48,32},{64,48},{80,64},{96,80},{112,96},{1... | collective-permute-start | bytes 393224 | tf_op jit(solution)/shard_map/while/body/eval_jaxpr/ppermute | solution.py:15
  957.8 14.1 %collective-permute-start.2 = (f32[128,256]{0,1:T(8,128)S(1)}, f32[128,256]{0,1:T(8,128)S(1)}, u32[]{:S(2)}, u32[]{:S(2)}) collective-permute-start(f32[128,256]{0,1:T(8,128)S(1)} %bitcast_add_fusion.7), channel_id=1, source_target_pairs={{0,240},{16,0},{32,16},{48,32},{64,48},{80,64},{96,80},{112,96},{1... | collective-permute-start | bytes 393224 | tf_op jit(solution)/shard_map/while/body/eval_jaxpr/ppermute | solution.py:15
  958.2 16.3 %collective-permute-start.3 = (f32[128,256]{0,1:T(8,128)S(1)}, f32[128,256]{0,1:T(8,128)S(1)}, u32[]{:S(2)}, u32[]{:S(2)}) collective-permute-start(f32[128,256]{0,1:T(8,128)S(1)} %bitcast_add_fusion.8), channel_id=1, source_target_pairs={{0,240},{16,0},{32,16},{48,32},{64,48},{80,64},{96,80},{112,96},{1... | collective-permute-start | bytes 393224 | tf_op jit(solution)/shard_map/while/body/eval_jaxpr/ppermute | solution.py:15
  974.5 13.8 %collective-permute-start = (bf16[128,256]{0,1:T(8,128)(2,1)S(1)}, bf16[128,256]{0,1:T(8,128)(2,1)S(1)}, u32[]{:S(2)}, u32[]{:S(2)}) collective-permute-start(bf16[128,256]{0,1:T(8,128)(2,1)S(1)} %copy.125), channel_id=1, source_target_pairs={{0,240},{16,0},{32,16},{48,32},{64,48},{80,64},{96,80},{112,96},{1... | collective-permute-start | bytes 196616 | tf_op jit(solution)/shard_map/while/body/eval_jaxpr/ppermute | solution.py:15
  982.2 10.3 collective-permute-start.2
  982.5 15.5 %collective-permute-start.3 = (f32[128,256]{0,1:T(8,128)S(1)}, f32[128,256]{0,1:T(8,128)S(1)}, u32[]{:S(2)}, u32[]{:S(2)}) collective-permute-start(f32[128,256]{0,1:T(8,128)S(1)} %bitcast_add_fusion.8), channel_id=1, source_target_pairs={{0,240},{16,0},{32,16},{48,32},{64,48},{80,64},{96,80},{112,96},{1... | collective-permute-start | bytes 393224 | tf_op jit(solution)/shard_map/while/body/eval_jaxpr/ppermute | solution.py:15
  (57 other events, 1088.0 us)
Sparse Core Ops, SparseCore 0:
  202.6 325.1 all-reduce.2
Sparse Core Ops, SparseCore 1:
  541.0 138.8 all-gather.2
  682.7 54.0 all-gather.4
where the time goes:
time: 1090 us
  waiting for transfers between devices  793 us (73%)
  starting transfers between devices  129 us (12%)
  local copies, waits for them, and re-layouts  70.2 us (6%)
  matrix products  50.4 us (5%)
  other arithmetic  27.8 us (3%)
  between operations  16 us (1%)
    psum x1, waiting for transfers between devices, body(): total_grad = lax.psum(dense_part, ('tp', 'ep')) + routed  325 us
    ppermute x62, waiting for transfers between devices, shifted(): lax.ppermute(shard, axis, [(i, (i + by) % devices) for i in range(devices)])  211 us
    all_gather x1, waiting for transfers between devices, body(): lax.all_gather(keys, 'ctx', axis=0, tiled=True)  140 us
    ppermute x62, starting transfers between devices, shifted(): lax.ppermute(shard, axis, [(i, (i + by) % devices) for i in range(devices)])  103 us
    all_to_all x1, waiting for transfers between devices, body(): lax.all_to_all(send_grad, 'ctx', split_axis=0, concat_axis=0, tiled=True)  49 us
    all_to_all x1, waiting for transfers between devices, body(): lax.all_to_all(send_in, 'ctx', split_axis=0, concat_axis=0, tiled=True)  45.9 us
  transfers between devices with their start and end apart: 68, of which 67 were waited for; matrix products, arithmetic and copies ran while one was open for 9% of the time, Pallas kernels for 0%

commit v1 on v0

v1 whole, which is shorter than its diff:
```python
import functools

import jax
import jax.numpy as jnp
from jax import lax
from jax.experimental import pallas as pl
from jax.experimental.pallas import tpu as pltpu
from jax.sharding import PartitionSpec as P

HEAD_DIM = 128
NEG_FILL = -1e30
EPSILON = 1e-05
BF = jnp.bfloat16
F32 = jnp.float32
BLOCK = 128
D = 3584
HALF = 10
PIECE = 896
CHUNK = 256
CHUNKS = D // CHUNK
GRAY = 144
GROUPS_Z = [[4 * i + g for i in range(4)] for g in range(4)]
GROUPS_X = [[4 * g + i for i in range(4)] for g in range(4)]
VMEM = pl.BlockSpec(memory_space=pltpu.VMEM)
SMEM = pl.BlockSpec(memory_space=pltpu.SMEM)
HBM = pl.BlockSpec(memory_space=pl.ANY)


def nt(a, b):
    return lax.dot_general(a, b, (((1,), (1,)), ((), ())), preferred_element_type=F32)


def tn(a, b):
    return lax.dot_general(a, b, (((0,), (0,)), ((), ())), preferred_element_type=F32)


def nn(a, b):
    return jnp.dot(a, b, preferred_element_type=F32)


def call(kernel, out_shape, in_specs, scratch=(), mib=48, flops=0, bytes_accessed=0, name=None):
    return pl.pallas_call(
        kernel,
        out_shape=out_shape,
        in_specs=in_specs,
        out_specs=jax.tree.map(lambda _: VMEM, out_shape),
        scratch_shapes=list(scratch),
        compiler_params=pltpu.CompilerParams(vmem_limit_bytes=mib * 1024 * 1024),
        cost_estimate=pl.CostEstimate(flops=flops, bytes_accessed=bytes_accessed, transcendentals=0),
        name=name,
    )


def to_tp(x):
    return lax.ppermute(x, "tp", [(0, 1), (1, 0)])


def to_ep(x, dy, dz):
    pairs = [(y * 2 + z, ((y + dy) % 4) * 2 + (z ^ dz)) for y in range(4) for z in range(2)]
    return lax.ppermute(x, "ep", pairs)


def prepare_kernel(me, hidden, grad_out, gain, ids, weights, mixed, send, spots):
    hid = hidden[...].astype(F32)
    inverse = lax.rsqrt(jnp.mean(hid * hid, axis=1, keepdims=True) + EPSILON)
    mixed[...] = (hid * inverse * gain[...]).astype(BF)
    experts = lax.broadcasted_iota(jnp.int32, (16, BLOCK), 0)
    hit = [(ids[k : k + 1, :] == experts).astype(F32) for k in range(2)]
    before = lax.broadcasted_iota(jnp.int32, (BLOCK, BLOCK), 0) < lax.broadcasted_iota(jnp.int32, (BLOCK, BLOCK), 1)
    earlier = nn((hit[0] + hit[1]).astype(BF), before.astype(BF))
    tp = me[1]
    place_rows = lax.broadcasted_iota(jnp.int32, (512, BLOCK), 0)
    local_rows = lax.broadcasted_iota(jnp.int32, (256, BLOCK), 0) + tp * 256
    spot = jnp.zeros((512, BLOCK), F32)
    own = jnp.zeros((256, BLOCK), F32)
    own_weight = jnp.zeros((256, BLOCK), F32)
    for k in range(2):
        slot = jnp.sum(earlier * hit[k], axis=0, keepdims=True).astype(jnp.int32)
        upper = (slot >= HALF).astype(jnp.int32)
        slot = slot - HALF * upper
        name = ids[k : k + 1, :]
        spot = spot + (place_rows == name * 32 + upper * 16 + slot).astype(F32)
        mark = (local_rows == upper * 256 + name * 16 + slot).astype(F32)
        own = own + mark
        own_weight = own_weight + mark * weights[k : k + 1, :]
    spots[...] = spot.astype(BF)
    own = own.astype(BF)
    scale = jnp.sum(own_weight, axis=1, keepdims=True)
    ep = me[2]

    @pl.when(ep < 4)
    def _():
        at = pl.multiple_of(ep * PIECE, PIECE)
        send[...] = nn(own, mixed[:, pl.ds(at, PIECE)]).astype(BF)

    @pl.when(ep >= 4)
    def _():
        at = pl.multiple_of((ep - 4) * PIECE, PIECE)
        send[...] = (nn(own, grad_out[:, pl.ds(at, PIECE)]) * scale).astype(BF)


def compact_kernel(rows, out):
    to = lax.broadcasted_iota(jnp.int32, (160, 256), 0)
    at = lax.broadcasted_iota(jnp.int32, (160, 256), 1)
    block = at // 16
    slot = at - block * 16
    pick = ((to == block * HALF + slot) & (slot < HALF)).astype(BF)
    out[...] = nn(pick, rows[...]).astype(BF)


def hidden_grads(x, y, gate, up, down):
    a = nt(x, gate)
    b = nt(x, up)
    back = nt(y, down)
    s = jax.nn.sigmoid(a)
    ga = (back * b * s * (1.0 + a * (1.0 - s))).astype(BF)
    gb = (back * a * s).astype(BF)
    return ga, gb


def chunk_lanes(chunk):
    return pl.ds(pl.multiple_of(jnp.minimum(chunk, CHUNKS - 1) * CHUNK, CHUNK), CHUNK)


def dense_kernel(mixed, grad_out, gate, up, down, out):
    ga, gb = hidden_grads(mixed[...], grad_out[...], gate[...], up[...], down[...])
    for c in range(CHUNKS):
        lanes = slice(c * CHUNK, (c + 1) * CHUNK)
        out[c] = (nn(ga, gate[:, lanes]) + nn(gb, up[:, lanes])).astype(BF)
    for c in range(CHUNKS, 16):
        out[c] = jnp.zeros((BLOCK, CHUNK), BF)


def expert_kernel(me, *refs):
    blocks, (gate, up, down, mine, other, rows, sems) = refs[:16], refs[16:]
    tp, ep = me[1], me[2]
    y, z = ep // 2, ep % 2
    z_other = 1 - z
    sources = [(0, z), (0, z_other), (3, z), (1, z_other), (1, z), (3, z_other), (2, z), (2, z_other)]
    copies = []
    for n, block in enumerate(blocks):
        dy, source_z = sources[n % 8]
        source = ((y + dy) % 4) * 2 + source_z
        core = tp if n < 8 else 1 - tp
        target = rows.at[
            pl.ds(pl.multiple_of(core * 160, 160), 160), pl.ds(pl.multiple_of(source * PIECE, PIECE), PIECE)
        ]
        copies.append(pltpu.make_async_copy(block, target, sems.at[n]))
    for copy in copies:
        copy.start()
    for copy in copies:
        copy.wait()
    ga, gb = hidden_grads(rows[:, :D], rows[:, D:], gate[...], up[...], down[...])
    for half, out in ((1 - tp, other), (tp, mine)):
        for d in range(4):
            for zz in range(2):
                lanes = chunk_lanes(half * 8 + ((y + d) % 4) * 2 + zz)
                out[d, zz] = (nn(ga, gate[:, lanes]) + nn(gb, up[:, lanes])).astype(BF)


def sum_kernel(me, first, second, third, fourth, keep, give):
    z = me[2] % 2
    for at, out in ((z, keep), (1 - z, give)):
        total = (
            first[at].astype(F32) + second[at].astype(F32) + third[at].astype(F32) + fourth[at].astype(F32)
        )
        out[...] = total.astype(BF)


def expand_kernel(keep, came, out):
    total = (keep[...].astype(F32) + came[...].astype(F32)).astype(BF)
    to = lax.broadcasted_iota(jnp.int32, (512, 320), 0)
    at = lax.broadcasted_iota(jnp.int32, (512, 320), 1)
    block = to // 32
    core = (to - block * 32) // 16
    slot = to - block * 32 - core * 16
    pick = ((at == core * 160 + block * HALF + slot) & (slot < HALF)).astype(BF)
    out[...] = nn(pick, total).astype(BF)


def combine_kernel(spots, rows, dense, out):
    total = (tn(spots[...], rows[...]) + dense[...].astype(F32)).astype(BF)
    for n in range(8):
        out[n] = total


def split3(x):
    hi = x.astype(BF).astype(F32)
    mid = (x - hi).astype(BF).astype(F32)
    return hi, mid, x - hi - mid


def norm_kernel(me, hidden, grad_out, gain, mine, other, out_proj, stats, heads_out, grad_hidden, message, total):
    tp = me[1]
    for n in range(8):
        total[:, pl.ds(pl.multiple_of((tp * 8 + n) * CHUNK, CHUNK), CHUNK)] = mine[n]
        total[:, pl.ds(pl.multiple_of(((1 - tp) * 8 + n) * CHUNK, CHUNK), CHUNK)] = other[n]
    hid = hidden[...].astype(F32)
    inverse = lax.rsqrt(jnp.mean(hid * hid, axis=1, keepdims=True) + EPSILON)
    normed = hid * inverse
    scaled = total[:, :D].astype(F32) * gain[...]
    mean = jnp.mean(scaled * normed, axis=1, keepdims=True)
    grad = (grad_out[...].astype(F32) + inverse * (scaled - normed * mean)).astype(BF)
    grad_hidden[...] = grad
    heads = nt(grad, out_proj[...]).astype(BF)
    heads_t = nt(out_proj[...], grad).astype(BF).astype(F32)
    rows = []
    for h in range(2):
        delta = jnp.sum(heads_t[h * HEAD_DIM : (h + 1) * HEAD_DIM] * heads_out[h], axis=0, keepdims=True)
        rows.append(list(split3(stats[h : h + 1, :])) + list(split3(delta)))
    for n in range(4):
        message[n, :BLOCK, :] = heads
    extra = jnp.concatenate(
        [jnp.concatenate([rows[0][k], rows[1][k]], axis=1) for k in range(6)] + [jnp.zeros((10, 256), F32)], axis=0
    ).astype(BF)
    for n in range(4):
        message[n, BLOCK:, :] = extra


def stats_kernel(me, own, gathered, stats, heads_out):
    block = me[0]
    key_at = lax.broadcasted_iota(jnp.int32, (2048, BLOCK), 0)
    query_at = lax.broadcasted_iota(jnp.int32, (2048, BLOCK), 1) + block * BLOCK
    allowed = key_at <= query_at
    lines = []
    for h in range(2):
        lanes = slice(h * HEAD_DIM, (h + 1) * HEAD_DIM)
        keys = gathered[:, 256 + h * HEAD_DIM : 256 + (h + 1) * HEAD_DIM]
        values = gathered[:, 512 + h * HEAD_DIM : 512 + (h + 1) * HEAD_DIM]
        scores = jnp.where(allowed, nt(keys, own[:, lanes]) * HEAD_DIM ** (-0.5), NEG_FILL)
        top = jnp.max(scores, axis=0, keepdims=True)
        weights = jnp.where(allowed, jnp.exp(scores - top), 0.0)
        lines.append(top + jnp.log(jnp.sum(weights, axis=0, keepdims=True)))
        half = weights.astype(BF)
        heads_out[h] = tn(values, half) / jnp.sum(half.astype(F32), axis=0, keepdims=True)
    stats[...] = jnp.concatenate(lines + [jnp.zeros((6, BLOCK), F32)], axis=0)


def attention_kernel(me, own_q, gathered, grads, grad_q, grad_k, grad_v, sum_q, sum_k, sum_v):
    block = me[0]
    scale = HEAD_DIM ** (-0.5)
    sum_q[...] = jnp.zeros_like(sum_q)
    sum_k[...] = jnp.zeros_like(sum_k)
    sum_v[...] = jnp.zeros_like(sum_v)
    own_rows = pl.ds(pl.multiple_of(block * BLOCK, BLOCK), BLOCK)
    x, z = block % 4, block // 4
    below = lax.broadcasted_iota(jnp.int32, (BLOCK, BLOCK), 0) <= lax.broadcasted_iota(jnp.int32, (BLOCK, BLOCK), 1)

    def pair(h, keys, values, queries, upstream, extra, allowed):
        at = slice(h * HEAD_DIM, (h + 1) * HEAD_DIM)
        line = extra[:, at].astype(F32)
        log_norm = line[0:1] + line[1:2] + line[2:3]
        delta = line[3:4] + line[4:5] + line[5:6]
        probs = jnp.exp(nt(keys, queries) * scale - log_norm)
        if allowed is not None:
            probs = jnp.where(allowed, probs, 0.0)
        grad_scores = probs * (nt(values, upstream) - delta)
        return probs.astype(BF), grad_scores.astype(BF)

    def keys_of(rows, h):
        return gathered[rows, 256 + h * HEAD_DIM : 256 + (h + 1) * HEAD_DIM]

    def values_of(rows, h):
        return gathered[rows, 512 + h * HEAD_DIM : 512 + (h + 1) * HEAD_DIM]

    own_extra = grads[x, z, BLOCK:, :]
    for i in range(16):
        rows = slice(i * BLOCK, (i + 1) * BLOCK)

        @pl.when(i < block)
        def _(rows=rows):
            for h in range(2):
                at = slice(h * HEAD_DIM, (h + 1) * HEAD_DIM)
                keys = keys_of(rows, h)
                _, half = pair(h, keys, values_of(rows, h), own_q[:, at], grads[x, z, :BLOCK, at], own_extra, None)
                sum_q[:, at] += tn(half, keys)

        @pl.when(i > block)
        def _(i=i, rows=rows):
            extra = grads[i % 4, i // 4, BLOCK:, :]
            for h in range(2):
                at = slice(h * HEAD_DIM, (h + 1) * HEAD_DIM)
                queries = gathered[rows, at]
                upstream = grads[i % 4, i // 4, :BLOCK, at]
                probs, half = pair(h, keys_of(own_rows, h), values_of(own_rows, h), queries, upstream, extra, None)
                sum_k[:, at] += nn(half, queries)
                sum_v[:, at] += nn(probs, upstream)

    for h in range(2):
        at = slice(h * HEAD_DIM, (h + 1) * HEAD_DIM)
        keys = keys_of(own_rows, h)
        queries = own_q[:, at]
        upstream = grads[x, z, :BLOCK, at]
        probs, half = pair(h, keys, values_of(own_rows, h), queries, upstream, own_extra, below)
        grad_q[:, at] = ((sum_q[:, at] + tn(half, keys)) * scale).astype(BF)
        grad_k[:, at] = ((sum_k[:, at] + nn(half, queries)) * scale).astype(BF)
        grad_v[:, at] = (sum_v[:, at] + nn(probs, upstream)).astype(BF)


def shape(*dims, kind=BF):
    return jax.ShapeDtypeStruct(dims, kind)


def body(
    hidden,
    grad_out,
    gain,
    dense_gate,
    dense_up,
    dense_down,
    expert_gate,
    expert_up,
    expert_down,
    out_proj,
    queries,
    keys,
    values,
    route_ids,
    route_weights,
):
    me = jnp.stack([lax.axis_index("ctx"), lax.axis_index("tp"), lax.axis_index("ep")]).astype(jnp.int32)
    gain_row = gain.reshape(1, D)
    gathered = lax.all_gather(jnp.concatenate([queries, keys, values], axis=1), "ctx", axis=0, tiled=True)

    mixed, send, spots = call(
        prepare_kernel,
        (shape(BLOCK, D), shape(256, PIECE), shape(512, BLOCK)),
        [SMEM] + [VMEM] * 5,
        flops=10**8,
        bytes_accessed=4 * 10**6,
        name="prepare",
    )(me, hidden, grad_out, gain_row, route_ids.T, route_weights.T)
    came = lax.all_to_all(send.reshape(16, 16, PIECE), "ctx", split_axis=0, concat_axis=0, tiled=True)

    dense = call(
        dense_kernel,
        shape(16, BLOCK, CHUNK),
        [VMEM] * 5,
        flops=10 * 128 * 152 * D,
        bytes_accessed=6 * 10**6,
        name="dense",
    )(mixed, grad_out, dense_gate, dense_up, dense_down)
    dense = lax.psum_scatter(dense, ("tp", "ep"), scatter_dimension=0, tiled=True)[0]

    piece = call(compact_kernel, shape(160, PIECE), [VMEM], name="compact")(came.reshape(256, PIECE))
    across = to_ep(piece, 0, 1)
    right, across_left = to_ep(piece, 1, 0), to_ep(across, -1, 0)
    left, across_right = to_ep(piece, -1, 0), to_ep(across, 1, 0)
    far, across_far = to_ep(right, 1, 0), to_ep(across_left, -1, 0)
    pieces = [piece, across, right, across_left, left, across_right, far, across_far]
    pieces = pieces + [to_tp(p) for p in pieces]
    mine, other = call(
        expert_kernel,
        (shape(4, 2, 320, CHUNK), shape(4, 2, 320, CHUNK)),
        [SMEM] + [HBM] * 16 + [VMEM] * 3,
        scratch=[pltpu.VMEM((320, 2 * D), BF), pltpu.SemaphoreType.DMA((16,))],
        flops=10 * 320 * 240 * D,
        bytes_accessed=13 * 10**6,
        name="expert",
    )(me, *pieces, expert_gate[0], expert_up[0], expert_down[0])
    other = to_tp(other)
    first, second, third, fourth = [
        (mine[d].astype(F32) + other[d].astype(F32)).astype(BF) for d in range(4)
    ]
    keep, give = call(
        sum_kernel,
        (shape(320, CHUNK), shape(320, CHUNK)),
        [SMEM] + [VMEM] * 4,
        name="sum",
    )(me, first, to_ep(second, 1, 0), to_ep(fourth, -1, 0), to_ep(third, 2, 0))
    back = call(expand_kernel, shape(512, CHUNK), [VMEM] * 2, name="expand")(keep, to_ep(give, 0, 1))
    back = lax.all_to_all(back.reshape(16, 32, CHUNK), "ctx", split_axis=0, concat_axis=0, tiled=True)

    stats, heads_out = call(
        stats_kernel,
        (shape(8, BLOCK, kind=F32), shape(2, HEAD_DIM, BLOCK, kind=F32)),
        [SMEM] + [VMEM] * 2,
        flops=4 * 2 * 2048 * 128 * 128,
        bytes_accessed=4 * 10**6,
        name="stats",
    )(me, queries, gathered)

    total = call(combine_kernel, shape(8, BLOCK, CHUNK), [VMEM] * 3, name="combine")(
        spots, back.reshape(512, CHUNK), dense
    )
    total = lax.all_to_all(total, "ep", split_axis=0, concat_axis=0, tiled=True)
    grad_hidden, message = call(
        norm_kernel,
        (shape(BLOCK, D), shape(4, GRAY, 256)),
        [SMEM] + [VMEM] * 8,
        scratch=[pltpu.VMEM((BLOCK, 16 * CHUNK), BF)],
        flops=4 * 128 * 256 * D,
        bytes_accessed=6 * 10**6,
        name="norm",
    )(me, hidden, grad_out, gain_row, total, to_tp(total), out_proj, stats, heads_out)
    message = lax.all_to_all(
        message, "ctx", split_axis=0, concat_axis=0, tiled=True, axis_index_groups=GROUPS_Z
    )
    message = lax.optimization_barrier(jnp.broadcast_to(message[None], (4, 4, GRAY, 256)))
    message = lax.all_to_all(
        message, "ctx", split_axis=0, concat_axis=0, tiled=True, axis_index_groups=GROUPS_X
    )
    grad_q, grad_k, grad_v = call(
        attention_kernel,
        (shape(BLOCK, 256),) * 3,
        [SMEM] + [VMEM] * 3,
        scratch=[pltpu.VMEM((BLOCK, 256), F32)] * 3,
        flops=17 * 2 * 5 * 2 * 128**3,
        bytes_accessed=5 * 10**6,
        name="attention",
    )(me, queries, gathered, message)
    return grad_hidden, grad_q, grad_k, grad_v


def solution(mesh):
    return jax.shard_map(
        body,
        mesh=mesh,
        in_specs=(
            P("ctx", None),
            P("ctx", None),
            P(),
            P(("tp", "ep"), None),
            P(("tp", "ep"), None),
            P(("tp", "ep"), None),
            P("ctx", ("tp", "ep"), None),
            P("ctx", ("tp", "ep"), None),
            P("ctx", ("tp", "ep"), None),
            P(("tp", "ep"), None),
            P("ctx", ("tp", "ep")),
            P("ctx", ("tp", "ep")),
            P("ctx", ("tp", "ep")),
            P("ctx", None),
            P("ctx", None),
        ),
        out_specs=(
            P("ctx", None),
            P("ctx", ("tp", "ep")),
            P("ctx", ("tp", "ep")),
            P("ctx", ("tp", "ep")),
        ),
        check_vma=False,
    )
```

time: 1090 us -> 217 us (0.20)
  waiting for transfers between devices: 793 us -> 71.1 us
  starting transfers between devices: 129 us -> 39.2 us
  local copies, waits for them, and re-layouts: 70.2 us -> 11 us
  matrix products: 50.4 us -> 0 us
  blocking collectives: 0 us -> 47.1 us
  Pallas kernels: 0 us -> 30.5 us
  other arithmetic: 27.8 us -> 1.15 us
    psum x1 -> x0, waiting for transfers between devices: 325 us -> none  [body(): total_grad = lax.psum(dense_part, ('tp', 'ep')) + routed]
    ppermute x62 -> x21, waiting for transfers between devices: 211 us -> 42.6 us  [the longest x11 38 us: to_ep(): return lax.ppermute(x, 'ep', pairs)]
    all_gather x2 -> x1, waiting for transfers between devices: 161 us -> 0.01 us  [body(): lax.all_gather(jnp.concatenate([queries, keys, values], axis=1), 'ctx', a...]
    ppermute x62 -> x21, starting transfers between devices: 103 us -> 24.4 us  [the longest x11 23.1 us: to_ep(): return lax.ppermute(x, 'ep', pairs)]
    all_to_all x3 -> x2, waiting for transfers between devices: 94.9 us -> 28.4 us  [the longest x1 16.8 us: body(): lax.all_to_all(send.reshape(16, 16, PIECE), 'ctx', split_axis=0, concat_a...]
    dot_general x91 -> x0, matrix products: 50.4 us -> none  [the longest x34 12 us: head_scores(): jnp.einsum('qhd,khd->hqk', left_heads, right_heads, preferred_element_typ...]
    all_to_all x0 -> x3, blocking collectives: none -> 47.1 us  [the longest x2 33.6 us: body(): lax.all_to_all(message, 'ctx', split_axis=0, concat_axis=0, tiled=True, a...]
    pallas_call x0 -> x10, Pallas kernels: none -> 30.5 us  [the longest x1 9.12 us: body(): call(attention_kernel, (shape(BLOCK, 256),) * 3, [SMEM] + [VMEM] * 3, scr...]
  transfers between devices with their start and end apart: 68 -> 25, of which waited for: 67 -> 11; matrix products, arithmetic and copies ran while one was open for 9% -> 0% of each run, Pallas kernels for 0% -> 6%
where the time goes in v1:
time: 217 us; the launch traced here: 216 us
  waiting for transfers between devices  71.1 us (33%)
  blocking collectives  47.1 us (22%)
  starting transfers between devices  39.2 us (18%)
  Pallas kernels  30.5 us (14%)
  between operations  15.7 us (7%)
  local copies, waits for them, and re-layouts  11 us (5%)
    ppermute x11, waiting for transfers between devices, to_ep(): return lax.ppermute(x, 'ep', pairs)  38 us
    all_to_all x2, blocking collectives, body(): lax.all_to_all(message, 'ctx', split_axis=0, concat_axis=0, tiled=True, a...  33.6 us
    ppermute x11, starting transfers between devices, to_ep(): return lax.ppermute(x, 'ep', pairs)  23.1 us
    all_to_all x1, waiting for transfers between devices, body(): lax.all_to_all(send.reshape(16, 16, PIECE), 'ctx', split_axis=0, concat_a...  16.8 us
    all_to_all x1, blocking collectives, body(): total = lax.all_to_all(total, 'ep', split_axis=0, concat_axis=0, tiled=True)  13.5 us
    all_to_all x1, waiting for transfers between devices, body(): lax.all_to_all(back.reshape(16, 32, CHUNK), 'ctx', split_axis=0, concat_a...  11.6 us
    all_to_all x1, starting transfers between devices, body(): lax.all_to_all(send.reshape(16, 16, PIECE), 'ctx', split_axis=0, concat_a...  10.3 us
    unnamed x32, local copies, waits for them, and re-layouts  10.2 us
  transfers between devices with their start and end apart: 25, of which 11 were waited for; matrix products, arithmetic and copies ran while one was open for 0% of the time, Pallas kernels for 6%

profile of v1, /device:TPU:32, one launch (start us, length us, event | category | flops | bytes accessed | tf_op | source)
XLA Modules:
  0.0 215.7 jit_solution(9891863963969565654)
XLA Ops:
  12.6 2.1 prepare.1
  14.7 1.2 copy-done.7
  16.0 1.2 copy-done.8
  18.5 3.3 %dense.1 = bf16[16,128,256]{2,1,0:T(8,128)(2,1)} custom-call(bf16[128,3584]{1,0:T(8,128)(2,1)S(1)} %get-tuple-element.24.mixed, bf16[128,3584]{1,0:T(8,128)(2,1)S(1)} %copy-done.3, bf16[152,3584]{1,0:T(8,128)(2,1)S(1)} %copy-done.7, bf16[152,3584]{1,0:T(8,128)(2,1)S(1)} %copy-done.8, bf16[152,3584]{1,0:T(8,128)(2,1)S(1)} %copy-done.9), custom_call_target="tpu_custom_call" | custom-call | flops 697303040 | bytes 6000000 | tf_op jit(solution)/shard_map/dense/pallas_call | solution.py:335
  21.8 10.3 %all-to-all-start = ((bf16[16,16,896]{2,1,0:T(8,128)(2,1)}), bf16[16,16,896]{2,1,0:T(8,128)(2,1)S(1)}, u32[]{:S(2)}, u32[]{:S(2)}) async-start(bf16[16,16,896]{2,1,0:T(8,128)(2,1)} %bitcast.5), calls=%async_computation | async-start | bytes 917504 | tf_op jit(solution)/shard_map/all_to_all | solution.py:333
  32.9 16.8 %all-to-all-done = bf16[16,16,896]{2,1,0:T(8,128)(2,1)S(1)} async-done(((bf16[16,16,896]{2,1,0:T(8,128)(2,1)}), bf16[16,16,896]{2,1,0:T(8,128)(2,1)S(1)}, u32[]{:S(2)}, u32[]{:S(2)}) %all-to-all-start) | async-done | bytes 458784 | tf_op jit(solution)/shard_map/all_to_all | solution.py:333
  49.9 2.0 collective-permute-start
  52.0 2.5 %collective-permute-start.1 = (bf16[160,896]{1,0:T(8,128)(2,1)S(1)}, bf16[160,896]{1,0:T(8,128)(2,1)S(1)}, u32[]{:S(2)}, u32[]{:S(2)}) collective-permute-start(bf16[160,896]{1,0:T(8,128)(2,1)S(1)} %compact.1.refs_0_), channel_id=1, source_target_pairs={{0,2},{1,3},{2,4},{3,5},{4,6},{5,7},{6,0},{7,1},{8,10},{9,11},{10,... | collective-permute-start | bytes 860168 | tf_op jit(solution)/shard_map/ppermute | solution.py:60
  54.5 1.7 collective-permute-start.3
  56.2 10.4 %collective-permute-done.refs_1_ = bf16[160,896]{1,0:T(8,128)(2,1)S(1)} collective-permute-done((bf16[160,896]{1,0:T(8,128)(2,1)S(1)}, bf16[160,896]{1,0:T(8,128)(2,1)S(1)}, u32[]{:S(2)}, u32[]{:S(2)}) %collective-permute-start) | collective-permute-done | bytes 286752 | tf_op jit(solution)/shard_map/ppermute | solution.py:60
  66.5 3.9 %collective-permute-start.2 = (bf16[160,896]{1,0:T(8,128)(2,1)S(1)}, bf16[160,896]{1,0:T(8,128)(2,1)S(1)}, u32[]{:S(2)}, u32[]{:S(2)}) collective-permute-start(bf16[160,896]{1,0:T(8,128)(2,1)S(1)} %collective-permute-done.refs_1_), channel_id=1, source_target_pairs={{0,6},{1,7},{2,0},{3,1},{4,2},{5,3},{6,4},{7,5},{8,14},{9,15},{10,... | collective-permute-start | bytes 860168 | tf_op jit(solution)/shard_map/ppermute | solution.py:60
  71.1 5.3 %collective-permute-done.2.refs_3_ = bf16[160,896]{1,0:T(8,128)(2,1)S(1)} collective-permute-done((bf16[160,896]{1,0:T(8,128)(2,1)S(1)}, bf16[160,896]{1,0:T(8,128)(2,1)S(1)}, u32[]{:S(2)}, u32[]{:S(2)}) %collective-permute-start.2) | collective-permute-done | bytes 286752 | tf_op jit(solution)/shard_map/ppermute | solution.py:60
  76.4 3.8 %collective-permute-start.6 = (bf16[160,896]{1,0:T(8,128)(2,1)S(1)}, bf16[160,896]{1,0:T(8,128)(2,1)S(1)}, u32[]{:S(2)}, u32[]{:S(2)}) collective-permute-start(bf16[160,896]{1,0:T(8,128)(2,1)S(1)} %collective-permute-done.2.refs_3_), channel_id=1, source_target_pairs={{0,6},{1,7},{2,0},{3,1},{4,2},{5,3},{6,4},{7,5},{8,14},{9,15},{10,... | collective-permute-start | bytes 860168 | tf_op jit(solution)/shard_map/ppermute | solution.py:60
  82.0 2.4 %collective-permute-done.6.refs_7_ = bf16[160,896]{1,0:T(8,128)(2,1)S(1)} collective-permute-done((bf16[160,896]{1,0:T(8,128)(2,1)S(1)}, bf16[160,896]{1,0:T(8,128)(2,1)S(1)}, u32[]{:S(2)}, u32[]{:S(2)}) %collective-permute-start.6) | collective-permute-done | bytes 286752 | tf_op jit(solution)/shard_map/ppermute | solution.py:60
  84.4 1.5 collective-permute-done.14.refs_15_
  85.9 8.2 %expert.1 = (bf16[4,2,320,256]{3,2,1,0:T(8,128)(2,1)S(1)}, bf16[4,2,320,256]{3,2,1,0:T(8,128)(2,1)}) custom-call(s32[3]{0:T(128)S(1)} %pad_add_fusion.me, bf16[160,896]{1,0:T(8,128)(2,1)S(1)} %compact.1.refs_0_, bf16[160,896]{1,0:T(8,128)(2,1)S(1)} %collective-permute-done.refs_1_, bf16[160,896]{1,0:T(8,128)(2,1)S(1)} %collective-permute-done.1.refs_2_, ...), custom_call_target="tpu_custom_call" | custom-call | flops 2752512000 | bytes 13000000 | tf_op jit(solution)/shard_map/expert/pallas_call | solution.py:352
  94.4 3.1 %collective-permute-done.15 = bf16[4,2,320,256]{3,2,1,0:T(8,128)(2,1)S(1)} collective-permute-done((bf16[4,2,320,256]{3,2,1,0:T(8,128)(2,1)}, bf16[4,2,320,256]{3,2,1,0:T(8,128)(2,1)S(1)}, u32[]{:S(2)}, u32[]{:S(2)}) %collective-permute-start.15) | collective-permute-done | bytes 1310752 | tf_op jit(solution)/shard_map/ppermute | solution.py:55
  98.0 3.7 %collective-permute-start.17 = (bf16[2,320,256]{2,1,0:T(8,128)(2,1)S(1)}, bf16[2,320,256]{2,1,0:T(8,128)(2,1)S(1)}, u32[]{:S(2)}, u32[]{:S(2)}) collective-permute-start(bf16[2,320,256]{2,1,0:T(8,128)(2,1)S(1)} %get-tuple-element.33), channel_id=1, source_target_pairs={{0,6},{1,7},{2,0},{3,1},{4,2},{5,3},{6,4},{7,5},{8,14},{9,15},{10,... | collective-permute-start | bytes 983048 | tf_op jit(solution)/shard_map/ppermute | solution.py:60
  101.7 1.4 collective-permute-start.18
  103.1 6.5 %collective-permute-done.16.second = bf16[2,320,256]{2,1,0:T(8,128)(2,1)S(1)} collective-permute-done((bf16[2,320,256]{2,1,0:T(8,128)(2,1)S(1)}, bf16[2,320,256]{2,1,0:T(8,128)(2,1)S(1)}, u32[]{:S(2)}, u32[]{:S(2)}) %collective-permute-start.16) | collective-permute-done | bytes 327712 | tf_op jit(solution)/shard_map/ppermute | solution.py:60
  109.6 8.2 %collective-permute-done.17.third = bf16[2,320,256]{2,1,0:T(8,128)(2,1)S(1)} collective-permute-done((bf16[2,320,256]{2,1,0:T(8,128)(2,1)S(1)}, bf16[2,320,256]{2,1,0:T(8,128)(2,1)S(1)}, u32[]{:S(2)}, u32[]{:S(2)}) %collective-permute-start.17) | collective-permute-done | bytes 327712 | tf_op jit(solution)/shard_map/ppermute | solution.py:60
  118.6 3.8 %collective-permute-start.19 = (bf16[320,256]{1,0:T(8,128)(2,1)S(1)}, bf16[320,256]{1,0:T(8,128)(2,1)S(1)}, u32[]{:S(2)}, u32[]{:S(2)}) collective-permute-start(bf16[320,256]{1,0:T(8,128)(2,1)S(1)} %get-tuple-element.23), channel_id=1, source_target_pairs={{0,1},{1,0},{2,3},{3,2},{4,5},{5,4},{6,7},{7,6},{8,9},{9,8},{10,11... | collective-permute-start | bytes 491528 | tf_op jit(solution)/shard_map/ppermute | solution.py:60
  122.4 4.0 %collective-permute-done.19.came = bf16[320,256]{1,0:T(8,128)(2,1)S(1)} collective-permute-done((bf16[320,256]{1,0:T(8,128)(2,1)S(1)}, bf16[320,256]{1,0:T(8,128)(2,1)S(1)}, u32[]{:S(2)}, u32[]{:S(2)}) %collective-permute-start.19) | collective-permute-done | bytes 163872 | tf_op jit(solution)/shard_map/ppermute | solution.py:60
  127.6 4.4 %all-to-all-start.1 = ((bf16[16,32,256]{2,1,0:T(8,128)(2,1)}), bf16[16,32,256]{2,1,0:T(8,128)(2,1)S(1)}, u32[]{:S(2)}, u32[]{:S(2)}) async-start(bf16[16,32,256]{2,1,0:T(8,128)(2,1)} %bitcast.14), calls=%async_computation.1 | async-start | bytes 524288 | tf_op jit(solution)/shard_map/all_to_all | solution.py:372
  132.0 11.6 %all-to-all-done.1 = bf16[16,32,256]{2,1,0:T(8,128)(2,1)S(1)} async-done(((bf16[16,32,256]{2,1,0:T(8,128)(2,1)}), bf16[16,32,256]{2,1,0:T(8,128)(2,1)S(1)}, u32[]{:S(2)}, u32[]{:S(2)}) %all-to-all-start.1) | async-done | bytes 262176 | tf_op jit(solution)/shard_map/all_to_all | solution.py:372
  144.7 13.5 %all_to_all.25.mine = bf16[8,128,256]{2,1,0:T(8,128)(2,1)S(1)} all-to-all(bf16[8,128,256]{2,1,0:T(8,128)(2,1)S(1)} %combine.1), channel_id=1, replica_groups=mesh['ctx'=16,'tp'=2,'ep'=8] {'ep'}, dimensions={0} | all-to-all | bytes 1048576 | tf_op jit(solution)/shard_map/all_to_all | solution.py:386
  158.2 1.9 copy-done
  160.1 2.7 %stats.1 = (f32[8,128]{1,0:T(8,128)S(1)}, f32[2,128,128]{2,1,0:T(8,128)S(1)}) custom-call(s32[3]{0:T(128)S(1)} %pad_add_fusion.me, bf16[128,256]{1,0:T(8,128)(2,1)S(1)} %copy-done.10, bf16[2048,768]{1,0:T(8,128)(2,1)S(1)} %copy-done), custom_call_target="tpu_custom_call" | custom-call | flops 268435456 | bytes 4000000 | tf_op jit(solution)/shard_map/stats/pallas_call | solution.py:374
  162.8 2.6 %norm.1 = (bf16[128,3584]{1,0:T(8,128)(2,1)}, bf16[4,144,256]{2,1,0:T(8,128)(2,1)S(1)}) custom-call(s32[3]{0:T(128)S(1)} %pad_add_fusion.me, bf16[128,3584]{1,0:T(8,128)(2,1)S(1)} %copy-done.5, bf16[128,3584]{1,0:T(8,128)(2,1)S(1)} %copy-done.3, f32[1,3584]{1,0:T(1,128)S(1)} %reshape.40.gain, bf16[8,128,256]{2,1,0:T(8,128)(2,1)S(1)} %all_to_all.25.mine, ...), custom_call_target="tpu_custom_call" | custom-call | flops 469762048 | bytes 6000000 | tf_op jit(solution)/shard_map/norm/pallas_call | solution.py:387
  165.4 15.6 %all_to_all.26 = bf16[4,144,256]{2,1,0:T(8,128)(2,1)S(1)} all-to-all(bf16[4,144,256]{2,1,0:T(8,128)(2,1)S(1)} %get-tuple-element.28), channel_id=1, replica_groups={{0,64,128,192},{16,80,144,208},{32,96,160,224},{48,112,176,240},{1,65,1..., dimensions={0} | all-to-all | bytes 589824 | tf_op jit(solution)/shard_map/all_to_all | solution.py:396
  181.1 18.0 %all_to_all.27.grads = bf16[4,4,144,256]{3,2,1,0:T(8,128)(2,1)S(1)} all-to-all(bf16[4,4,144,256]{3,2,1,0:T(8,128)(2,1)S(1)} %broadcast_in_dim.2), channel_id=1, replica_groups={{0,16,32,48},{64,80,96,112},{128,144,160,176},{192,208,224,240},{1,17,3..., dimensions={0} | all-to-all | bytes 2359296 | tf_op jit(solution)/shard_map/all_to_all | solution.py:400
  199.1 9.1 %attention.1 = (bf16[128,256]{1,0:T(8,128)(2,1)}, bf16[128,256]{1,0:T(8,128)(2,1)}, bf16[128,256]{1,0:T(8,128)(2,1)}) custom-call(s32[3]{0:T(128)S(1)} %pad_add_fusion.me, bf16[128,256]{1,0:T(8,128)(2,1)S(1)} %copy-done.10, bf16[2048,768]{1,0:T(8,128)(2,1)S(1)} %copy-done.1, bf16[4,4,144,256]{3,2,1,0:T(8,128)(2,1)S(1)} %all_to_all.27.grads), custom_call_target="tpu_custom_call" | custom-call | flops 713031680 | bytes 5000000 | tf_op jit(solution)/shard_map/attention/pallas_call | solution.py:403
  (70 shorter events, 13.0 us)
Async XLA Ops:
  8.0 124.0 %reduce-scatter.2.cloned.1.call-start = ((), (), s32[]{:S(2)}) async-start(), calls=%async_computation.6 | async-start | bytes 1114112 | tf_op jit(solution)/shard_map/reduce_scatter | solution.py:343
  12.6 2.2 copy-start.3
  21.7 10.4 %copy-start.10 = (bf16[128,256]{1,0:T(8,128)(2,1)S(1)}, bf16[128,256]{1,0:T(8,128)(2,1)}, u32[]{:S(2)}) copy-start(bf16[128,256]{1,0:T(8,128)(2,1)} %own_q.1) | copy-start | bytes 196612
  21.8 10.4 %copy-start.14 = (bf16[128,256]{1,0:T(8,128)(2,1)S(1)}, bf16[128,256]{1,0:T(8,128)(2,1)}, u32[]{:S(2)}) copy-start(bf16[128,256]{1,0:T(8,128)(2,1)} %param.27) | copy-start | bytes 196612
  21.8 10.4 %copy-start.15 = (bf16[128,256]{1,0:T(8,128)(2,1)S(1)}, bf16[128,256]{1,0:T(8,128)(2,1)}, u32[]{:S(2)}) copy-start(bf16[128,256]{1,0:T(8,128)(2,1)} %param.26) | copy-start | bytes 196612
  21.8 27.9 %all-to-all-start = ((bf16[16,16,896]{2,1,0:T(8,128)(2,1)}), bf16[16,16,896]{2,1,0:T(8,128)(2,1)S(1)}, u32[]{:S(2)}, u32[]{:S(2)}) async-start(bf16[16,16,896]{2,1,0:T(8,128)(2,1)} %bitcast.5), calls=%async_computation | async-start | bytes 917504 | tf_op jit(solution)/shard_map/all_to_all | solution.py:333
  32.1 126.1 %all-gather.2.cloned.1.call-start = ((), (), s32[]{:S(2)}) async-start(), calls=%async_computation.7 | async-start | bytes 3342336 | tf_op jit(solution)/shard_map/all_gather | solution.py:323
  49.9 16.6 %collective-permute-start = (bf16[160,896]{1,0:T(8,128)(2,1)S(1)}, bf16[160,896]{1,0:T(8,128)(2,1)S(1)}, u32[]{:S(2)}, u32[]{:S(2)}) collective-permute-start(bf16[160,896]{1,0:T(8,128)(2,1)S(1)} %compact.1.refs_0_), channel_id=1, source_target_pairs={{0,1},{1,0},{2,3},{3,2},{4,5},{5,4},{6,7},{7,6},{8,9},{9,8},{10,11... | collective-permute-start | bytes 860168 | tf_op jit(solution)/shard_map/ppermute | solution.py:60
  52.0 18.5 %collective-permute-start.1 = (bf16[160,896]{1,0:T(8,128)(2,1)S(1)}, bf16[160,896]{1,0:T(8,128)(2,1)S(1)}, u32[]{:S(2)}, u32[]{:S(2)}) collective-permute-start(bf16[160,896]{1,0:T(8,128)(2,1)S(1)} %compact.1.refs_0_), channel_id=1, source_target_pairs={{0,2},{1,3},{2,4},{3,5},{4,6},{5,7},{6,0},{7,1},{8,10},{9,11},{10,... | collective-permute-start | bytes 860168 | tf_op jit(solution)/shard_map/ppermute | solution.py:60
  54.5 16.1 %collective-permute-start.3 = (bf16[160,896]{1,0:T(8,128)(2,1)S(1)}, bf16[160,896]{1,0:T(8,128)(2,1)S(1)}, u32[]{:S(2)}, u32[]{:S(2)}) collective-permute-start(bf16[160,896]{1,0:T(8,128)(2,1)S(1)} %compact.1.refs_0_), channel_id=1, source_target_pairs={{0,6},{1,7},{2,0},{3,1},{4,2},{5,3},{6,4},{7,5},{8,14},{9,15},{10,... | collective-permute-start | bytes 860168 | tf_op jit(solution)/shard_map/ppermute | solution.py:60
  56.2 14.4 %collective-permute-start.7 = (bf16[160,896]{1,0:T(8,128)(2,1)S(1)}, bf16[160,896]{1,0:T(8,128)(2,1)S(1)}, u32[]{:S(2)}, u32[]{:S(2)}) collective-permute-start(bf16[160,896]{1,0:T(8,128)(2,1)S(1)} %compact.1.refs_0_), channel_id=1, source_target_pairs={{0,8},{8,0},{1,9},{9,1},{2,10},{10,2},{3,11},{11,3},{4,12},{12,4},... | collective-permute-start | bytes 860168 | tf_op jit(solution)/shard_map/ppermute | solution.py:55
  66.5 9.8 %collective-permute-start.2 = (bf16[160,896]{1,0:T(8,128)(2,1)S(1)}, bf16[160,896]{1,0:T(8,128)(2,1)S(1)}, u32[]{:S(2)}, u32[]{:S(2)}) collective-permute-start(bf16[160,896]{1,0:T(8,128)(2,1)S(1)} %collective-permute-done.refs_1_), channel_id=1, source_target_pairs={{0,6},{1,7},{2,0},{3,1},{4,2},{5,3},{6,4},{7,5},{8,14},{9,15},{10,... | collective-permute-start | bytes 860168 | tf_op jit(solution)/shard_map/ppermute | solution.py:60
  70.5 9.8 %collective-permute-start.4 = (bf16[160,896]{1,0:T(8,128)(2,1)S(1)}, bf16[160,896]{1,0:T(8,128)(2,1)S(1)}, u32[]{:S(2)}, u32[]{:S(2)}) collective-permute-start(bf16[160,896]{1,0:T(8,128)(2,1)S(1)} %collective-permute-done.refs_1_), channel_id=1, source_target_pairs={{0,2},{1,3},{2,4},{3,5},{4,6},{5,7},{6,0},{7,1},{8,10},{9,11},{10,... | collective-permute-start | bytes 860168 | tf_op jit(solution)/shard_map/ppermute | solution.py:60
  70.5 10.9 %collective-permute-start.5 = (bf16[160,896]{1,0:T(8,128)(2,1)S(1)}, bf16[160,896]{1,0:T(8,128)(2,1)S(1)}, u32[]{:S(2)}, u32[]{:S(2)}) collective-permute-start(bf16[160,896]{1,0:T(8,128)(2,1)S(1)} %collective-permute-done.1.refs_2_), channel_id=1, source_target_pairs={{0,2},{1,3},{2,4},{3,5},{4,6},{5,7},{6,0},{7,1},{8,10},{9,11},{10,... | collective-permute-start | bytes 860168 | tf_op jit(solution)/shard_map/ppermute | solution.py:60
  70.6 10.8 %collective-permute-start.8 = (bf16[160,896]{1,0:T(8,128)(2,1)S(1)}, bf16[160,896]{1,0:T(8,128)(2,1)S(1)}, u32[]{:S(2)}, u32[]{:S(2)}) collective-permute-start(bf16[160,896]{1,0:T(8,128)(2,1)S(1)} %collective-permute-done.refs_1_), channel_id=1, source_target_pairs={{0,8},{8,0},{1,9},{9,1},{2,10},{10,2},{3,11},{11,3},{4,12},{12,4},... | collective-permute-start | bytes 860168 | tf_op jit(solution)/shard_map/ppermute | solution.py:55
  70.6 11.3 %collective-permute-start.9 = (bf16[160,896]{1,0:T(8,128)(2,1)S(1)}, bf16[160,896]{1,0:T(8,128)(2,1)S(1)}, u32[]{:S(2)}, u32[]{:S(2)}) collective-permute-start(bf16[160,896]{1,0:T(8,128)(2,1)S(1)} %collective-permute-done.1.refs_2_), channel_id=1, source_target_pairs={{0,8},{8,0},{1,9},{9,1},{2,10},{10,2},{3,11},{11,3},{4,12},{12,4},... | collective-permute-start | bytes 860168 | tf_op jit(solution)/shard_map/ppermute | solution.py:55
  76.4 8.0 %collective-permute-start.6 = (bf16[160,896]{1,0:T(8,128)(2,1)S(1)}, bf16[160,896]{1,0:T(8,128)(2,1)S(1)}, u32[]{:S(2)}, u32[]{:S(2)}) collective-permute-start(bf16[160,896]{1,0:T(8,128)(2,1)S(1)} %collective-permute-done.2.refs_3_), channel_id=1, source_target_pairs={{0,6},{1,7},{2,0},{3,1},{4,2},{5,3},{6,4},{7,5},{8,14},{9,15},{10,... | collective-permute-start | bytes 860168 | tf_op jit(solution)/shard_map/ppermute | solution.py:60
  80.2 4.2 %collective-permute-start.11 = (bf16[160,896]{1,0:T(8,128)(2,1)S(1)}, bf16[160,896]{1,0:T(8,128)(2,1)S(1)}, u32[]{:S(2)}, u32[]{:S(2)}) collective-permute-start(bf16[160,896]{1,0:T(8,128)(2,1)S(1)} %collective-permute-done.3.refs_4_), channel_id=1, source_target_pairs={{0,8},{8,0},{1,9},{9,1},{2,10},{10,2},{3,11},{11,3},{4,12},{12,4},... | collective-permute-start | bytes 860168 | tf_op jit(solution)/shard_map/ppermute | solution.py:55
  81.4 3.0 %collective-permute-start.10 = (bf16[160,896]{1,0:T(8,128)(2,1)S(1)}, bf16[160,896]{1,0:T(8,128)(2,1)S(1)}, u32[]{:S(2)}, u32[]{:S(2)}) collective-permute-start(bf16[160,896]{1,0:T(8,128)(2,1)S(1)} %collective-permute-done.2.refs_3_), channel_id=1, source_target_pairs={{0,8},{8,0},{1,9},{9,1},{2,10},{10,2},{3,11},{11,3},{4,12},{12,4},... | collective-permute-start | bytes 860168 | tf_op jit(solution)/shard_map/ppermute | solution.py:55
  81.4 3.0 %collective-permute-start.12 = (bf16[160,896]{1,0:T(8,128)(2,1)S(1)}, bf16[160,896]{1,0:T(8,128)(2,1)S(1)}, u32[]{:S(2)}, u32[]{:S(2)}) collective-permute-start(bf16[160,896]{1,0:T(8,128)(2,1)S(1)} %collective-permute-done.4.refs_5_), channel_id=1, source_target_pairs={{0,8},{8,0},{1,9},{9,1},{2,10},{10,2},{3,11},{11,3},{4,12},{12,4},... | collective-permute-start | bytes 860168 | tf_op jit(solution)/shard_map/ppermute | solution.py:55
  81.9 2.5 %collective-permute-start.13 = (bf16[160,896]{1,0:T(8,128)(2,1)S(1)}, bf16[160,896]{1,0:T(8,128)(2,1)S(1)}, u32[]{:S(2)}, u32[]{:S(2)}) collective-permute-start(bf16[160,896]{1,0:T(8,128)(2,1)S(1)} %collective-permute-done.5.refs_6_), channel_id=1, source_target_pairs={{0,8},{8,0},{1,9},{9,1},{2,10},{10,2},{3,11},{11,3},{4,12},{12,4},... | collective-permute-start | bytes 860168 | tf_op jit(solution)/shard_map/ppermute | solution.py:55
  84.4 1.6 collective-permute-start.14
  94.2 3.3 %collective-permute-start.15 = (bf16[4,2,320,256]{3,2,1,0:T(8,128)(2,1)}, bf16[4,2,320,256]{3,2,1,0:T(8,128)(2,1)S(1)}, u32[]{:S(2)}, u32[]{:S(2)}) collective-permute-start(bf16[4,2,320,256]{3,2,1,0:T(8,128)(2,1)} %get-tuple-element.21), channel_id=1, source_target_pairs={{0,8},{8,0},{1,9},{9,1},{2,10},{10,2},{3,11},{11,3},{4,12},{12,4},... | collective-permute-start | bytes 3932168 | tf_op jit(solution)/shard_map/ppermute | solution.py:55
  97.9 11.7 %collective-permute-start.16 = (bf16[2,320,256]{2,1,0:T(8,128)(2,1)S(1)}, bf16[2,320,256]{2,1,0:T(8,128)(2,1)S(1)}, u32[]{:S(2)}, u32[]{:S(2)}) collective-permute-start(bf16[2,320,256]{2,1,0:T(8,128)(2,1)S(1)} %get-tuple-element.34), channel_id=1, source_target_pairs={{0,2},{1,3},{2,4},{3,5},{4,6},{5,7},{6,0},{7,1},{8,10},{9,11},{10,... | collective-permute-start | bytes 983048 | tf_op jit(solution)/shard_map/ppermute | solution.py:60
  98.0 19.9 %collective-permute-start.17 = (bf16[2,320,256]{2,1,0:T(8,128)(2,1)S(1)}, bf16[2,320,256]{2,1,0:T(8,128)(2,1)S(1)}, u32[]{:S(2)}, u32[]{:S(2)}) collective-permute-start(bf16[2,320,256]{2,1,0:T(8,128)(2,1)S(1)} %get-tuple-element.33), channel_id=1, source_target_pairs={{0,6},{1,7},{2,0},{3,1},{4,2},{5,3},{6,4},{7,5},{8,14},{9,15},{10,... | collective-permute-start | bytes 983048 | tf_op jit(solution)/shard_map/ppermute | solution.py:60
  101.7 16.2 %collective-permute-start.18 = (bf16[2,320,256]{2,1,0:T(8,128)(2,1)S(1)}, bf16[2,320,256]{2,1,0:T(8,128)(2,1)S(1)}, u32[]{:S(2)}, u32[]{:S(2)}) collective-permute-start(bf16[2,320,256]{2,1,0:T(8,128)(2,1)S(1)} %get-tuple-element.32), channel_id=1, source_target_pairs={{0,4},{1,5},{2,6},{3,7},{4,0},{5,1},{6,2},{7,3},{8,12},{9,13},{10,... | collective-permute-start | bytes 983048 | tf_op jit(solution)/shard_map/ppermute | solution.py:60
  118.6 7.8 %collective-permute-start.19 = (bf16[320,256]{1,0:T(8,128)(2,1)S(1)}, bf16[320,256]{1,0:T(8,128)(2,1)S(1)}, u32[]{:S(2)}, u32[]{:S(2)}) collective-permute-start(bf16[320,256]{1,0:T(8,128)(2,1)S(1)} %get-tuple-element.23), channel_id=1, source_target_pairs={{0,1},{1,0},{2,3},{3,2},{4,5},{5,4},{6,7},{7,6},{8,9},{9,8},{10,11... | collective-permute-start | bytes 491528 | tf_op jit(solution)/shard_map/ppermute | solution.py:60
  127.6 16.0 %all-to-all-start.1 = ((bf16[16,32,256]{2,1,0:T(8,128)(2,1)}), bf16[16,32,256]{2,1,0:T(8,128)(2,1)S(1)}, u32[]{:S(2)}, u32[]{:S(2)}) async-start(bf16[16,32,256]{2,1,0:T(8,128)(2,1)} %bitcast.14), calls=%async_computation.1 | async-start | bytes 524288 | tf_op jit(solution)/shard_map/all_to_all | solution.py:372
  144.7 18.1 %copy-start.5 = (bf16[128,3584]{1,0:T(8,128)(2,1)S(1)}, bf16[128,3584]{1,0:T(8,128)(2,1)}, u32[]{:S(2)}) copy-start(bf16[128,3584]{1,0:T(8,128)(2,1)} %hidden.3) | copy-start | bytes 2752516
  158.2 4.6 %collective-permute-start.20 = (bf16[8,128,256]{2,1,0:T(8,128)(2,1)S(1)}, bf16[8,128,256]{2,1,0:T(8,128)(2,1)S(1)}, u32[]{:S(2)}, u32[]{:S(2)}) collective-permute-start(bf16[8,128,256]{2,1,0:T(8,128)(2,1)S(1)} %all_to_all.25.mine), channel_id=1, source_target_pairs={{0,8},{8,0},{1,9},{9,1},{2,10},{10,2},{3,11},{11,3},{4,12},{12,4},... | collective-permute-start | bytes 1572872 | tf_op jit(solution)/shard_map/ppermute | solution.py:55
  160.1 2.7 %copy-start.6 = (bf16[256,3584]{1,0:T(8,128)(2,1)S(1)}, bf16[256,3584]{1,0:T(8,128)(2,1)}, u32[]{:S(2)}) copy-start(bf16[256,3584]{1,0:T(8,128)(2,1)} %out_proj.1) | copy-start | bytes 5505028
  181.0 18.1 %copy-start.1 = (bf16[2048,768]{1,0:T(8,128)(2,1)S(1)}, bf16[2048,768]{1,0:T(8,128)(2,1)}, u32[]{:S(2)}) copy-start(bf16[2048,768]{1,0:T(8,128)(2,1)} %all-gather.2.cloned.1.call-done.gathered) | copy-start | bytes 9437188
  (9 other events, 10.2 us)
Sparse Core Ops, SparseCore 0:
  21.9 95.3 reduce-scatter.1
Sparse Core Ops, SparseCore 1:
  35.3 76.4 all-gather.1

commit v2 on v1

v2 whole, which is shorter than its diff:
```python
import functools

import jax
import jax.numpy as jnp
from jax import lax
from jax.experimental import pallas as pl
from jax.experimental.pallas import tpu as pltpu
from jax.sharding import PartitionSpec as P

HEAD_DIM = 128
NEG_FILL = -1e30
EPSILON = 1e-05
BF = jnp.bfloat16
F32 = jnp.float32
BLOCK = 128
D = 3584
HALF = 10
PIECE = 896
CHUNK = 512
STRIDE = 24
SCALE = HEAD_DIM ** (-0.5)
CHUNKS = D // CHUNK
GRAY = 144
VMEM = pl.BlockSpec(memory_space=pltpu.VMEM)
SMEM = pl.BlockSpec(memory_space=pltpu.SMEM)
HBM = pl.BlockSpec(memory_space=pltpu.HBM)


def nt(a, b):
    return lax.dot_general(a, b, (((1,), (1,)), ((), ())), preferred_element_type=F32)


def tn(a, b):
    return lax.dot_general(a, b, (((0,), (0,)), ((), ())), preferred_element_type=F32)


def nn(a, b):
    return jnp.dot(a, b, preferred_element_type=F32)


def call(kernel, out_shape, in_specs, scratch=(), mib=12, flops=0, bytes_accessed=0, name=None):
    return pl.pallas_call(
        kernel,
        out_shape=out_shape,
        in_specs=in_specs,
        out_specs=jax.tree.map(lambda _: VMEM, out_shape),
        scratch_shapes=list(scratch),
        compiler_params=pltpu.CompilerParams(vmem_limit_bytes=mib * 1024 * 1024),
        cost_estimate=pl.CostEstimate(flops=flops, bytes_accessed=bytes_accessed, transcendentals=0),
        name=name,
    )


def in_hbm(x):
    return pltpu.with_memory_space_constraint(x, pltpu.HBM)


def in_vmem(x):
    return pltpu.with_memory_space_constraint(x, pltpu.VMEM)


def to_tp(x):
    return lax.ppermute(x, "tp", [(0, 1), (1, 0)])


def to_ep(x, dy, dz):
    pairs = [(y * 2 + z, ((y + dy) % 4) * 2 + (z ^ dz)) for y in range(4) for z in range(2)]
    return lax.ppermute(x, "ep", pairs)


def to_ctx(x, dz, dx):
    pairs = [
        (z * 4 + q, (z + dz) * 4 + (q + dx) % 4) for z in range(4) for q in range(4) if 0 <= z + dz < 4
    ]
    return lax.ppermute(x, "ctx", pairs)


def sum_over_y(me, parts, name):
    size = shape(parts[0].shape[0], CHUNK)
    return call(sum_kernel, (size, size), [SMEM] + [VMEM] * 4, name=name)(
        me, parts[0], to_ep(parts[1], 1, 0), to_ep(parts[3], -1, 0), to_ep(parts[2], 2, 0)
    )


def prepare_kernel(
    me, hidden, grad_out, gain, ids, weights, queries, keys, values, mixed, send, spots, heads, hid_rows, grad_rows, sems
):
    copies = []
    for n in range(8):
        part = pl.ds(n * 16, 16)
        copies.append(pltpu.make_async_copy(hidden.at[part], hid_rows.at[part], sems.at[n]))
        copies[-1].start()
    lanes = pl.ds(pl.multiple_of((me[2] // 2 % 2) * 2 * PIECE, 2 * PIECE), 2 * PIECE)
    for n in range(4):
        part = pl.ds(n * 32, 32)
        copies.append(pltpu.make_async_copy(grad_out.at[part, lanes], grad_rows.at[part], sems.at[8 + n]))
        copies[-1].start()
    for n, source in enumerate((queries, keys, values)):
        copies.append(pltpu.make_async_copy(source, heads.at[:, pl.ds(n * 256, 256)], sems.at[12 + n]))
        copies[-1].start()
    tp = me[1]
    y = me[2] // 2
    experts = lax.broadcasted_iota(jnp.int32, (16, BLOCK), 0)
    hit = [(ids[k : k + 1, :] == experts).astype(F32) for k in range(2)]
    before = lax.broadcasted_iota(jnp.int32, (BLOCK, BLOCK), 0) < lax.broadcasted_iota(jnp.int32, (BLOCK, BLOCK), 1)
    earlier = nn((hit[0] + hit[1]).astype(BF), before.astype(BF))
    place_rows = lax.broadcasted_iota(jnp.int32, (256, BLOCK), 0)
    send_rows = lax.broadcasted_iota(jnp.int32, (16 * STRIDE, BLOCK), 0)
    spot = jnp.zeros((256, BLOCK), F32)
    own = [jnp.zeros((16 * STRIDE, BLOCK), F32) for _ in range(2)]
    weight = jnp.zeros((16 * STRIDE, BLOCK), F32)
    for k in range(2):
        slot = jnp.sum(earlier * hit[k], axis=0, keepdims=True).astype(jnp.int32)
        upper = (slot >= HALF).astype(jnp.int32)
        slot = slot - HALF * upper
        name = ids[k : k + 1, :]
        away = jnp.where(upper == tp, 0, 4096)
        spot = spot + (place_rows == name * 16 + slot + away).astype(F32)
        for h in range(2):
            mark = (send_rows == name * STRIDE + h * HALF + slot + away).astype(F32)
            own[h] = own[h] + mark
            weight = weight + mark * weights[k : k + 1, :]
    spots[...] = spot.astype(BF)
    scale = jnp.sum(weight, axis=1, keepdims=True)
    own = [o.astype(BF) for o in own]
    for n in range(8):
        copies[n].wait()
        part = slice(n * 16, (n + 1) * 16)
        hid = hid_rows[part, :].astype(F32)
        inverse = lax.rsqrt(jnp.mean(hid * hid, axis=1, keepdims=True) + EPSILON)
        mixed[part, :] = (hid * inverse * gain[...][None, :]).astype(BF)
    for copy in copies[8:]:
        copy.wait()

    @pl.when(y < 2)
    def _():
        at = (y % 2) * 2 * PIECE
        first = pl.ds(pl.multiple_of(at, PIECE), PIECE)
        second = pl.ds(pl.multiple_of(at + PIECE, PIECE), PIECE)
        rows = nn(own[0], mixed[:, first]) + nn(own[1], mixed[:, second])
        send[...] = rows.reshape(16, STRIDE, PIECE).astype(BF)

    @pl.when(y >= 2)
    def _():
        rows = (nn(own[0], grad_rows[:, :PIECE]) + nn(own[1], grad_rows[:, PIECE:])) * scale
        send[...] = rows.reshape(16, STRIDE, PIECE).astype(BF)


def compact_kernel(came, out):
    rows = came[...].astype(F32).reshape(16 * STRIDE, PIECE).astype(BF)
    to = lax.broadcasted_iota(jnp.int32, (320, 16 * STRIDE), 0)
    at = lax.broadcasted_iota(jnp.int32, (320, 16 * STRIDE), 1)
    block = at // STRIDE
    place = at - block * STRIDE
    half = (place >= HALF).astype(jnp.int32)
    pick = ((to == half * 160 + block * HALF + place - half * HALF) & (place < 2 * HALF)).astype(BF)
    out[...] = nn(pick, rows).astype(BF)


def hidden_grads(x, y, gate, up, down):
    a = nt(x, gate)
    b = nt(x, up)
    back = nt(y, down)
    s = jax.nn.sigmoid(a)
    ga = (back * b * s * (1.0 + a * (1.0 - s))).astype(BF)
    gb = (back * a * s).astype(BF)
    return ga, gb


def piece_lanes(index):
    return pl.ds(pl.multiple_of(index * PIECE, PIECE), PIECE)


def dense_kernel(me, mixed, grad_out, gate_in, up_in, down_in, *refs):
    outs, (grad_rows, gate, up, down, sems) = refs[:4], refs[4:]
    copies = []
    for source, target in ((gate_in, gate), (up_in, up), (down_in, down), (grad_out, grad_rows)):
        for start in range(0, D, PIECE):
            part = pl.ds(start, PIECE)
            copies.append(pltpu.make_async_copy(source.at[:, part], target.at[:, part], sems.at[len(copies)]))
    for copy in copies:
        copy.start()
    for copy in copies:
        copy.wait()
    y = me[2] // 2
    ga, gb = hidden_grads(mixed[...], grad_rows[...], gate[...], up[...], down[...])
    for d, out in enumerate(outs):
        lanes = piece_lanes((y + d) % 4)
        out[...] = (nn(ga, gate[:, lanes]) + nn(gb, up[:, lanes])).astype(BF)


def expert_kernel(me, own, right, left, far0, far1, gate, up, down, gate2, up2, down2, *refs):
    outs, (rows, sems) = refs[:4], refs[4:]
    y = me[2] // 2

    def copy(block, from_row, dy, h, n):
        target = rows.at[:, piece_lanes(((y + dy) % 4) * 2 + h)]
        return pltpu.make_async_copy(block.at[pl.ds(from_row, 160)], target, sems.at[n])

    copies = [
        copy(own, 0, 0, 0, 0),
        copy(own, 160, 0, 1, 1),
        copy(right, 0, 3, 0, 2),
        copy(right, 160, 3, 1, 3),
        copy(left, 0, 1, 0, 4),
        copy(left, 160, 1, 1, 5),
        copy(far0, 0, 2, 0, 6),
        copy(far1, 0, 2, 1, 7),
    ]
    for c in copies:
        c.start()
    for c in copies:
        c.wait()
    x, g = rows[:, :D], rows[:, D:]
    ga, gb = hidden_grads(x, g, gate[...], up[...], down[...])
    ga2, gb2 = hidden_grads(x, g, gate2[...], up2[...], down2[...])
    for d, out in enumerate(outs):
        lanes = piece_lanes((y + d) % 4)
        total = nn(ga, gate[:, lanes]) + nn(gb, up[:, lanes])
        total = total + (nn(ga2, gate2[:, lanes]) + nn(gb2, up2[:, lanes]))
        out[...] = total.astype(BF)


def sum_kernel(me, first, second, third, fourth, keep, give):
    z = me[2] % 2
    for side, out in ((z, keep), (1 - z, give)):
        lanes = pl.ds(pl.multiple_of(side * (PIECE - CHUNK), 128), CHUNK)
        total = first[:, lanes].astype(F32) + second[:, lanes].astype(F32)
        total = total + third[:, lanes].astype(F32) + fourth[:, lanes].astype(F32)
        out[...] = total.astype(BF)


def expand_kernel(keep, came, out):
    total = (keep[...].astype(F32) + came[...].astype(F32)).astype(BF)
    to = lax.broadcasted_iota(jnp.int32, (256, 160), 0)
    at = lax.broadcasted_iota(jnp.int32, (256, 160), 1)
    block = to // 16
    slot = to - block * 16
    pick = ((at == block * HALF + slot) & (slot < HALF)).astype(BF)
    out[...] = nn(pick, total).astype(BF)


def combine_kernel(me, spots, rows, dense_keep, dense_came, keep, give):
    tp = me[1]
    for half, out in ((tp, keep), (1 - tp, give)):
        lanes = pl.ds(pl.multiple_of(half * 256, 256), 256)
        total = tn(spots[...], rows[:, lanes]) + dense_keep[:, lanes].astype(F32) + dense_came[:, lanes].astype(F32)
        out[...] = total.astype(out.dtype)


def split3(x):
    hi = x.astype(BF).astype(F32)
    mid = (x - hi).astype(BF).astype(F32)
    return hi, mid, x - hi - mid


def norm_kernel(
    me, hidden, grad_out, gain, mine, other, proj_in, stats, heads_out, grad_hidden, message, total, out_proj, sems
):
    copies = []
    for n in range(8):
        part = pl.ds(n * 32, 32)
        copies.append(pltpu.make_async_copy(proj_in.at[part], out_proj.at[part], sems.at[n]))
        copies[-1].start()
    tp = me[1]
    for n in range(8):
        at = (n // 2) * PIECE + (n % 2) * (PIECE - CHUNK)
        total[:, pl.ds(pl.multiple_of(at + tp * 256, 128), 256)] = mine[n]
        total[:, pl.ds(pl.multiple_of(at + (1 - tp) * 256, 128), 256)] = other[n]
    hid = hidden[...].astype(F32)
    inverse = lax.rsqrt(jnp.mean(hid * hid, axis=1, keepdims=True) + EPSILON)
    normed = hid * inverse
    scaled = total[...].astype(F32) * gain[...][None, :]
    mean = jnp.mean(scaled * normed, axis=1, keepdims=True)
    grad = (grad_out[...].astype(F32) + inverse * (scaled - normed * mean)).astype(BF)
    grad_hidden[...] = grad
    for copy in copies:
        copy.wait()
    heads = nt(grad, out_proj[...]).astype(BF)
    heads_t = nt(out_proj[...], grad).astype(BF).astype(F32)
    rows = []
    for h in range(2):
        delta = jnp.sum(heads_t[h * HEAD_DIM : (h + 1) * HEAD_DIM] * heads_out[h], axis=0, keepdims=True)
        rows.append(list(split3(stats[h : h + 1, :])) + list(split3(delta)))
    message[:BLOCK, :] = heads
    message[BLOCK:, :] = jnp.concatenate(
        [jnp.concatenate([rows[0][k], rows[1][k]], axis=1) for k in range(6)] + [jnp.zeros((10, 256), F32)], axis=0
    ).astype(BF)


def stats_kernel(me, own, gathered, stats, heads_out):
    block = me[0]
    key_at = lax.broadcasted_iota(jnp.int32, (2048, BLOCK), 0)
    query_at = lax.broadcasted_iota(jnp.int32, (2048, BLOCK), 1) + block * BLOCK
    allowed = key_at <= query_at
    lines = []
    for h in range(2):
        lanes = slice(h * HEAD_DIM, (h + 1) * HEAD_DIM)
        keys = gathered[:, 256 + h * HEAD_DIM : 256 + (h + 1) * HEAD_DIM]
        values = gathered[:, 512 + h * HEAD_DIM : 512 + (h + 1) * HEAD_DIM]
        scores = jnp.where(allowed, nt(keys, own[:, lanes]) * HEAD_DIM ** (-0.5), NEG_FILL)
        top = jnp.max(scores, axis=0, keepdims=True)
        weights = jnp.where(allowed, jnp.exp(scores - top), 0.0)
        lines.append(top + jnp.log(jnp.sum(weights, axis=0, keepdims=True)))
        half = weights.astype(BF)
        heads_out[h] = tn(values, half) / jnp.sum(half.astype(F32), axis=0, keepdims=True)
    stats[...] = jnp.concatenate(lines + [jnp.zeros((6, BLOCK), F32)], axis=0)


def pair(keys, values, queries, upstream, lines, allowed):
    log_norm = lines[0:1] + lines[1:2] + lines[2:3]
    delta = lines[3:4] + lines[4:5] + lines[5:6]
    probs = jnp.where(allowed, jnp.exp(nt(keys, queries) * SCALE - log_norm), 0.0)
    grad_scores = probs * (nt(values, upstream) - delta)
    return probs.astype(BF), grad_scores.astype(BF)


def head(h, start=0):
    return slice(start + h * HEAD_DIM, start + (h + 1) * HEAD_DIM)


def queries_kernel(me, own_q, gathered, message, grad_q, total):
    block = me[0]
    lines = message[BLOCK:, :].astype(F32)
    query_at = lax.broadcasted_iota(jnp.int32, (512, BLOCK), 1) + block * BLOCK
    total[...] = jnp.zeros_like(total)
    for i in range(4):

        @pl.when(4 * i <= block)
        def _(i=i):
            rows = slice(i * 512, (i + 1) * 512)
            allowed = lax.broadcasted_iota(jnp.int32, (512, BLOCK), 0) + i * 512 <= query_at
            for h in range(2):
                keys = gathered[rows, head(h, 256)]
                values = gathered[rows, head(h, 512)]
                _, half = pair(keys, values, own_q[:, head(h)], message[:BLOCK, head(h)], lines[:, head(h)], allowed)
                total[:, head(h)] += tn(half, keys)

    grad_q[...] = (total[...] * SCALE).astype(BF)


def keys_kernel(shifts, first, last, me, gathered, *refs):
    count = len(shifts)
    grads, refs = refs[:count], refs[count:]
    if first:
        out_k, out_v, sum_k, sum_v = refs
        sum_k[...] = jnp.zeros_like(sum_k)
        sum_v[...] = jnp.zeros_like(sum_v)
    else:
        in_k, in_v, out_k, out_v, sum_k, sum_v = refs
        sum_k[...] = in_k[...]
        sum_v[...] = in_v[...]
    block = me[0]
    x, z = block % 4, block // 4
    own_rows = pl.ds(pl.multiple_of(block * BLOCK, BLOCK), BLOCK)
    lane = lax.broadcasted_iota(jnp.int32, (BLOCK, 4 * BLOCK), 1)
    key_at = lax.broadcasted_iota(jnp.int32, (BLOCK, 4 * BLOCK), 0) + block * BLOCK
    row = z + lane // BLOCK
    for shift, source in zip(shifts, grads):
        column = (x + shift) % 4
        allowed = (row < 4) & (key_at <= (row * 4 + column) * BLOCK + lane % BLOCK)
        blocks = [jnp.minimum((z + n) * 4 + column, 15) for n in range(4)]
        queries = jnp.concatenate(
            [gathered[pl.ds(pl.multiple_of(i * BLOCK, BLOCK), BLOCK), :256] for i in blocks], axis=0
        )
        upstream = jnp.concatenate([source[n, :BLOCK, :] for n in range(4)], axis=0)
        lines = [source[n, BLOCK:, :].astype(F32) for n in range(4)]
        for h in range(2):
            line = jnp.concatenate([part[:, head(h)] for part in lines], axis=1)
            keys = gathered[own_rows, head(h, 256)]
            values = gathered[own_rows, head(h, 512)]
            probs, half = pair(keys, values, queries[:, head(h)], upstream[:, head(h)], line, allowed)
            sum_k[:, head(h)] += nn(half, queries[:, head(h)])
            sum_v[:, head(h)] += nn(probs, upstream[:, head(h)])

    if last:
        out_k[...] = (sum_k[...] * SCALE).astype(BF)
        out_v[...] = sum_v[...].astype(BF)
    else:
        out_k[...] = sum_k[...]
        out_v[...] = sum_v[...]


def shape(*dims, kind=BF):
    return jax.ShapeDtypeStruct(dims, kind)


def body(
    hidden,
    grad_out,
    gain,
    dense_gate,
    dense_up,
    dense_down,
    expert_gate,
    expert_up,
    expert_down,
    out_proj,
    queries,
    keys,
    values,
    route_ids,
    route_weights,
):
    me = jnp.stack([lax.axis_index("ctx"), lax.axis_index("tp"), lax.axis_index("ep")]).astype(jnp.int32)
    experts = [expert_gate[0], expert_up[0], expert_down[0]]

    mixed, send, spots, heads = call(
        prepare_kernel,
        (shape(BLOCK, D), shape(16, STRIDE, PIECE), shape(256, BLOCK), shape(BLOCK, 768)),
        [SMEM, HBM, HBM, VMEM, VMEM, VMEM, HBM, HBM, HBM],
        scratch=[pltpu.VMEM((BLOCK, D), BF), pltpu.VMEM((BLOCK, 2 * PIECE), BF), pltpu.SemaphoreType.DMA((15,))],
        flops=10**8,
        bytes_accessed=4 * 10**6,
        mib=16,
        name="prepare",
    )(me, in_hbm(hidden), in_hbm(grad_out), gain, route_ids.T, route_weights.T, *[in_hbm(w) for w in (queries, keys, values)])
    gathered = lax.all_gather(heads, "ctx", axis=0, tiled=True)
    came = lax.all_to_all(send, "ctx", split_axis=0, concat_axis=0, tiled=True)

    dense = call(
        dense_kernel,
        (shape(BLOCK, PIECE),) * 4,
        [SMEM, VMEM] + [HBM] * 4,
        scratch=[pltpu.VMEM((BLOCK, D), BF)] + [pltpu.VMEM((152, D), BF)] * 3 + [pltpu.SemaphoreType.DMA((16,))],
        flops=10 * 128 * 152 * D,
        bytes_accessed=6 * 10**6,
        mib=16,
        name="dense",
    )(me, mixed, *[in_hbm(w) for w in (grad_out, dense_gate, dense_up, dense_down)])
    peers = [to_tp(w) for w in experts]
    dense_keep, dense_give = sum_over_y(me, dense, "dense_sum")

    came, dense_keep, dense_give, peers = lax.optimization_barrier((came, dense_keep, dense_give, peers))
    own = call(compact_kernel, shape(320, PIECE), [VMEM], name="compact")(came)
    right, left = to_ep(own, 1, 0), to_ep(own, -1, 0)
    far = [to_ep(right[:160], 1, 0), to_ep(left[160:], -1, 0)]
    parts = call(
        expert_kernel,
        (shape(160, PIECE),) * 4,
        [SMEM] + [HBM] * 5 + [VMEM] * 6,
        scratch=[pltpu.VMEM((160, 2 * D), BF), pltpu.SemaphoreType.DMA((8,))],
        mib=16,
        flops=10 * 320 * 240 * D,
        bytes_accessed=18 * 10**6,
        name="expert",
    )(me, own, right, left, *far, *[in_vmem(w) for w in (*experts, *peers)])
    keep, give = sum_over_y(me, parts, "sum")
    back = call(expand_kernel, shape(256, CHUNK), [VMEM] * 2, name="expand")(keep, to_ep(give, 0, 1))
    back = lax.all_to_all(back.reshape(16, 16, CHUNK), "ctx", split_axis=0, concat_axis=0, tiled=True)

    stats, heads_out = call(
        stats_kernel,
        (shape(8, BLOCK, kind=F32), shape(2, HEAD_DIM, BLOCK, kind=F32)),
        [SMEM] + [VMEM] * 2,
        flops=4 * 2 * 2048 * 128 * 128,
        bytes_accessed=4 * 10**6,
        mib=16,
        name="stats",
    )(me, queries, gathered)

    back, stats, heads_out, dense_came = lax.optimization_barrier((back, stats, heads_out, to_ep(dense_give, 0, 1)))
    keep, give = call(
        combine_kernel,
        (shape(BLOCK, 256, kind=F32), shape(BLOCK, 256)),
        [SMEM] + [VMEM] * 4,
        name="combine",
    )(me, spots, back.reshape(256, CHUNK), dense_keep, dense_came)
    total = (keep + to_tp(give).astype(F32)).astype(BF)
    total = jnp.broadcast_to(total[None], (8, BLOCK, 256))
    total = lax.all_to_all(total, "ep", split_axis=0, concat_axis=0, tiled=True)
    grad_hidden, message = call(
        norm_kernel,
        (shape(BLOCK, D), shape(GRAY, 256)),
        [SMEM, VMEM, VMEM, VMEM, VMEM, VMEM, HBM, VMEM, VMEM],
        scratch=[pltpu.VMEM((BLOCK, D), BF), pltpu.VMEM((256, D), BF), pltpu.SemaphoreType.DMA((8,))],
        flops=4 * 128 * 256 * D,
        bytes_accessed=6 * 10**6,
        mib=16,
        name="norm",
    )(me, hidden, grad_out, gain, total, to_tp(total), in_hbm(out_proj), stats, heads_out)
    column = jnp.stack([message] + [to_ctx(message, -n, 0) for n in range(1, 4)])
    grad_q = call(
        queries_kernel,
        shape(BLOCK, 256),
        [SMEM] + [VMEM] * 3,
        scratch=[pltpu.VMEM((BLOCK, 256), F32)],
        flops=8 * 2 * 3 * 2 * 128**3,
        bytes_accessed=4 * 10**6,
        mib=16,
        name="queries",
    )(me, queries, gathered, message)

    def keys_part(shifts, columns, sums, first, last):
        return call(
            functools.partial(keys_kernel, shifts, first, last),
            (shape(BLOCK, 256, kind=BF if last else F32),) * 2,
            [SMEM] + [VMEM] * (1 + len(columns) + len(sums)),
            scratch=[pltpu.VMEM((BLOCK, 256), F32)] * 2,
            flops=4 * len(shifts) * 2 * 4 * 2 * 128**3,
            bytes_accessed=4 * 10**6,
            mib=16,
        name="keys",
        )(me, gathered, *columns, *sums)

    beside = [to_ctx(column, 0, -1), to_ctx(column, 0, 1)]
    opposite = to_ctx(column, 0, 2)
    sums = keys_part((0,), [column], [], True, False)
    sums = keys_part((1, 3), beside, sums, False, False)
    grad_k, grad_v = keys_part((2,), [opposite], sums, False, True)
    return grad_hidden, grad_q, grad_k, grad_v


def solution(mesh):
    return jax.shard_map(
        body,
        mesh=mesh,
        in_specs=(
            P("ctx", None),
            P("ctx", None),
            P(),
            P(("tp", "ep"), None),
            P(("tp", "ep"), None),
            P(("tp", "ep"), None),
            P("ctx", ("tp", "ep"), None),
            P("ctx", ("tp", "ep"), None),
            P("ctx", ("tp", "ep"), None),
            P(("tp", "ep"), None),
            P("ctx", ("tp", "ep")),
            P("ctx", ("tp", "ep")),
            P("ctx", ("tp", "ep")),
            P("ctx", None),
            P("ctx", None),
        ),
        out_specs=(
            P("ctx", None),
            P("ctx", ("tp", "ep")),
            P("ctx", ("tp", "ep")),
            P("ctx", ("tp", "ep")),
        ),
        check_vma=False,
    )
```

time: 217 us -> 189 us (0.87)
  blocking collectives: 47.1 us -> 13.7 us
  waiting for transfers between devices: 71.1 us -> 79.1 us
  local copies, waits for them, and re-layouts: 11 us -> 6.49 us
  Pallas kernels: 30.5 us -> 33.7 us
    all_to_all x2 -> x0, blocking collectives: 33.6 us -> none  [body(): lax.all_to_all(message, 'ctx', split_axis=0, concat_axis=0, tiled=True, a...]
    ppermute x0 -> x6, waiting for transfers between devices: none -> 23.8 us  [to_ctx(): return lax.ppermute(x, 'ctx', pairs)]
    all_to_all x2, waiting for transfers between devices: 28.4 us -> 8.36 us  [the longest x1 4.98 us: body(): lax.all_to_all(back.reshape(16, 16, CHUNK), 'ctx', split_axis=0, concat_a...]
    ppermute x0 -> x6, starting transfers between devices: none -> 7.63 us  [to_ctx(): return lax.ppermute(x, 'ctx', pairs)]
    ppermute x11 -> x12, waiting for transfers between devices: 38 us -> 43.8 us  [to_ep(): return lax.ppermute(x, 'ep', pairs)]
    ppermute x11 -> x12, starting transfers between devices: 23.1 us -> 18.5 us  [to_ep(): return lax.ppermute(x, 'ep', pairs)]
    unnamed x32 -> x26, local copies, waits for them, and re-layouts: 10.2 us -> 6.4 us
    pallas_call x9 -> x13, Pallas kernels: 27.8 us -> 31 us  [the longest x1 7.94 us: body(): call(expert_kernel, (shape(160, PIECE),) * 4, [SMEM] + [HBM] * 5 + [VMEM]...]
  transfers between devices with their start and end apart: 25 -> 26, of which waited for: 11 -> 17; matrix products, arithmetic and copies ran while one was open for 0% -> 0% of each run, Pallas kernels for 6% -> 12%
where the time goes in v2:
time: 189 us
  waiting for transfers between devices  79.1 us (42%)
  starting transfers between devices  41.2 us (22%)
  Pallas kernels  33.7 us (18%)
  between operations  14.3 us (8%)
  blocking collectives  13.7 us (7%)
  local copies, waits for them, and re-layouts  6.49 us (3%)
    ppermute x12, waiting for transfers between devices, to_ep(): return lax.ppermute(x, 'ep', pairs)  43.8 us
    ppermute x6, waiting for transfers between devices, to_ctx(): return lax.ppermute(x, 'ctx', pairs)  23.8 us
    ppermute x12, starting transfers between devices, to_ep(): return lax.ppermute(x, 'ep', pairs)  18.5 us
    all_to_all x1, blocking collectives, body(): total = lax.all_to_all(total, 'ep', split_axis=0, concat_axis=0, tiled=True)  13.7 us
    all_to_all x1, starting transfers between devices, body(): came = lax.all_to_all(send, 'ctx', split_axis=0, concat_axis=0, tiled=True)  10.1 us
    pallas_call x1, Pallas kernels, body(): call(expert_kernel, (shape(160, PIECE),) * 4, [SMEM] + [HBM] * 5 + [VMEM]...  7.94 us
    ppermute x6, starting transfers between devices, to_ctx(): return lax.ppermute(x, 'ctx', pairs)  7.63 us
    unnamed x26, local copies, waits for them, and re-layouts  6.4 us
  transfers between devices with their start and end apart: 26, of which 17 were waited for; matrix products, arithmetic and copies ran while one was open for 0% of the time, Pallas kernels for 12%

profile of v2, /device:TPU:32, one launch (start us, length us, event | category | flops | bytes accessed | tf_op | source)
XLA Modules:
  0.0 188.6 jit_solution(5187464899243700166)
XLA Ops:
  9.5 3.9 %prepare.1 = (bf16[128,3584]{1,0:T(8,128)(2,1)S(1)}, bf16[16,24,896]{2,1,0:T(8,128)(2,1)S(1)}, bf16[256,128]{1,0:T(8,128)(2,1)S(1)}, bf16[128,768]{1,0:T(8,128)(2,1)}) custom-call(s32[3]{0:T(128)S(1)} %pad_add_fusion.me, bf16[128,3584]{1,0:T(8,128)(2,1)} %hidden.3, bf16[128,3584]{1,0:T(8,128)(2,1)} %grad_out.5, f32[3584]{0:T(1024)S(1)} %copy-done.9, ...), custom_call_target="tpu_custom_call" | custom-call | flops 100000000 | bytes 4000000 | tf_op jit(solution)/shard_map/prepare/pallas_call | solution.py:408
  15.0 10.1 %all-to-all-start = ((bf16[16,24,896]{2,1,0:T(8,128)(2,1)}), bf16[16,24,896]{2,1,0:T(8,128)(2,1)S(1)}, u32[]{:S(2)}, u32[]{:S(2)}) async-start(bf16[16,24,896]{2,1,0:T(8,128)(2,1)} %copy-done.7), calls=%async_computation | async-start | bytes 1376256 | tf_op jit(solution)/shard_map/all_to_all | solution.py:419
  25.1 5.1 %dense.1 = (bf16[128,896]{1,0:T(8,128)(2,1)S(1)}, bf16[128,896]{1,0:T(8,128)(2,1)S(1)}, bf16[128,896]{1,0:T(8,128)(2,1)S(1)}, bf16[128,896]{1,0:T(8,128)(2,1)S(1)}) custom-call(s32[3]{0:T(128)S(1)} %pad_add_fusion.me, bf16[128,3584]{1,0:T(8,128)(2,1)S(1)} %get-tuple-element.44.mixed, bf16[128,3584]{1,0:T(8,128)(2,1)} %grad_out.5, bf16[152,3584]{1,0:T(8,128)(2,1)} %gate_in.1, ...), custom_call_target="tpu_custom_call" | custom-call | flops 697303040 | bytes 6000000 | tf_op jit(solution)/shard_map/dense/pallas_call | solution.py:421
  33.6 5.7 %collective-permute-done.second = bf16[128,896]{1,0:T(8,128)(2,1)S(1)} collective-permute-done((bf16[128,896]{1,0:T(8,128)(2,1)S(1)}, bf16[128,896]{1,0:T(8,128)(2,1)S(1)}, u32[]{:S(2)}, u32[]{:S(2)}) %collective-permute-start) | collective-permute-done | bytes 229408 | tf_op jit(solution)/shard_map/ppermute | solution.py:68
  39.3 1.9 %collective-permute-start.2 = (bf16[128,896]{1,0:T(8,128)(2,1)S(1)}, bf16[128,896]{1,0:T(8,128)(2,1)S(1)}, u32[]{:S(2)}, u32[]{:S(2)}) collective-permute-start(bf16[128,896]{1,0:T(8,128)(2,1)S(1)} %get-tuple-element.48), channel_id=1, source_target_pairs={{0,4},{1,5},{2,6},{3,7},{4,0},{5,1},{6,2},{7,3},{8,12},{9,13},{10,... | collective-permute-start | bytes 688136 | tf_op jit(solution)/shard_map/ppermute | solution.py:68
  41.2 6.6 %collective-permute-done.2.fourth = bf16[128,896]{1,0:T(8,128)(2,1)S(1)} collective-permute-done((bf16[128,896]{1,0:T(8,128)(2,1)S(1)}, bf16[128,896]{1,0:T(8,128)(2,1)S(1)}, u32[]{:S(2)}, u32[]{:S(2)}) %collective-permute-start.2) | collective-permute-done | bytes 229408 | tf_op jit(solution)/shard_map/ppermute | solution.py:68
  48.5 3.4 %all-to-all-done.came = bf16[16,24,896]{2,1,0:T(8,128)(2,1)S(1)} async-done(((bf16[16,24,896]{2,1,0:T(8,128)(2,1)}), bf16[16,24,896]{2,1,0:T(8,128)(2,1)S(1)}, u32[]{:S(2)}, u32[]{:S(2)}) %all-to-all-start) | async-done | bytes 688160 | tf_op jit(solution)/shard_map/all_to_all | solution.py:419
  53.9 1.8 collective-permute-start.7
  55.7 11.8 %collective-permute-done.6.right = bf16[320,896]{1,0:T(8,128)(2,1)S(1)} collective-permute-done((bf16[320,896]{1,0:T(8,128)(2,1)S(1)}, bf16[320,896]{1,0:T(8,128)(2,1)S(1)}, u32[]{:S(2)}, u32[]{:S(2)}) %collective-permute-start.6) | collective-permute-done | bytes 573472 | tf_op jit(solution)/shard_map/ppermute | solution.py:68
  68.0 3.1 %collective-permute-start.9 = (bf16[160,896]{1,0:T(8,128)(2,1)S(1)}, bf16[160,896]{1,0:T(8,128)(2,1)S(1)}, u32[]{:S(2)}, u32[]{:S(2)}) collective-permute-start(bf16[160,896]{1,0:T(8,128)(2,1)S(1)} %slice.9), channel_id=1, source_target_pairs={{0,6},{1,7},{2,0},{3,1},{4,2},{5,3},{6,4},{7,5},{8,14},{9,15},{10,... | collective-permute-start | bytes 860168 | tf_op jit(solution)/shard_map/ppermute | solution.py:68
  71.1 4.5 %collective-permute-done.8.far0 = bf16[160,896]{1,0:T(8,128)(2,1)S(1)} collective-permute-done((bf16[160,896]{1,0:T(8,128)(2,1)S(1)}, bf16[160,896]{1,0:T(8,128)(2,1)S(1)}, u32[]{:S(2)}, u32[]{:S(2)}) %collective-permute-start.8) | collective-permute-done | bytes 286752 | tf_op jit(solution)/shard_map/ppermute | solution.py:68
  77.1 7.9 %expert.1 = (bf16[160,896]{1,0:T(8,128)(2,1)S(1)}, bf16[160,896]{1,0:T(8,128)(2,1)S(1)}, bf16[160,896]{1,0:T(8,128)(2,1)S(1)}, bf16[160,896]{1,0:T(8,128)(2,1)S(1)}) custom-call(s32[3]{0:T(128)S(1)} %pad_add_fusion.me, bf16[320,896]{1,0:T(8,128)(2,1)S(1)} %compact.1.own, bf16[320,896]{1,0:T(8,128)(2,1)S(1)} %collective-permute-done.6.right, ...), custom_call_target="tpu_custom_call" | custom-call | flops 2752512000 | bytes 18000000 | tf_op jit(solution)/shard_map/expert/pallas_call | solution.py:438
  85.9 2.7 %collective-permute-start.11 = (bf16[160,896]{1,0:T(8,128)(2,1)S(1)}, bf16[160,896]{1,0:T(8,128)(2,1)S(1)}, u32[]{:S(2)}, u32[]{:S(2)}) collective-permute-start(bf16[160,896]{1,0:T(8,128)(2,1)S(1)} %get-tuple-element.57), channel_id=1, source_target_pairs={{0,6},{1,7},{2,0},{3,1},{4,2},{5,3},{6,4},{7,5},{8,14},{9,15},{10,... | collective-permute-start | bytes 860168 | tf_op jit(solution)/shard_map/ppermute | solution.py:68
  89.9 6.2 %collective-permute-done.10.second = bf16[160,896]{1,0:T(8,128)(2,1)S(1)} collective-permute-done((bf16[160,896]{1,0:T(8,128)(2,1)S(1)}, bf16[160,896]{1,0:T(8,128)(2,1)S(1)}, u32[]{:S(2)}, u32[]{:S(2)}) %collective-permute-start.10) | collective-permute-done | bytes 286752 | tf_op jit(solution)/shard_map/ppermute | solution.py:68
  96.2 1.8 collective-permute-done.11.third
  98.0 1.8 collective-permute-done.12.fourth
  100.7 5.3 %collective-permute-done.13.came = bf16[160,512]{1,0:T(8,128)(2,1)S(1)} collective-permute-done((bf16[160,512]{1,0:T(8,128)(2,1)S(1)}, bf16[160,512]{1,0:T(8,128)(2,1)S(1)}, u32[]{:S(2)}, u32[]{:S(2)}) %collective-permute-start.13) | collective-permute-done | bytes 163872 | tf_op jit(solution)/shard_map/ppermute | solution.py:68
  106.9 4.1 %all-to-all-start.1 = ((bf16[16,16,512]{2,1,0:T(8,128)(2,1)}), bf16[16,16,512]{2,1,0:T(8,128)(2,1)S(1)}, u32[]{:S(2)}, u32[]{:S(2)}) async-start(bf16[16,16,512]{2,1,0:T(8,128)(2,1)} %bitcast.8), calls=%async_computation.1 | async-start | bytes 524288 | tf_op jit(solution)/shard_map/all_to_all | solution.py:450
  112.5 1.9 %copy-done = bf16[2048,768]{1,0:T(8,128)(2,1)S(1)} copy-done((bf16[2048,768]{1,0:T(8,128)(2,1)S(1)}, bf16[2048,768]{1,0:T(8,128)(2,1)}, u32[]{:S(2)}) %copy-start) | copy-done | bytes 3145752
  114.4 2.7 %stats.1 = (f32[8,128]{1,0:T(8,128)S(1)}, f32[2,128,128]{2,1,0:T(8,128)S(1)}) custom-call(s32[3]{0:T(128)S(1)} %pad_add_fusion.me, bf16[128,256]{1,0:T(8,128)(2,1)S(1)} %copy-done.8, bf16[2048,768]{1,0:T(8,128)(2,1)S(1)} %copy-done), custom_call_target="tpu_custom_call" | custom-call | flops 268435456 | bytes 4000000 | tf_op jit(solution)/shard_map/stats/pallas_call | solution.py:452
  117.1 5.0 %all-to-all-done.1 = bf16[16,16,512]{2,1,0:T(8,128)(2,1)S(1)} async-done(((bf16[16,16,512]{2,1,0:T(8,128)(2,1)}), bf16[16,16,512]{2,1,0:T(8,128)(2,1)S(1)}, u32[]{:S(2)}, u32[]{:S(2)}) %all-to-all-start.1) | async-done | bytes 262176 | tf_op jit(solution)/shard_map/all_to_all | solution.py:450
  124.3 13.7 %all_to_all.15.mine = bf16[8,128,256]{2,1,0:T(8,128)(2,1)S(1)} all-to-all(bf16[8,128,256]{2,1,0:T(8,128)(2,1)S(1)} %broadcast_in_dim.2), channel_id=1, replica_groups=mesh['ctx'=16,'tp'=2,'ep'=8] {'ep'}, dimensions={0} | all-to-all | bytes 1048576 | tf_op jit(solution)/shard_map/all_to_all | solution.py:471
  137.9 1.9 %collective-permute-done.16.other = bf16[8,128,256]{2,1,0:T(8,128)(2,1)S(1)} collective-permute-done((bf16[8,128,256]{2,1,0:T(8,128)(2,1)S(1)}, bf16[8,128,256]{2,1,0:T(8,128)(2,1)S(1)}, u32[]{:S(2)}, u32[]{:S(2)}) %collective-permute-start.16) | collective-permute-done | bytes 524320 | tf_op jit(solution)/shard_map/ppermute | solution.py:63
  139.8 3.6 %norm.1 = (bf16[128,3584]{1,0:T(8,128)(2,1)}, bf16[144,256]{1,0:T(8,128)(2,1)S(1)}) custom-call(s32[3]{0:T(128)S(1)} %pad_add_fusion.me, bf16[128,3584]{1,0:T(8,128)(2,1)S(1)} %copy-done.3, bf16[128,3584]{1,0:T(8,128)(2,1)S(1)} %copy-done.2, f32[3584]{0:T(1024)S(1)} %copy-done.10, bf16[8,128,256]{2,1,0:T(8,128)(2,1)S(1)} %all_to_all.15.mine, ...), custom_call_target="tpu_custom_call" | custom-call | flops 469762048 | bytes 6000000 | tf_op jit(solution)/shard_map/norm/pallas_call | solution.py:472
  147.4 3.3 %collective-permute-done.17 = bf16[144,256]{1,0:T(8,128)(2,1)S(1)} collective-permute-done((bf16[144,256]{1,0:T(8,128)(2,1)S(1)}, bf16[144,256]{1,0:T(8,128)(2,1)S(1)}, u32[]{:S(2)}, u32[]{:S(2)}) %collective-permute-start.17) | collective-permute-done | bytes 73760 | tf_op jit(solution)/shard_map/ppermute | solution.py:75
  150.7 5.1 %collective-permute-done.18 = bf16[144,256]{1,0:T(8,128)(2,1)S(1)} collective-permute-done((bf16[144,256]{1,0:T(8,128)(2,1)S(1)}, bf16[144,256]{1,0:T(8,128)(2,1)S(1)}, u32[]{:S(2)}, u32[]{:S(2)}) %collective-permute-start.18) | collective-permute-done | bytes 73760 | tf_op jit(solution)/shard_map/ppermute | solution.py:75
  155.8 4.5 %collective-permute-done.19 = bf16[144,256]{1,0:T(8,128)(2,1)S(1)} collective-permute-done((bf16[144,256]{1,0:T(8,128)(2,1)S(1)}, bf16[144,256]{1,0:T(8,128)(2,1)S(1)}, u32[]{:S(2)}, u32[]{:S(2)}) %collective-permute-start.19) | collective-permute-done | bytes 73760 | tf_op jit(solution)/shard_map/ppermute | solution.py:75
  164.1 1.9 %queries.3 = bf16[128,256]{1,0:T(8,128)(2,1)} custom-call(s32[3]{0:T(128)S(1)} %pad_add_fusion.me, bf16[128,256]{1,0:T(8,128)(2,1)S(1)} %copy-done.8, bf16[2048,768]{1,0:T(8,128)(2,1)S(1)} %copy-done.1, bf16[144,256]{1,0:T(8,128)(2,1)S(1)} %get-tuple-element.73.message), custom_call_target="tpu_custom_call" | custom-call | flops 201326592 | bytes 4000000 | tf_op jit(solution)/shard_map/queries/pallas_call | solution.py:483
  167.2 3.0 %collective-permute-done.21.refs_0_ = bf16[4,144,256]{2,1,0:T(8,128)(2,1)S(1)} collective-permute-done((bf16[4,144,256]{2,1,0:T(8,128)(2,1)S(1)}, bf16[4,144,256]{2,1,0:T(8,128)(2,1)S(1)}, u32[]{:S(2)}, u32[]{:S(2)}) %collective-permute-start.21) | collective-permute-done | bytes 294944 | tf_op jit(solution)/shard_map/ppermute | solution.py:75
  170.3 7.8 %collective-permute-done.22.refs_1_ = bf16[4,144,256]{2,1,0:T(8,128)(2,1)S(1)} collective-permute-done((bf16[4,144,256]{2,1,0:T(8,128)(2,1)S(1)}, bf16[4,144,256]{2,1,0:T(8,128)(2,1)S(1)}, u32[]{:S(2)}, u32[]{:S(2)}) %collective-permute-start.22) | collective-permute-done | bytes 294944 | tf_op jit(solution)/shard_map/ppermute | solution.py:75
  178.1 1.8 keys.6
  179.9 1.9 keys.7
  (68 shorter events, 28.3 us)
Async XLA Ops:
  7.2 105.3 %all-gather.2.cloned.1.call-start = ((), (), s32[]{:S(2)}) async-start(), calls=%async_computation.3 | async-start | bytes 3342336 | tf_op jit(solution)/shard_map/all_gather | solution.py:418
  14.3 37.6 %collective-permute-start.3 = (bf16[240,3584]{1,0:T(8,128)(2,1)S(1)}, bf16[240,3584]{1,0:T(8,128)(2,1)}, u32[]{:S(2)}, u32[]{:S(2)}) collective-permute-start(bf16[240,3584]{1,0:T(8,128)(2,1)S(1)} %bitcast.14), channel_id=1, source_target_pairs={{0,8},{8,0},{1,9},{9,1},{2,10},{10,2},{3,11},{11,3},{4,12},{12,4},... | collective-permute-start | bytes 5160968 | tf_op jit(solution)/shard_map/ppermute | solution.py:63
  14.4 37.5 %collective-permute-start.4 = (bf16[240,3584]{1,0:T(8,128)(2,1)}, bf16[240,3584]{1,0:T(8,128)(2,1)}, u32[]{:S(2)}, u32[]{:S(2)}) collective-permute-start(bf16[240,3584]{1,0:T(8,128)(2,1)} %bitcast.16), channel_id=1, source_target_pairs={{0,8},{8,0},{1,9},{9,1},{2,10},{10,2},{3,11},{11,3},{4,12},{12,4},... | collective-permute-start | bytes 5160968 | tf_op jit(solution)/shard_map/ppermute | solution.py:63
  14.9 37.0 %collective-permute-start.5 = (bf16[240,3584]{1,0:T(8,128)(2,1)}, bf16[240,3584]{1,0:T(8,128)(2,1)}, u32[]{:S(2)}, u32[]{:S(2)}) collective-permute-start(bf16[240,3584]{1,0:T(8,128)(2,1)} %bitcast.18), channel_id=1, source_target_pairs={{0,8},{8,0},{1,9},{9,1},{2,10},{10,2},{3,11},{11,3},{4,12},{12,4},... | collective-permute-start | bytes 5160968 | tf_op jit(solution)/shard_map/ppermute | solution.py:63
  15.0 36.9 %all-to-all-start = ((bf16[16,24,896]{2,1,0:T(8,128)(2,1)}), bf16[16,24,896]{2,1,0:T(8,128)(2,1)S(1)}, u32[]{:S(2)}, u32[]{:S(2)}) async-start(bf16[16,24,896]{2,1,0:T(8,128)(2,1)} %copy-done.7), calls=%async_computation | async-start | bytes 1376256 | tf_op jit(solution)/shard_map/all_to_all | solution.py:419
  30.3 9.0 %collective-permute-start = (bf16[128,896]{1,0:T(8,128)(2,1)S(1)}, bf16[128,896]{1,0:T(8,128)(2,1)S(1)}, u32[]{:S(2)}, u32[]{:S(2)}) collective-permute-start(bf16[128,896]{1,0:T(8,128)(2,1)S(1)} %get-tuple-element.46), channel_id=1, source_target_pairs={{0,2},{1,3},{2,4},{3,5},{4,6},{5,7},{6,0},{7,1},{8,10},{9,11},{10,... | collective-permute-start | bytes 688136 | tf_op jit(solution)/shard_map/ppermute | solution.py:68
  31.9 9.3 %collective-permute-start.1 = (bf16[128,896]{1,0:T(8,128)(2,1)S(1)}, bf16[128,896]{1,0:T(8,128)(2,1)S(1)}, u32[]{:S(2)}, u32[]{:S(2)}) collective-permute-start(bf16[128,896]{1,0:T(8,128)(2,1)S(1)} %get-tuple-element.47), channel_id=1, source_target_pairs={{0,6},{1,7},{2,0},{3,1},{4,2},{5,3},{6,4},{7,5},{8,14},{9,15},{10,... | collective-permute-start | bytes 688136 | tf_op jit(solution)/shard_map/ppermute | solution.py:68
  39.3 8.5 %collective-permute-start.2 = (bf16[128,896]{1,0:T(8,128)(2,1)S(1)}, bf16[128,896]{1,0:T(8,128)(2,1)S(1)}, u32[]{:S(2)}, u32[]{:S(2)}) collective-permute-start(bf16[128,896]{1,0:T(8,128)(2,1)S(1)} %get-tuple-element.48), channel_id=1, source_target_pairs={{0,4},{1,5},{2,6},{3,7},{4,0},{5,1},{6,2},{7,3},{8,12},{9,13},{10,... | collective-permute-start | bytes 688136 | tf_op jit(solution)/shard_map/ppermute | solution.py:68
  51.8 23.8 %copy-start.5 = (bf16[1,240,3584]{2,1,0:T(8,128)(2,1)S(1)}, bf16[1,240,3584]{2,1,0:T(8,128)(2,1)}, u32[]{:S(2)}) copy-start(bf16[1,240,3584]{2,1,0:T(8,128)(2,1)} %param.22) | copy-start | bytes 5160964
  52.4 15.2 %collective-permute-start.6 = (bf16[320,896]{1,0:T(8,128)(2,1)S(1)}, bf16[320,896]{1,0:T(8,128)(2,1)S(1)}, u32[]{:S(2)}, u32[]{:S(2)}) collective-permute-start(bf16[320,896]{1,0:T(8,128)(2,1)S(1)} %compact.1.own), channel_id=1, source_target_pairs={{0,2},{1,3},{2,4},{3,5},{4,6},{5,7},{6,0},{7,1},{8,10},{9,11},{10,... | collective-permute-start | bytes 1720328 | tf_op jit(solution)/shard_map/ppermute | solution.py:68
  53.9 14.1 %collective-permute-start.7 = (bf16[320,896]{1,0:T(8,128)(2,1)S(1)}, bf16[320,896]{1,0:T(8,128)(2,1)S(1)}, u32[]{:S(2)}, u32[]{:S(2)}) collective-permute-start(bf16[320,896]{1,0:T(8,128)(2,1)S(1)} %compact.1.own), channel_id=1, source_target_pairs={{0,6},{1,7},{2,0},{3,1},{4,2},{5,3},{6,4},{7,5},{8,14},{9,15},{10,... | collective-permute-start | bytes 1720328 | tf_op jit(solution)/shard_map/ppermute | solution.py:68
  67.5 8.1 %collective-permute-start.8 = (bf16[160,896]{1,0:T(8,128)(2,1)S(1)}, bf16[160,896]{1,0:T(8,128)(2,1)S(1)}, u32[]{:S(2)}, u32[]{:S(2)}) collective-permute-start(bf16[160,896]{1,0:T(8,128)(2,1)S(1)} %slice.8), channel_id=1, source_target_pairs={{0,2},{1,3},{2,4},{3,5},{4,6},{5,7},{6,0},{7,1},{8,10},{9,11},{10,... | collective-permute-start | bytes 860168 | tf_op jit(solution)/shard_map/ppermute | solution.py:68
  68.0 7.6 %collective-permute-start.9 = (bf16[160,896]{1,0:T(8,128)(2,1)S(1)}, bf16[160,896]{1,0:T(8,128)(2,1)S(1)}, u32[]{:S(2)}, u32[]{:S(2)}) collective-permute-start(bf16[160,896]{1,0:T(8,128)(2,1)S(1)} %slice.9), channel_id=1, source_target_pairs={{0,6},{1,7},{2,0},{3,1},{4,2},{5,3},{6,4},{7,5},{8,14},{9,15},{10,... | collective-permute-start | bytes 860168 | tf_op jit(solution)/shard_map/ppermute | solution.py:68
  85.0 27.4 %copy-start.8 = (bf16[128,256]{1,0:T(8,128)(2,1)S(1)}, bf16[128,256]{1,0:T(8,128)(2,1)}, u32[]{:S(2)}) copy-start(bf16[128,256]{1,0:T(8,128)(2,1)} %own_q.1) | copy-start | bytes 196612
  85.1 11.1 %collective-permute-start.10 = (bf16[160,896]{1,0:T(8,128)(2,1)S(1)}, bf16[160,896]{1,0:T(8,128)(2,1)S(1)}, u32[]{:S(2)}, u32[]{:S(2)}) collective-permute-start(bf16[160,896]{1,0:T(8,128)(2,1)S(1)} %get-tuple-element.56), channel_id=1, source_target_pairs={{0,2},{1,3},{2,4},{3,5},{4,6},{5,7},{6,0},{7,1},{8,10},{9,11},{10,... | collective-permute-start | bytes 860168 | tf_op jit(solution)/shard_map/ppermute | solution.py:68
  85.9 12.1 %collective-permute-start.11 = (bf16[160,896]{1,0:T(8,128)(2,1)S(1)}, bf16[160,896]{1,0:T(8,128)(2,1)S(1)}, u32[]{:S(2)}, u32[]{:S(2)}) collective-permute-start(bf16[160,896]{1,0:T(8,128)(2,1)S(1)} %get-tuple-element.57), channel_id=1, source_target_pairs={{0,6},{1,7},{2,0},{3,1},{4,2},{5,3},{6,4},{7,5},{8,14},{9,15},{10,... | collective-permute-start | bytes 860168 | tf_op jit(solution)/shard_map/ppermute | solution.py:68
  88.6 11.3 %collective-permute-start.12 = (bf16[160,896]{1,0:T(8,128)(2,1)S(1)}, bf16[160,896]{1,0:T(8,128)(2,1)S(1)}, u32[]{:S(2)}, u32[]{:S(2)}) collective-permute-start(bf16[160,896]{1,0:T(8,128)(2,1)S(1)} %get-tuple-element.58), channel_id=1, source_target_pairs={{0,4},{1,5},{2,6},{3,7},{4,0},{5,1},{6,2},{7,3},{8,12},{9,13},{10,... | collective-permute-start | bytes 860168 | tf_op jit(solution)/shard_map/ppermute | solution.py:68
  100.6 5.4 %collective-permute-start.13 = (bf16[160,512]{1,0:T(8,128)(2,1)S(1)}, bf16[160,512]{1,0:T(8,128)(2,1)S(1)}, u32[]{:S(2)}, u32[]{:S(2)}) collective-permute-start(bf16[160,512]{1,0:T(8,128)(2,1)S(1)} %get-tuple-element.60), channel_id=1, source_target_pairs={{0,1},{1,0},{2,3},{3,2},{4,5},{5,4},{6,7},{7,6},{8,9},{9,8},{10,11... | collective-permute-start | bytes 491528 | tf_op jit(solution)/shard_map/ppermute | solution.py:68
  106.9 15.2 %all-to-all-start.1 = ((bf16[16,16,512]{2,1,0:T(8,128)(2,1)}), bf16[16,16,512]{2,1,0:T(8,128)(2,1)S(1)}, u32[]{:S(2)}, u32[]{:S(2)}) async-start(bf16[16,16,512]{2,1,0:T(8,128)(2,1)} %bitcast.8), calls=%async_computation.1 | async-start | bytes 524288 | tf_op jit(solution)/shard_map/all_to_all | solution.py:450
  111.1 6.0 %collective-permute-start.14 = (bf16[128,512]{1,0:T(8,128)(2,1)S(1)}, bf16[128,512]{1,0:T(8,128)(2,1)S(1)}, u32[]{:S(2)}, u32[]{:S(2)}) collective-permute-start(bf16[128,512]{1,0:T(8,128)(2,1)S(1)} %get-tuple-element.64), channel_id=1, source_target_pairs={{0,1},{1,0},{2,3},{3,2},{4,5},{5,4},{6,7},{7,6},{8,9},{9,8},{10,11... | collective-permute-start | bytes 393224 | tf_op jit(solution)/shard_map/ppermute | solution.py:68
  117.0 22.8 %copy-start.2 = (bf16[128,3584]{1,0:T(8,128)(2,1)S(1)}, bf16[128,3584]{1,0:T(8,128)(2,1)}, u32[]{:S(2)}) copy-start(bf16[128,3584]{1,0:T(8,128)(2,1)} %grad_out.5) | copy-start | bytes 2752516
  117.1 22.8 %copy-start.3 = (bf16[128,3584]{1,0:T(8,128)(2,1)S(1)}, bf16[128,3584]{1,0:T(8,128)(2,1)}, u32[]{:S(2)}) copy-start(bf16[128,3584]{1,0:T(8,128)(2,1)} %hidden.3) | copy-start | bytes 2752516
  117.1 22.8 %copy-start.10 = (f32[3584]{0:T(1024)S(1)}, f32[3584]{0:T(1024)}, u32[]{:S(2)}) copy-start(f32[3584]{0:T(1024)} %gain.3) | copy-start | bytes 43012
  122.8 1.3 collective-permute-start.15
  137.9 26.2 %copy-start.1 = (bf16[2048,768]{1,0:T(8,128)(2,1)S(1)}, bf16[2048,768]{1,0:T(8,128)(2,1)}, u32[]{:S(2)}) copy-start(bf16[2048,768]{1,0:T(8,128)(2,1)} %all-gather.2.cloned.1.call-done.gathered) | copy-start | bytes 9437188
  137.9 1.9 %collective-permute-start.16 = (bf16[8,128,256]{2,1,0:T(8,128)(2,1)S(1)}, bf16[8,128,256]{2,1,0:T(8,128)(2,1)S(1)}, u32[]{:S(2)}, u32[]{:S(2)}) collective-permute-start(bf16[8,128,256]{2,1,0:T(8,128)(2,1)S(1)} %all_to_all.15.mine), channel_id=1, source_target_pairs={{0,8},{8,0},{1,9},{9,1},{2,10},{10,2},{3,11},{11,3},{4,12},{12,4},... | collective-permute-start | bytes 1572872 | tf_op jit(solution)/shard_map/ppermute | solution.py:63
  143.5 7.2 %collective-permute-start.17 = (bf16[144,256]{1,0:T(8,128)(2,1)S(1)}, bf16[144,256]{1,0:T(8,128)(2,1)S(1)}, u32[]{:S(2)}, u32[]{:S(2)}) collective-permute-start(bf16[144,256]{1,0:T(8,128)(2,1)S(1)} %get-tuple-element.73.message), channel_id=1, source_target_pairs={{64,0},{80,16},{96,32},{112,48},{128,64},{144,80},{160,96},{176,11... | collective-permute-start | bytes 221192 | tf_op jit(solution)/shard_map/ppermute | solution.py:75
  144.8 11.0 %collective-permute-start.18 = (bf16[144,256]{1,0:T(8,128)(2,1)S(1)}, bf16[144,256]{1,0:T(8,128)(2,1)S(1)}, u32[]{:S(2)}, u32[]{:S(2)}) collective-permute-start(bf16[144,256]{1,0:T(8,128)(2,1)S(1)} %get-tuple-element.73.message), channel_id=1, source_target_pairs={{128,0},{144,16},{160,32},{176,48},{192,64},{208,80},{224,96},{240... | collective-permute-start | bytes 221192 | tf_op jit(solution)/shard_map/ppermute | solution.py:75
  146.1 14.2 %collective-permute-start.19 = (bf16[144,256]{1,0:T(8,128)(2,1)S(1)}, bf16[144,256]{1,0:T(8,128)(2,1)S(1)}, u32[]{:S(2)}, u32[]{:S(2)}) collective-permute-start(bf16[144,256]{1,0:T(8,128)(2,1)S(1)} %get-tuple-element.73.message), channel_id=1, source_target_pairs={{192,0},{208,16},{224,32},{240,48},{193,1},{209,17},{225,33},{241,... | collective-permute-start | bytes 221192 | tf_op jit(solution)/shard_map/ppermute | solution.py:75
  160.3 9.9 %collective-permute-start.21 = (bf16[4,144,256]{2,1,0:T(8,128)(2,1)S(1)}, bf16[4,144,256]{2,1,0:T(8,128)(2,1)S(1)}, u32[]{:S(2)}, u32[]{:S(2)}) collective-permute-start(bf16[4,144,256]{2,1,0:T(8,128)(2,1)S(1)} %pad_maximum_fusion.refs_0_), channel_id=1, source_target_pairs={{0,48},{16,0},{32,16},{48,32},{64,112},{80,64},{96,80},{112,96},{1... | collective-permute-start | bytes 884744 | tf_op jit(solution)/shard_map/ppermute | solution.py:75
  161.9 16.2 %collective-permute-start.22 = (bf16[4,144,256]{2,1,0:T(8,128)(2,1)S(1)}, bf16[4,144,256]{2,1,0:T(8,128)(2,1)S(1)}, u32[]{:S(2)}, u32[]{:S(2)}) collective-permute-start(bf16[4,144,256]{2,1,0:T(8,128)(2,1)S(1)} %pad_maximum_fusion.refs_0_), channel_id=1, source_target_pairs={{0,16},{16,32},{32,48},{48,0},{64,80},{80,96},{96,112},{112,64},{1... | collective-permute-start | bytes 884744 | tf_op jit(solution)/shard_map/ppermute | solution.py:75
  162.4 17.5 %collective-permute-start.20 = (bf16[4,144,256]{2,1,0:T(8,128)(2,1)S(1)}, bf16[4,144,256]{2,1,0:T(8,128)(2,1)S(1)}, u32[]{:S(2)}, u32[]{:S(2)}) collective-permute-start(bf16[4,144,256]{2,1,0:T(8,128)(2,1)S(1)} %pad_maximum_fusion.refs_0_), channel_id=1, source_target_pairs={{0,32},{16,48},{32,0},{48,16},{64,96},{80,112},{96,64},{112,80},{1... | collective-permute-start | bytes 884744 | tf_op jit(solution)/shard_map/ppermute | solution.py:75
  (7 other events, 13.5 us)
Sparse Core Ops, SparseCore 0:
  14.4 75.8 all-gather.1

commit v3 on v2

--- a/solution.py
+++ b/solution.py
@@ -20,6 +20,7 @@
 STRIDE = 24
 SCALE = HEAD_DIM ** (-0.5)
 CHUNKS = D // CHUNK
+COLUMNS = [[4 * z + x for z in range(4)] for x in range(4)]
 GRAY = 144
 VMEM = pl.BlockSpec(memory_space=pltpu.VMEM)
 SMEM = pl.BlockSpec(memory_space=pltpu.SMEM)
@@ -55,10 +56,6 @@
     return pltpu.with_memory_space_constraint(x, pltpu.HBM)
 
 
-def in_vmem(x):
-    return pltpu.with_memory_space_constraint(x, pltpu.VMEM)
-
-
 def to_tp(x):
     return lax.ppermute(x, "tp", [(0, 1), (1, 0)])
 
@@ -68,11 +65,8 @@
     return lax.ppermute(x, "ep", pairs)
 
 
-def to_ctx(x, dz, dx):
-    pairs = [
-        (z * 4 + q, (z + dz) * 4 + (q + dx) % 4) for z in range(4) for q in range(4) if 0 <= z + dz < 4
-    ]
-    return lax.ppermute(x, "ctx", pairs)
+def to_ctx(x, dx):
+    return lax.ppermute(x, "ctx", [(z * 4 + q, z * 4 + (q + dx) % 4) for z in range(4) for q in range(4)])
 
 
 def sum_over_y(me, parts, name):
@@ -157,16 +151,17 @@
     out[...] = nn(pick, rows).astype(BF)
 
 
-def hidden_grads(x, y, gate, up, down):
-    a = nt(x, gate)
-    b = nt(x, up)
-    back = nt(y, down)
+def gate_grads(a, b, back):
     s = jax.nn.sigmoid(a)
     ga = (back * b * s * (1.0 + a * (1.0 - s))).astype(BF)
     gb = (back * a * s).astype(BF)
     return ga, gb
 
 
+def hidden_grads(x, y, gate, up, down):
+    return gate_grads(nt(x, gate), nt(x, up), nt(y, down))
+
+
 def piece_lanes(index):
     return pl.ds(pl.multiple_of(index * PIECE, PIECE), PIECE)
 
@@ -174,43 +169,49 @@
 def dense_kernel(me, mixed, grad_out, gate_in, up_in, down_in, *refs):
     outs, (grad_rows, gate, up, down, sems) = refs[:4], refs[4:]
     copies = []
-    for source, target in ((gate_in, gate), (up_in, up), (down_in, down), (grad_out, grad_rows)):
+    for source, target in ((gate_in, gate), (up_in, up), (grad_out, grad_rows), (down_in, down)):
         for start in range(0, D, PIECE):
             part = pl.ds(start, PIECE)
             copies.append(pltpu.make_async_copy(source.at[:, part], target.at[:, part], sems.at[len(copies)]))
-    for copy in copies:
-        copy.start()
-    for copy in copies:
+            copies[-1].start()
+    for copy in copies[:4]:
         copy.wait()
+    a = nt(mixed[...], gate[...])
+    for copy in copies[4:8]:
+        copy.wait()
+    b = nt(mixed[...], up[...])
+    for copy in copies[8:]:
+        copy.wait()
+    ga, gb = gate_grads(a, b, nt(grad_rows[...], down[...]))
     y = me[2] // 2
-    ga, gb = hidden_grads(mixed[...], grad_rows[...], gate[...], up[...], down[...])
     for d, out in enumerate(outs):
         lanes = piece_lanes((y + d) % 4)
         out[...] = (nn(ga, gate[:, lanes]) + nn(gb, up[:, lanes])).astype(BF)
 
 
+def load_kernel(*refs):
+    count = (len(refs) - 1) // 2
+    sems = refs[-1]
+    copies = []
+    for source, target in zip(refs[:count], refs[count:-1]):
+        for n in range(3):
+            part = pl.ds(n * 80, 80)
+            copies.append(pltpu.make_async_copy(source.at[part], target.at[part], sems.at[len(copies)]))
+            copies[-1].start()
+    for copy in copies:
+        copy.wait()
+
+
 def expert_kernel(me, own, right, left, far0, far1, gate, up, down, gate2, up2, down2, *refs):
-    outs, (rows, sems) = refs[:4], refs[4:]
+    outs, rows = refs[:4], refs[4]
     y = me[2] // 2
-
-    def copy(block, from_row, dy, h, n):
-        target = rows.at[:, piece_lanes(((y + dy) % 4) * 2 + h)]
-        return pltpu.make_async_copy(block.at[pl.ds(from_row, 160)], target, sems.at[n])
-
-    copies = [
-        copy(own, 0, 0, 0, 0),
-        copy(own, 160, 0, 1, 1),
-        copy(right, 0, 3, 0, 2),
-        copy(right, 160, 3, 1, 3),
-        copy(left, 0, 1, 0, 4),
-        copy(left, 160, 1, 1, 5),
-        copy(far0, 0, 2, 0, 6),
-        copy(far1, 0, 2, 1, 7),
-    ]
-    for c in copies:
-        c.start()
-    for c in copies:
-        c.wait()
+    for h in range(2):
+        part = slice(h * 160, (h + 1) * 160)
+        rows[:, piece_lanes(y * 2 + h)] = own[part, :]
+        rows[:, piece_lanes((y + 3) % 4 * 2 + h)] = right[part, :]
+        rows[:, piece_lanes((y + 1) % 4 * 2 + h)] = left[part, :]
+    rows[:, piece_lanes((y + 2) % 4 * 2)] = far0[...]
+    rows[:, piece_lanes((y + 2) % 4 * 2 + 1)] = far1[...]
     x, g = rows[:, :D], rows[:, D:]
     ga, gb = hidden_grads(x, g, gate[...], up[...], down[...])
     ga2, gb2 = hidden_grads(x, g, gate2[...], up2[...], down2[...])
@@ -277,15 +278,17 @@
     for copy in copies:
         copy.wait()
     heads = nt(grad, out_proj[...]).astype(BF)
-    heads_t = nt(out_proj[...], grad).astype(BF).astype(F32)
     rows = []
     for h in range(2):
-        delta = jnp.sum(heads_t[h * HEAD_DIM : (h + 1) * HEAD_DIM] * heads_out[h], axis=0, keepdims=True)
+        heads_t = jnp.transpose(heads[:, head(h)].astype(F32))
+        delta = jnp.sum(heads_t * heads_out[h], axis=0, keepdims=True)
         rows.append(list(split3(stats[h : h + 1, :])) + list(split3(delta)))
-    message[:BLOCK, :] = heads
-    message[BLOCK:, :] = jnp.concatenate(
+    extra = jnp.concatenate(
         [jnp.concatenate([rows[0][k], rows[1][k]], axis=1) for k in range(6)] + [jnp.zeros((10, 256), F32)], axis=0
     ).astype(BF)
+    for n in range(4):
+        message[n, :BLOCK, :] = heads
+        message[n, BLOCK:, :] = extra
 
 
 def stats_kernel(me, own, gathered, stats, heads_out):
@@ -319,8 +322,9 @@
     return slice(start + h * HEAD_DIM, start + (h + 1) * HEAD_DIM)
 
 
-def queries_kernel(me, own_q, gathered, message, grad_q, total):
+def queries_kernel(me, own_q, gathered, grads, grad_q, total):
     block = me[0]
+    message = grads.at[block // 4]
     lines = message[BLOCK:, :].astype(F32)
     query_at = lax.broadcasted_iota(jnp.int32, (512, BLOCK), 1) + block * BLOCK
     total[...] = jnp.zeros_like(total)
@@ -351,15 +355,13 @@
         sum_k[...] = in_k[...]
         sum_v[...] = in_v[...]
     block = me[0]
-    x, z = block % 4, block // 4
     own_rows = pl.ds(pl.multiple_of(block * BLOCK, BLOCK), BLOCK)
     lane = lax.broadcasted_iota(jnp.int32, (BLOCK, 4 * BLOCK), 1)
     key_at = lax.broadcasted_iota(jnp.int32, (BLOCK, 4 * BLOCK), 0) + block * BLOCK
-    row = z + lane // BLOCK
     for shift, source in zip(shifts, grads):
-        column = (x + shift) % 4
-        allowed = (row < 4) & (key_at <= (row * 4 + column) * BLOCK + lane % BLOCK)
-        blocks = [jnp.minimum((z + n) * 4 + column, 15) for n in range(4)]
+        column = (block + shift) % 4
+        allowed = key_at <= (lane // BLOCK * 4 + column) * BLOCK + lane % BLOCK
+        blocks = [n * 4 + column for n in range(4)]
         queries = jnp.concatenate(
             [gathered[pl.ds(pl.multiple_of(i * BLOCK, BLOCK), BLOCK), :256] for i in blocks], axis=0
         )
@@ -431,20 +433,29 @@
     peers = [to_tp(w) for w in experts]
     dense_keep, dense_give = sum_over_y(me, dense, "dense_sum")
 
-    came, dense_keep, dense_give, peers = lax.optimization_barrier((came, dense_keep, dense_give, peers))
+    came, dense_keep, dense_give = lax.optimization_barrier((came, dense_keep, dense_give))
     own = call(compact_kernel, shape(320, PIECE), [VMEM], name="compact")(came)
     right, left = to_ep(own, 1, 0), to_ep(own, -1, 0)
     far = [to_ep(right[:160], 1, 0), to_ep(left[160:], -1, 0)]
+    *weights, _ = lax.optimization_barrier((*experts, *peers, own))
+    weights = call(
+        load_kernel,
+        (shape(240, D),) * 6,
+        [HBM] * 6,
+        scratch=[pltpu.SemaphoreType.DMA((18,))],
+        bytes_accessed=10**7,
+        name="load",
+    )(*[in_hbm(w) for w in weights])
     parts = call(
         expert_kernel,
         (shape(160, PIECE),) * 4,
-        [SMEM] + [HBM] * 5 + [VMEM] * 6,
-        scratch=[pltpu.VMEM((160, 2 * D), BF), pltpu.SemaphoreType.DMA((8,))],
+        [SMEM] + [VMEM] * 11,
+        scratch=[pltpu.VMEM((160, 2 * D), BF)],
         mib=16,
         flops=10 * 320 * 240 * D,
         bytes_accessed=18 * 10**6,
         name="expert",
-    )(me, own, right, left, *far, *[in_vmem(w) for w in (*experts, *peers)])
+    )(me, own, right, left, *far, *weights)
     keep, give = sum_over_y(me, parts, "sum")
     back = call(expand_kernel, shape(256, CHUNK), [VMEM] * 2, name="expand")(keep, to_ep(give, 0, 1))
     back = lax.all_to_all(back.reshape(16, 16, CHUNK), "ctx", split_axis=0, concat_axis=0, tiled=True)
@@ -471,7 +482,7 @@
     total = lax.all_to_all(total, "ep", split_axis=0, concat_axis=0, tiled=True)
     grad_hidden, message = call(
         norm_kernel,
-        (shape(BLOCK, D), shape(GRAY, 256)),
+        (shape(BLOCK, D), shape(4, GRAY, 256)),
         [SMEM, VMEM, VMEM, VMEM, VMEM, VMEM, HBM, VMEM, VMEM],
         scratch=[pltpu.VMEM((BLOCK, D), BF), pltpu.VMEM((256, D), BF), pltpu.SemaphoreType.DMA((8,))],
         flops=4 * 128 * 256 * D,
@@ -479,7 +490,7 @@
         mib=16,
         name="norm",
     )(me, hidden, grad_out, gain, total, to_tp(total), in_hbm(out_proj), stats, heads_out)
-    column = jnp.stack([message] + [to_ctx(message, -n, 0) for n in range(1, 4)])
+    column = lax.all_to_all(message, "ctx", split_axis=0, concat_axis=0, tiled=True, axis_index_groups=COLUMNS)
     grad_q = call(
         queries_kernel,
         shape(BLOCK, 256),
@@ -489,7 +500,7 @@
         bytes_accessed=4 * 10**6,
         mib=16,
         name="queries",
-    )(me, queries, gathered, message)
+    )(me, queries, gathered, column)
 
     def keys_part(shifts, columns, sums, first, last):
         return call(
@@ -503,8 +514,8 @@
         name="keys",
         )(me, gathered, *columns, *sums)
 
-    beside = [to_ctx(column, 0, -1), to_ctx(column, 0, 1)]
-    opposite = to_ctx(column, 0, 2)
+    beside = [to_ctx(column, -1), to_ctx(column, 1)]
+    opposite = to_ctx(column, 2)
     sums = keys_part((0,), [column], [], True, False)
     sums = keys_part((1, 3), beside, sums, False, False)
     grad_k, grad_v = keys_part((2,), [opposite], sums, False, True)

time: 189 us -> 184 us (0.974)
  waiting for transfers between devices: 79.1 us -> 57 us
  blocking collectives: 13.7 us -> 29 us
  local copies, waits for them, and re-layouts: 6.49 us -> 4.08 us
    ppermute x6 -> x3, waiting for transfers between devices: 23.8 us -> 8.35 us  [to_ctx(): lax.ppermute(x, 'ctx', [(z * 4 + q, z * 4 + (q + dx) % 4) for z in range(...]
    all_to_all x0 -> x1, blocking collectives: none -> 15.4 us  [body(): lax.all_to_all(message, 'ctx', split_axis=0, concat_axis=0, tiled=True, a...]
    all_to_all x1, starting transfers between devices: 4.14 us -> 9.31 us  [body(): lax.all_to_all(back.reshape(16, 16, CHUNK), 'ctx', split_axis=0, concat_a...]
    ppermute x12, waiting for transfers between devices: 43.8 us -> 39.3 us  [to_ep(): return lax.ppermute(x, 'ep', pairs)]
    ppermute x6 -> x3, starting transfers between devices: 7.63 us -> 4.46 us  [to_ctx(): lax.ppermute(x, 'ctx', [(z * 4 + q, z * 4 + (q + dx) % 4) for z in range(...]
    all_to_all x1, waiting for transfers between devices: 3.38 us -> 0.74 us  [body(): came = lax.all_to_all(send, 'ctx', split_axis=0, concat_axis=0, tiled=True)]
    unnamed x26 -> x18, local copies, waits for them, and re-layouts: 6.4 us -> 3.99 us
    pallas_call x2 -> x3, Pallas kernels: 11.6 us -> 13.2 us  [the longest x1 5.66 us: body(): call(expert_kernel, (shape(160, PIECE),) * 4, [SMEM] + [VMEM] * 11, scrat...]
  transfers between devices with their start and end apart: 26 -> 23, of which waited for: 17 -> 14; matrix products, arithmetic and copies ran while one was open for 0% -> 0% of each run, Pallas kernels for 12% -> 14%
where the time goes in v3:
time: 184 us; the launch traced here: 183 us
  waiting for transfers between devices  57 us (31%)
  starting transfers between devices  43 us (23%)
  Pallas kernels  35.5 us (19%)
  blocking collectives  29 us (16%)
  between operations  14.3 us (8%)
  local copies, waits for them, and re-layouts  4.08 us (2%)
    ppermute x12, waiting for transfers between devices, to_ep(): return lax.ppermute(x, 'ep', pairs)  39.3 us
    ppermute x12, starting transfers between devices, to_ep(): return lax.ppermute(x, 'ep', pairs)  18.2 us
    all_to_all x1, blocking collectives, body(): lax.all_to_all(message, 'ctx', split_axis=0, concat_axis=0, tiled=True, a...  15.4 us
    all_to_all x1, blocking collectives, body(): total = lax.all_to_all(total, 'ep', split_axis=0, concat_axis=0, tiled=True)  13.6 us
    all_to_all x1, starting transfers between devices, body(): came = lax.all_to_all(send, 'ctx', split_axis=0, concat_axis=0, tiled=True)  10.1 us
    all_to_all x1, starting transfers between devices, body(): lax.all_to_all(back.reshape(16, 16, CHUNK), 'ctx', split_axis=0, concat_a...  9.31 us
    ppermute x3, waiting for transfers between devices, to_ctx(): lax.ppermute(x, 'ctx', [(z * 4 + q, z * 4 + (q + dx) % 4) for z in range(...  8.35 us
    pallas_call x1, Pallas kernels, body(): call(expert_kernel, (shape(160, PIECE),) * 4, [SMEM] + [VMEM] * 11, scrat...  5.66 us
  transfers between devices with their start and end apart: 23, of which 14 were waited for; matrix products, arithmetic and copies ran while one was open for 0% of the time, Pallas kernels for 14%

profile of v3, /device:TPU:32, one launch (start us, length us, event | category | flops | bytes accessed | tf_op | source)
XLA Modules:
  0.0 182.9 jit_solution(8282191607819805241)
XLA Ops:
  9.4 4.1 %prepare.1 = (bf16[128,3584]{1,0:T(8,128)(2,1)S(1)}, bf16[16,24,896]{2,1,0:T(8,128)(2,1)}, bf16[256,128]{1,0:T(8,128)(2,1)S(1)}, bf16[128,768]{1,0:T(8,128)(2,1)}) custom-call(s32[3]{0:T(128)S(1)} %pad_add_fusion.me, bf16[128,3584]{1,0:T(8,128)(2,1)} %hidden.3, bf16[128,3584]{1,0:T(8,128)(2,1)} %grad_out.5, f32[3584]{0:T(1024)S(1)} %copy-done.5, ...), custom_call_target="tpu_custom_call" | custom-call | flops 100000000 | bytes 4000000 | tf_op jit(solution)/shard_map/prepare/pallas_call | solution.py:410
  13.5 10.1 %all-to-all-start = ((bf16[16,24,896]{2,1,0:T(8,128)(2,1)}), bf16[16,24,896]{2,1,0:T(8,128)(2,1)S(1)}, u32[]{:S(2)}, u32[]{:S(2)}) async-start(bf16[16,24,896]{2,1,0:T(8,128)(2,1)} %get-tuple-element.52), calls=%async_computation | async-start | bytes 1376256 | tf_op jit(solution)/shard_map/all_to_all | solution.py:421
  24.4 5.1 %dense.1 = (bf16[128,896]{1,0:T(8,128)(2,1)S(1)}, bf16[128,896]{1,0:T(8,128)(2,1)S(1)}, bf16[128,896]{1,0:T(8,128)(2,1)S(1)}, bf16[128,896]{1,0:T(8,128)(2,1)S(1)}) custom-call(s32[3]{0:T(128)S(1)} %pad_add_fusion.me, bf16[128,3584]{1,0:T(8,128)(2,1)S(1)} %get-tuple-element.53.mixed, bf16[128,3584]{1,0:T(8,128)(2,1)} %grad_out.5, bf16[152,3584]{1,0:T(8,128)(2,1)} %gate_in.1, ...), custom_call_target="tpu_custom_call" | custom-call | flops 697303040 | bytes 6000000 | tf_op jit(solution)/shard_map/dense/pallas_call | solution.py:423
  29.5 1.7 collective-permute-start
  31.2 1.7 collective-permute-start.1
  32.8 6.0 %collective-permute-done.second = bf16[128,896]{1,0:T(8,128)(2,1)S(1)} collective-permute-done((bf16[128,896]{1,0:T(8,128)(2,1)S(1)}, bf16[128,896]{1,0:T(8,128)(2,1)S(1)}, u32[]{:S(2)}, u32[]{:S(2)}) %collective-permute-start) | collective-permute-done | bytes 229408 | tf_op jit(solution)/shard_map/ppermute | solution.py:65
  38.8 1.9 %collective-permute-start.2 = (bf16[128,896]{1,0:T(8,128)(2,1)S(1)}, bf16[128,896]{1,0:T(8,128)(2,1)S(1)}, u32[]{:S(2)}, u32[]{:S(2)}) collective-permute-start(bf16[128,896]{1,0:T(8,128)(2,1)S(1)} %get-tuple-element.57), channel_id=1, source_target_pairs={{0,4},{1,5},{2,6},{3,7},{4,0},{5,1},{6,2},{7,3},{8,12},{9,13},{10,... | collective-permute-start | bytes 688136 | tf_op jit(solution)/shard_map/ppermute | solution.py:65
  40.7 6.9 %collective-permute-done.2.fourth = bf16[128,896]{1,0:T(8,128)(2,1)S(1)} collective-permute-done((bf16[128,896]{1,0:T(8,128)(2,1)S(1)}, bf16[128,896]{1,0:T(8,128)(2,1)S(1)}, u32[]{:S(2)}, u32[]{:S(2)}) %collective-permute-start.2) | collective-permute-done | bytes 229408 | tf_op jit(solution)/shard_map/ppermute | solution.py:65
  49.5 1.8 %collective-permute-start.3 = (bf16[320,896]{1,0:T(8,128)(2,1)S(1)}, bf16[320,896]{1,0:T(8,128)(2,1)S(1)}, u32[]{:S(2)}, u32[]{:S(2)}) collective-permute-start(bf16[320,896]{1,0:T(8,128)(2,1)S(1)} %compact.1.own), channel_id=1, source_target_pairs={{0,2},{1,3},{2,4},{3,5},{4,6},{5,7},{6,0},{7,1},{8,10},{9,11},{10,... | collective-permute-start | bytes 1720328 | tf_op jit(solution)/shard_map/ppermute | solution.py:65
  52.9 11.4 %collective-permute-done.3.right = bf16[320,896]{1,0:T(8,128)(2,1)S(1)} collective-permute-done((bf16[320,896]{1,0:T(8,128)(2,1)S(1)}, bf16[320,896]{1,0:T(8,128)(2,1)S(1)}, u32[]{:S(2)}, u32[]{:S(2)}) %collective-permute-start.3) | collective-permute-done | bytes 573472 | tf_op jit(solution)/shard_map/ppermute | solution.py:65
  65.2 2.7 %collective-permute-start.6 = (bf16[160,896]{1,0:T(8,128)(2,1)S(1)}, bf16[160,896]{1,0:T(8,128)(2,1)S(1)}, u32[]{:S(2)}, u32[]{:S(2)}) collective-permute-start(bf16[160,896]{1,0:T(8,128)(2,1)S(1)} %slice.9), channel_id=1, source_target_pairs={{0,6},{1,7},{2,0},{3,1},{4,2},{5,3},{6,4},{7,5},{8,14},{9,15},{10,... | collective-permute-start | bytes 860168 | tf_op jit(solution)/shard_map/ppermute | solution.py:65
  67.9 4.1 %load.1 = (bf16[240,3584]{1,0:T(8,128)(2,1)S(1)}, bf16[240,3584]{1,0:T(8,128)(2,1)S(1)}, bf16[240,3584]{1,0:T(8,128)(2,1)S(1)}, bf16[240,3584]{1,0:T(8,128)(2,1)...) custom-call(bf16[240,3584]{1,0:T(8,128)(2,1)} %bitcast.14, bf16[240,3584]{1,0:T(8,128)(2,1)} %bitcast.16, ...), custom_call_target="tpu_custom_call" | custom-call | bytes 10000000 | tf_op jit(solution)/shard_map/load/pallas_call | solution.py:441
  72.3 5.7 %expert.1 = (bf16[160,896]{1,0:T(8,128)(2,1)S(1)}, bf16[160,896]{1,0:T(8,128)(2,1)S(1)}, bf16[160,896]{1,0:T(8,128)(2,1)S(1)}, bf16[160,896]{1,0:T(8,128)(2,1)S(1)}) custom-call(s32[3]{0:T(128)S(1)} %pad_add_fusion.me, bf16[320,896]{1,0:T(8,128)(2,1)S(1)} %compact.1.own, bf16[320,896]{1,0:T(8,128)(2,1)S(1)} %collective-permute-done.3.right, ...), custom_call_target="tpu_custom_call" | custom-call | flops 2752512000 | bytes 18000000 | tf_op jit(solution)/shard_map/expert/pallas_call | solution.py:449
  79.4 2.2 %collective-permute-start.11 = (bf16[160,896]{1,0:T(8,128)(2,1)S(1)}, bf16[160,896]{1,0:T(8,128)(2,1)S(1)}, u32[]{:S(2)}, u32[]{:S(2)}) collective-permute-start(bf16[160,896]{1,0:T(8,128)(2,1)S(1)} %get-tuple-element.75), channel_id=1, source_target_pairs={{0,6},{1,7},{2,0},{3,1},{4,2},{5,3},{6,4},{7,5},{8,14},{9,15},{10,... | collective-permute-start | bytes 860168 | tf_op jit(solution)/shard_map/ppermute | solution.py:65
  83.0 6.2 %collective-permute-done.10.second = bf16[160,896]{1,0:T(8,128)(2,1)S(1)} collective-permute-done((bf16[160,896]{1,0:T(8,128)(2,1)S(1)}, bf16[160,896]{1,0:T(8,128)(2,1)S(1)}, u32[]{:S(2)}, u32[]{:S(2)}) %collective-permute-start.10) | collective-permute-done | bytes 286752 | tf_op jit(solution)/shard_map/ppermute | solution.py:65
  90.7 1.8 %collective-permute-done.12.fourth = bf16[160,896]{1,0:T(8,128)(2,1)S(1)} collective-permute-done((bf16[160,896]{1,0:T(8,128)(2,1)S(1)}, bf16[160,896]{1,0:T(8,128)(2,1)S(1)}, u32[]{:S(2)}, u32[]{:S(2)}) %collective-permute-start.12) | collective-permute-done | bytes 286752 | tf_op jit(solution)/shard_map/ppermute | solution.py:65
  93.4 5.3 %collective-permute-done.13.came = bf16[160,512]{1,0:T(8,128)(2,1)S(1)} collective-permute-done((bf16[160,512]{1,0:T(8,128)(2,1)S(1)}, bf16[160,512]{1,0:T(8,128)(2,1)S(1)}, u32[]{:S(2)}, u32[]{:S(2)}) %collective-permute-start.13) | collective-permute-done | bytes 163872 | tf_op jit(solution)/shard_map/ppermute | solution.py:65
  99.6 9.3 %all-to-all-start.1 = ((bf16[16,16,512]{2,1,0:T(8,128)(2,1)}), bf16[16,16,512]{2,1,0:T(8,128)(2,1)S(1)}, u32[]{:S(2)}, u32[]{:S(2)}) async-start(bf16[16,16,512]{2,1,0:T(8,128)(2,1)} %bitcast.8), calls=%async_computation.1 | async-start | bytes 524288 | tf_op jit(solution)/shard_map/all_to_all | solution.py:461
  109.9 1.9 %copy-done = bf16[2048,768]{1,0:T(8,128)(2,1)S(1)} copy-done((bf16[2048,768]{1,0:T(8,128)(2,1)S(1)}, bf16[2048,768]{1,0:T(8,128)(2,1)}, u32[]{:S(2)}) %copy-start) | copy-done | bytes 3145752
  111.8 2.7 %stats.1 = (f32[8,128]{1,0:T(8,128)S(1)}, f32[2,128,128]{2,1,0:T(8,128)S(1)}) custom-call(s32[3]{0:T(128)S(1)} %pad_add_fusion.me, bf16[128,256]{1,0:T(8,128)(2,1)S(1)} %copy-done.4, bf16[2048,768]{1,0:T(8,128)(2,1)S(1)} %copy-done), custom_call_target="tpu_custom_call" | custom-call | flops 268435456 | bytes 4000000 | tf_op jit(solution)/shard_map/stats/pallas_call | solution.py:463
  114.5 5.4 %all-to-all-done.1 = bf16[16,16,512]{2,1,0:T(8,128)(2,1)S(1)} async-done(((bf16[16,16,512]{2,1,0:T(8,128)(2,1)}), bf16[16,16,512]{2,1,0:T(8,128)(2,1)S(1)}, u32[]{:S(2)}, u32[]{:S(2)}) %all-to-all-start.1) | async-done | bytes 262176 | tf_op jit(solution)/shard_map/all_to_all | solution.py:461
  122.1 13.6 %all_to_all.20.mine = bf16[8,128,256]{2,1,0:T(8,128)(2,1)S(1)} all-to-all(bf16[8,128,256]{2,1,0:T(8,128)(2,1)S(1)} %broadcast_in_dim.2), channel_id=1, replica_groups=mesh['ctx'=16,'tp'=2,'ep'=8] {'ep'}, dimensions={0} | all-to-all | bytes 1048576 | tf_op jit(solution)/shard_map/all_to_all | solution.py:482
  135.7 1.9 %collective-permute-done.16.other = bf16[8,128,256]{2,1,0:T(8,128)(2,1)S(1)} collective-permute-done((bf16[8,128,256]{2,1,0:T(8,128)(2,1)S(1)}, bf16[8,128,256]{2,1,0:T(8,128)(2,1)S(1)}, u32[]{:S(2)}, u32[]{:S(2)}) %collective-permute-start.16) | collective-permute-done | bytes 524320 | tf_op jit(solution)/shard_map/ppermute | solution.py:60
  137.6 3.4 %norm.1 = (bf16[128,3584]{1,0:T(8,128)(2,1)}, bf16[4,144,256]{2,1,0:T(8,128)(2,1)S(1)}) custom-call(s32[3]{0:T(128)S(1)} %pad_add_fusion.me, bf16[128,3584]{1,0:T(8,128)(2,1)S(1)} %copy-done.3, bf16[128,3584]{1,0:T(8,128)(2,1)S(1)} %copy-done.2, f32[3584]{0:T(1024)S(1)} %copy-done.6, bf16[8,128,256]{2,1,0:T(8,128)(2,1)S(1)} %all_to_all.20.mine, ...), custom_call_target="tpu_custom_call" | custom-call | flops 469762048 | bytes 6000000 | tf_op jit(solution)/shard_map/norm/pallas_call | solution.py:483
  141.1 15.4 %all_to_all.21.grads.refs_0_ = bf16[4,144,256]{2,1,0:T(8,128)(2,1)S(1)} all-to-all(bf16[4,144,256]{2,1,0:T(8,128)(2,1)S(1)} %get-tuple-element.91), channel_id=1, replica_groups={{0,64,128,192},{16,80,144,208},{32,96,160,224},{48,112,176,240},{1,65,1..., dimensions={0} | all-to-all | bytes 589824 | tf_op jit(solution)/shard_map/all_to_all | solution.py:493
  156.5 2.1 %collective-permute-start.18 = (bf16[4,144,256]{2,1,0:T(8,128)(2,1)S(1)}, bf16[4,144,256]{2,1,0:T(8,128)(2,1)S(1)}, u32[]{:S(2)}, u32[]{:S(2)}) collective-permute-start(bf16[4,144,256]{2,1,0:T(8,128)(2,1)S(1)} %all_to_all.21.grads.refs_0_), channel_id=1, source_target_pairs={{0,48},{16,0},{32,16},{48,32},{64,112},{80,64},{96,80},{112,96},{1... | collective-permute-start | bytes 884744 | tf_op jit(solution)/shard_map/ppermute | solution.py:69
  158.6 2.3 %collective-permute-start.17 = (bf16[4,144,256]{2,1,0:T(8,128)(2,1)S(1)}, bf16[4,144,256]{2,1,0:T(8,128)(2,1)S(1)}, u32[]{:S(2)}, u32[]{:S(2)}) collective-permute-start(bf16[4,144,256]{2,1,0:T(8,128)(2,1)S(1)} %all_to_all.21.grads.refs_0_), channel_id=1, source_target_pairs={{0,32},{16,48},{32,0},{48,16},{64,96},{80,112},{96,64},{112,80},{1... | collective-permute-start | bytes 884744 | tf_op jit(solution)/shard_map/ppermute | solution.py:69
  162.2 1.9 %queries.3 = bf16[128,256]{1,0:T(8,128)(2,1)} custom-call(s32[3]{0:T(128)S(1)} %pad_add_fusion.me, bf16[128,256]{1,0:T(8,128)(2,1)S(1)} %copy-done.4, bf16[2048,768]{1,0:T(8,128)(2,1)S(1)} %copy-done.1, bf16[4,144,256]{2,1,0:T(8,128)(2,1)S(1)} %all_to_all.21.grads.refs_0_), custom_call_target="tpu_custom_call" | custom-call | flops 201326592 | bytes 4000000 | tf_op jit(solution)/shard_map/queries/pallas_call | solution.py:494
  164.1 5.0 %collective-permute-done.18.refs_0_ = bf16[4,144,256]{2,1,0:T(8,128)(2,1)S(1)} collective-permute-done((bf16[4,144,256]{2,1,0:T(8,128)(2,1)S(1)}, bf16[4,144,256]{2,1,0:T(8,128)(2,1)S(1)}, u32[]{:S(2)}, u32[]{:S(2)}) %collective-permute-start.18) | collective-permute-done | bytes 294944 | tf_op jit(solution)/shard_map/ppermute | solution.py:69
  169.1 3.4 %collective-permute-done.19.refs_1_ = bf16[4,144,256]{2,1,0:T(8,128)(2,1)S(1)} collective-permute-done((bf16[4,144,256]{2,1,0:T(8,128)(2,1)S(1)}, bf16[4,144,256]{2,1,0:T(8,128)(2,1)S(1)}, u32[]{:S(2)}, u32[]{:S(2)}) %collective-permute-start.19) | collective-permute-done | bytes 294944 | tf_op jit(solution)/shard_map/ppermute | solution.py:69
  172.5 1.7 keys.6
  174.2 1.9 %keys.7 = (bf16[128,256]{1,0:T(8,128)(2,1)}, bf16[128,256]{1,0:T(8,128)(2,1)}) custom-call(s32[3]{0:T(128)S(1)} %pad_add_fusion.me, bf16[2048,768]{1,0:T(8,128)(2,1)S(1)} %copy-done.1, bf16[4,144,256]{2,1,0:T(8,128)(2,1)S(1)} %collective-permute-done.17.refs_0_, f32[128,256]{1,0:T(8,128)S(1)} %get-tuple-element.94.refs_1_, ...), custom_call_target="tpu_custom_call" | custom-call | flops 134217728 | bytes 4000000 | tf_op jit(solution)/shard_map/keys/pallas_call | solution.py:506
  (55 shorter events, 17.8 us)
Async XLA Ops:
  7.2 102.7 %all-gather.2.cloned.1.call-start = ((), (), s32[]{:S(2)}) async-start(), calls=%async_computation.4 | async-start | bytes 3342336 | tf_op jit(solution)/shard_map/all_gather | solution.py:420
  7.3 0.7 copy-start.5
  8.0 0.7 copy-start.7
  8.7 0.7 copy-start.8
  13.5 35.5 %all-to-all-start = ((bf16[16,24,896]{2,1,0:T(8,128)(2,1)}), bf16[16,24,896]{2,1,0:T(8,128)(2,1)S(1)}, u32[]{:S(2)}, u32[]{:S(2)}) async-start(bf16[16,24,896]{2,1,0:T(8,128)(2,1)} %get-tuple-element.52), calls=%async_computation | async-start | bytes 1376256 | tf_op jit(solution)/shard_map/all_to_all | solution.py:421
  23.7 44.2 %collective-permute-start.7 = (bf16[240,3584]{1,0:T(8,128)(2,1)}, bf16[240,3584]{1,0:T(8,128)(2,1)}, u32[]{:S(2)}, u32[]{:S(2)}) collective-permute-start(bf16[240,3584]{1,0:T(8,128)(2,1)} %bitcast.13), channel_id=1, source_target_pairs={{0,8},{8,0},{1,9},{9,1},{2,10},{10,2},{3,11},{11,3},{4,12},{12,4},... | collective-permute-start | bytes 5160968 | tf_op jit(solution)/shard_map/ppermute | solution.py:60
  23.8 44.1 %collective-permute-start.8 = (bf16[240,3584]{1,0:T(8,128)(2,1)}, bf16[240,3584]{1,0:T(8,128)(2,1)}, u32[]{:S(2)}, u32[]{:S(2)}) collective-permute-start(bf16[240,3584]{1,0:T(8,128)(2,1)} %bitcast.15), channel_id=1, source_target_pairs={{0,8},{8,0},{1,9},{9,1},{2,10},{10,2},{3,11},{11,3},{4,12},{12,4},... | collective-permute-start | bytes 5160968 | tf_op jit(solution)/shard_map/ppermute | solution.py:60
  24.3 43.6 %collective-permute-start.9 = (bf16[240,3584]{1,0:T(8,128)(2,1)}, bf16[240,3584]{1,0:T(8,128)(2,1)}, u32[]{:S(2)}, u32[]{:S(2)}) collective-permute-start(bf16[240,3584]{1,0:T(8,128)(2,1)} %bitcast.17), channel_id=1, source_target_pairs={{0,8},{8,0},{1,9},{9,1},{2,10},{10,2},{3,11},{11,3},{4,12},{12,4},... | collective-permute-start | bytes 5160968 | tf_op jit(solution)/shard_map/ppermute | solution.py:60
  29.5 9.3 %collective-permute-start = (bf16[128,896]{1,0:T(8,128)(2,1)S(1)}, bf16[128,896]{1,0:T(8,128)(2,1)S(1)}, u32[]{:S(2)}, u32[]{:S(2)}) collective-permute-start(bf16[128,896]{1,0:T(8,128)(2,1)S(1)} %get-tuple-element.55), channel_id=1, source_target_pairs={{0,2},{1,3},{2,4},{3,5},{4,6},{5,7},{6,0},{7,1},{8,10},{9,11},{10,... | collective-permute-start | bytes 688136 | tf_op jit(solution)/shard_map/ppermute | solution.py:65
  31.2 9.6 %collective-permute-start.1 = (bf16[128,896]{1,0:T(8,128)(2,1)S(1)}, bf16[128,896]{1,0:T(8,128)(2,1)S(1)}, u32[]{:S(2)}, u32[]{:S(2)}) collective-permute-start(bf16[128,896]{1,0:T(8,128)(2,1)S(1)} %get-tuple-element.56), channel_id=1, source_target_pairs={{0,6},{1,7},{2,0},{3,1},{4,2},{5,3},{6,4},{7,5},{8,14},{9,15},{10,... | collective-permute-start | bytes 688136 | tf_op jit(solution)/shard_map/ppermute | solution.py:65
  38.8 8.8 %collective-permute-start.2 = (bf16[128,896]{1,0:T(8,128)(2,1)S(1)}, bf16[128,896]{1,0:T(8,128)(2,1)S(1)}, u32[]{:S(2)}, u32[]{:S(2)}) collective-permute-start(bf16[128,896]{1,0:T(8,128)(2,1)S(1)} %get-tuple-element.57), channel_id=1, source_target_pairs={{0,4},{1,5},{2,6},{3,7},{4,0},{5,1},{6,2},{7,3},{8,12},{9,13},{10,... | collective-permute-start | bytes 688136 | tf_op jit(solution)/shard_map/ppermute | solution.py:65
  49.5 14.8 %collective-permute-start.3 = (bf16[320,896]{1,0:T(8,128)(2,1)S(1)}, bf16[320,896]{1,0:T(8,128)(2,1)S(1)}, u32[]{:S(2)}, u32[]{:S(2)}) collective-permute-start(bf16[320,896]{1,0:T(8,128)(2,1)S(1)} %compact.1.own), channel_id=1, source_target_pairs={{0,2},{1,3},{2,4},{3,5},{4,6},{5,7},{6,0},{7,1},{8,10},{9,11},{10,... | collective-permute-start | bytes 1720328 | tf_op jit(solution)/shard_map/ppermute | solution.py:65
  51.4 13.8 %collective-permute-start.4 = (bf16[320,896]{1,0:T(8,128)(2,1)S(1)}, bf16[320,896]{1,0:T(8,128)(2,1)S(1)}, u32[]{:S(2)}, u32[]{:S(2)}) collective-permute-start(bf16[320,896]{1,0:T(8,128)(2,1)S(1)} %compact.1.own), channel_id=1, source_target_pairs={{0,6},{1,7},{2,0},{3,1},{4,2},{5,3},{6,4},{7,5},{8,14},{9,15},{10,... | collective-permute-start | bytes 1720328 | tf_op jit(solution)/shard_map/ppermute | solution.py:65
  64.3 7.9 %collective-permute-start.5 = (bf16[160,896]{1,0:T(8,128)(2,1)S(1)}, bf16[160,896]{1,0:T(8,128)(2,1)S(1)}, u32[]{:S(2)}, u32[]{:S(2)}) collective-permute-start(bf16[160,896]{1,0:T(8,128)(2,1)S(1)} %slice.8), channel_id=1, source_target_pairs={{0,2},{1,3},{2,4},{3,5},{4,6},{5,7},{6,0},{7,1},{8,10},{9,11},{10,... | collective-permute-start | bytes 860168 | tf_op jit(solution)/shard_map/ppermute | solution.py:65
  65.2 7.0 %collective-permute-start.6 = (bf16[160,896]{1,0:T(8,128)(2,1)S(1)}, bf16[160,896]{1,0:T(8,128)(2,1)S(1)}, u32[]{:S(2)}, u32[]{:S(2)}) collective-permute-start(bf16[160,896]{1,0:T(8,128)(2,1)S(1)} %slice.9), channel_id=1, source_target_pairs={{0,6},{1,7},{2,0},{3,1},{4,2},{5,3},{6,4},{7,5},{8,14},{9,15},{10,... | collective-permute-start | bytes 860168 | tf_op jit(solution)/shard_map/ppermute | solution.py:65
  77.9 32.0 %copy-start.4 = (bf16[128,256]{1,0:T(8,128)(2,1)S(1)}, bf16[128,256]{1,0:T(8,128)(2,1)}, u32[]{:S(2)}) copy-start(bf16[128,256]{1,0:T(8,128)(2,1)} %own_q.1) | copy-start | bytes 196612
  77.9 11.3 %collective-permute-start.10 = (bf16[160,896]{1,0:T(8,128)(2,1)S(1)}, bf16[160,896]{1,0:T(8,128)(2,1)S(1)}, u32[]{:S(2)}, u32[]{:S(2)}) collective-permute-start(bf16[160,896]{1,0:T(8,128)(2,1)S(1)} %get-tuple-element.74), channel_id=1, source_target_pairs={{0,2},{1,3},{2,4},{3,5},{4,6},{5,7},{6,0},{7,1},{8,10},{9,11},{10,... | collective-permute-start | bytes 860168 | tf_op jit(solution)/shard_map/ppermute | solution.py:65
  79.4 11.3 %collective-permute-start.11 = (bf16[160,896]{1,0:T(8,128)(2,1)S(1)}, bf16[160,896]{1,0:T(8,128)(2,1)S(1)}, u32[]{:S(2)}, u32[]{:S(2)}) collective-permute-start(bf16[160,896]{1,0:T(8,128)(2,1)S(1)} %get-tuple-element.75), channel_id=1, source_target_pairs={{0,6},{1,7},{2,0},{3,1},{4,2},{5,3},{6,4},{7,5},{8,14},{9,15},{10,... | collective-permute-start | bytes 860168 | tf_op jit(solution)/shard_map/ppermute | solution.py:65
  81.6 10.9 %collective-permute-start.12 = (bf16[160,896]{1,0:T(8,128)(2,1)S(1)}, bf16[160,896]{1,0:T(8,128)(2,1)S(1)}, u32[]{:S(2)}, u32[]{:S(2)}) collective-permute-start(bf16[160,896]{1,0:T(8,128)(2,1)S(1)} %get-tuple-element.76), channel_id=1, source_target_pairs={{0,4},{1,5},{2,6},{3,7},{4,0},{5,1},{6,2},{7,3},{8,12},{9,13},{10,... | collective-permute-start | bytes 860168 | tf_op jit(solution)/shard_map/ppermute | solution.py:65
  93.3 5.4 %collective-permute-start.13 = (bf16[160,512]{1,0:T(8,128)(2,1)S(1)}, bf16[160,512]{1,0:T(8,128)(2,1)S(1)}, u32[]{:S(2)}, u32[]{:S(2)}) collective-permute-start(bf16[160,512]{1,0:T(8,128)(2,1)S(1)} %get-tuple-element.78), channel_id=1, source_target_pairs={{0,1},{1,0},{2,3},{3,2},{4,5},{5,4},{6,7},{7,6},{8,9},{9,8},{10,11... | collective-permute-start | bytes 491528 | tf_op jit(solution)/shard_map/ppermute | solution.py:65
  99.6 20.3 %all-to-all-start.1 = ((bf16[16,16,512]{2,1,0:T(8,128)(2,1)}), bf16[16,16,512]{2,1,0:T(8,128)(2,1)S(1)}, u32[]{:S(2)}, u32[]{:S(2)}) async-start(bf16[16,16,512]{2,1,0:T(8,128)(2,1)} %bitcast.8), calls=%async_computation.1 | async-start | bytes 524288 | tf_op jit(solution)/shard_map/all_to_all | solution.py:461
  108.9 5.6 %collective-permute-start.14 = (bf16[128,512]{1,0:T(8,128)(2,1)S(1)}, bf16[128,512]{1,0:T(8,128)(2,1)S(1)}, u32[]{:S(2)}, u32[]{:S(2)}) collective-permute-start(bf16[128,512]{1,0:T(8,128)(2,1)S(1)} %get-tuple-element.82), channel_id=1, source_target_pairs={{0,1},{1,0},{2,3},{3,2},{4,5},{5,4},{6,7},{7,6},{8,9},{9,8},{10,11... | collective-permute-start | bytes 393224 | tf_op jit(solution)/shard_map/ppermute | solution.py:65
  109.9 1.9 %copy-start = (bf16[2048,768]{1,0:T(8,128)(2,1)S(1)}, bf16[2048,768]{1,0:T(8,128)(2,1)}, u32[]{:S(2)}) copy-start(bf16[2048,768]{1,0:T(8,128)(2,1)} %all-gather.2.cloned.1.call-done.gathered) | copy-start | bytes 9437188
  114.5 23.1 %copy-start.2 = (bf16[128,3584]{1,0:T(8,128)(2,1)S(1)}, bf16[128,3584]{1,0:T(8,128)(2,1)}, u32[]{:S(2)}) copy-start(bf16[128,3584]{1,0:T(8,128)(2,1)} %grad_out.5) | copy-start | bytes 2752516
  114.5 23.1 %copy-start.3 = (bf16[128,3584]{1,0:T(8,128)(2,1)S(1)}, bf16[128,3584]{1,0:T(8,128)(2,1)}, u32[]{:S(2)}) copy-start(bf16[128,3584]{1,0:T(8,128)(2,1)} %hidden.3) | copy-start | bytes 2752516
  114.5 23.1 %copy-start.6 = (f32[3584]{0:T(1024)S(1)}, f32[3584]{0:T(1024)}, u32[]{:S(2)}) copy-start(f32[3584]{0:T(1024)} %gain.3) | copy-start | bytes 43012
  120.7 1.3 collective-permute-start.15
  135.7 25.2 %copy-start.1 = (bf16[2048,768]{1,0:T(8,128)(2,1)S(1)}, bf16[2048,768]{1,0:T(8,128)(2,1)}, u32[]{:S(2)}) copy-start(bf16[2048,768]{1,0:T(8,128)(2,1)} %all-gather.2.cloned.1.call-done.gathered) | copy-start | bytes 9437188
  135.7 1.9 %collective-permute-start.16 = (bf16[8,128,256]{2,1,0:T(8,128)(2,1)S(1)}, bf16[8,128,256]{2,1,0:T(8,128)(2,1)S(1)}, u32[]{:S(2)}, u32[]{:S(2)}) collective-permute-start(bf16[8,128,256]{2,1,0:T(8,128)(2,1)S(1)} %all_to_all.20.mine), channel_id=1, source_target_pairs={{0,8},{8,0},{1,9},{9,1},{2,10},{10,2},{3,11},{11,3},{4,12},{12,4},... | collective-permute-start | bytes 1572872 | tf_op jit(solution)/shard_map/ppermute | solution.py:60
  156.5 12.6 %collective-permute-start.18 = (bf16[4,144,256]{2,1,0:T(8,128)(2,1)S(1)}, bf16[4,144,256]{2,1,0:T(8,128)(2,1)S(1)}, u32[]{:S(2)}, u32[]{:S(2)}) collective-permute-start(bf16[4,144,256]{2,1,0:T(8,128)(2,1)S(1)} %all_to_all.21.grads.refs_0_), channel_id=1, source_target_pairs={{0,48},{16,0},{32,16},{48,32},{64,112},{80,64},{96,80},{112,96},{1... | collective-permute-start | bytes 884744 | tf_op jit(solution)/shard_map/ppermute | solution.py:69
  158.6 13.8 %collective-permute-start.19 = (bf16[4,144,256]{2,1,0:T(8,128)(2,1)S(1)}, bf16[4,144,256]{2,1,0:T(8,128)(2,1)S(1)}, u32[]{:S(2)}, u32[]{:S(2)}) collective-permute-start(bf16[4,144,256]{2,1,0:T(8,128)(2,1)S(1)} %all_to_all.21.grads.refs_0_), channel_id=1, source_target_pairs={{0,16},{16,32},{32,48},{48,0},{64,80},{80,96},{96,112},{112,64},{1... | collective-permute-start | bytes 884744 | tf_op jit(solution)/shard_map/ppermute | solution.py:69
  158.6 15.6 %collective-permute-start.17 = (bf16[4,144,256]{2,1,0:T(8,128)(2,1)S(1)}, bf16[4,144,256]{2,1,0:T(8,128)(2,1)S(1)}, u32[]{:S(2)}, u32[]{:S(2)}) collective-permute-start(bf16[4,144,256]{2,1,0:T(8,128)(2,1)S(1)} %all_to_all.21.grads.refs_0_), channel_id=1, source_target_pairs={{0,32},{16,48},{32,0},{48,16},{64,96},{80,112},{96,64},{112,80},{1... | collective-permute-start | bytes 884744 | tf_op jit(solution)/shard_map/ppermute | solution.py:69
Sparse Core Ops, SparseCore 0:
  13.7 74.6 all-gather.1

commit v4 on v3

--- a/solution.py
+++ b/solution.py
@@ -514,11 +514,11 @@
         name="keys",
         )(me, gathered, *columns, *sums)
 
+    opposite = to_ctx(column, 2)
     beside = [to_ctx(column, -1), to_ctx(column, 1)]
-    opposite = to_ctx(column, 2)
     sums = keys_part((0,), [column], [], True, False)
-    sums = keys_part((1, 3), beside, sums, False, False)
-    grad_k, grad_v = keys_part((2,), [opposite], sums, False, True)
+    sums = keys_part((2,), [opposite], sums, False, False)
+    grad_k, grad_v = keys_part((1, 3), beside, sums, False, True)
     return grad_hidden, grad_q, grad_k, grad_v
 
 

time: 184 us -> 181 us (0.984)
  waiting for transfers between devices: 57 us -> 54.2 us
    ppermute x3, waiting for transfers between devices: 8.35 us -> 5.54 us  [to_ctx(): lax.ppermute(x, 'ctx', [(z * 4 + q, z * 4 + (q + dx) % 4) for z in range(...]
  transfers between devices with their start and end apart: 23 -> 23, of which waited for: 14 -> 15; matrix products, arithmetic and copies ran while one was open for 0% -> 0% of each run, Pallas kernels for 14% -> 14%
where the time goes in v4:
time: 181 us; the launch traced here: 180 us
  waiting for transfers between devices  54.2 us (30%)
  starting transfers between devices  43 us (24%)
  Pallas kernels  35.5 us (20%)
  blocking collectives  29 us (16%)
  between operations  14.2 us (8%)
  local copies, waits for them, and re-layouts  4.08 us (2%)
    ppermute x12, waiting for transfers between devices, to_ep(): return lax.ppermute(x, 'ep', pairs)  39.3 us
    ppermute x12, starting transfers between devices, to_ep(): return lax.ppermute(x, 'ep', pairs)  18.2 us
    all_to_all x1, blocking collectives, body(): lax.all_to_all(message, 'ctx', split_axis=0, concat_axis=0, tiled=True, a...  15.4 us
    all_to_all x1, blocking collectives, body(): total = lax.all_to_all(total, 'ep', split_axis=0, concat_axis=0, tiled=True)  13.6 us
    all_to_all x1, starting transfers between devices, body(): came = lax.all_to_all(send, 'ctx', split_axis=0, concat_axis=0, tiled=True)  10.1 us
    all_to_all x1, starting transfers between devices, body(): lax.all_to_all(back.reshape(16, 16, CHUNK), 'ctx', split_axis=0, concat_a...  9.31 us
    pallas_call x1, Pallas kernels, body(): call(expert_kernel, (shape(160, PIECE),) * 4, [SMEM] + [VMEM] * 11, scrat...  5.66 us
    ppermute x3, waiting for transfers between devices, to_ctx(): lax.ppermute(x, 'ctx', [(z * 4 + q, z * 4 + (q + dx) % 4) for z in range(...  5.54 us
  transfers between devices with their start and end apart: 23, of which 15 were waited for; matrix products, arithmetic and copies ran while one was open for 0% of the time, Pallas kernels for 14%

profile of v4, /device:TPU:32, one launch (start us, length us, event | category | flops | bytes accessed | tf_op | source)
XLA Modules:
  0.0 180.1 jit_solution(739505212092966980)
XLA Ops:
  9.4 4.1 %prepare.1 = (bf16[128,3584]{1,0:T(8,128)(2,1)S(1)}, bf16[16,24,896]{2,1,0:T(8,128)(2,1)}, bf16[256,128]{1,0:T(8,128)(2,1)S(1)}, bf16[128,768]{1,0:T(8,128)(2,1)}) custom-call(s32[3]{0:T(128)S(1)} %pad_add_fusion.me, bf16[128,3584]{1,0:T(8,128)(2,1)} %hidden.3, bf16[128,3584]{1,0:T(8,128)(2,1)} %grad_out.5, f32[3584]{0:T(1024)S(1)} %copy-done.5, ...), custom_call_target="tpu_custom_call" | custom-call | flops 100000000 | bytes 4000000 | tf_op jit(solution)/shard_map/prepare/pallas_call | solution.py:410
  13.5 10.1 %all-to-all-start = ((bf16[16,24,896]{2,1,0:T(8,128)(2,1)}), bf16[16,24,896]{2,1,0:T(8,128)(2,1)S(1)}, u32[]{:S(2)}, u32[]{:S(2)}) async-start(bf16[16,24,896]{2,1,0:T(8,128)(2,1)} %get-tuple-element.52), calls=%async_computation | async-start | bytes 1376256 | tf_op jit(solution)/shard_map/all_to_all | solution.py:421
  24.4 5.1 %dense.1 = (bf16[128,896]{1,0:T(8,128)(2,1)S(1)}, bf16[128,896]{1,0:T(8,128)(2,1)S(1)}, bf16[128,896]{1,0:T(8,128)(2,1)S(1)}, bf16[128,896]{1,0:T(8,128)(2,1)S(1)}) custom-call(s32[3]{0:T(128)S(1)} %pad_add_fusion.me, bf16[128,3584]{1,0:T(8,128)(2,1)S(1)} %get-tuple-element.53.mixed, bf16[128,3584]{1,0:T(8,128)(2,1)} %grad_out.5, bf16[152,3584]{1,0:T(8,128)(2,1)} %gate_in.1, ...), custom_call_target="tpu_custom_call" | custom-call | flops 697303040 | bytes 6000000 | tf_op jit(solution)/shard_map/dense/pallas_call | solution.py:423
  29.5 1.7 collective-permute-start
  31.2 1.7 collective-permute-start.1
  32.8 6.0 %collective-permute-done.second = bf16[128,896]{1,0:T(8,128)(2,1)S(1)} collective-permute-done((bf16[128,896]{1,0:T(8,128)(2,1)S(1)}, bf16[128,896]{1,0:T(8,128)(2,1)S(1)}, u32[]{:S(2)}, u32[]{:S(2)}) %collective-permute-start) | collective-permute-done | bytes 229408 | tf_op jit(solution)/shard_map/ppermute | solution.py:65
  38.8 1.9 %collective-permute-start.2 = (bf16[128,896]{1,0:T(8,128)(2,1)S(1)}, bf16[128,896]{1,0:T(8,128)(2,1)S(1)}, u32[]{:S(2)}, u32[]{:S(2)}) collective-permute-start(bf16[128,896]{1,0:T(8,128)(2,1)S(1)} %get-tuple-element.57), channel_id=1, source_target_pairs={{0,4},{1,5},{2,6},{3,7},{4,0},{5,1},{6,2},{7,3},{8,12},{9,13},{10,... | collective-permute-start | bytes 688136 | tf_op jit(solution)/shard_map/ppermute | solution.py:65
  40.7 6.9 %collective-permute-done.2.fourth = bf16[128,896]{1,0:T(8,128)(2,1)S(1)} collective-permute-done((bf16[128,896]{1,0:T(8,128)(2,1)S(1)}, bf16[128,896]{1,0:T(8,128)(2,1)S(1)}, u32[]{:S(2)}, u32[]{:S(2)}) %collective-permute-start.2) | collective-permute-done | bytes 229408 | tf_op jit(solution)/shard_map/ppermute | solution.py:65
  49.5 1.8 %collective-permute-start.3 = (bf16[320,896]{1,0:T(8,128)(2,1)S(1)}, bf16[320,896]{1,0:T(8,128)(2,1)S(1)}, u32[]{:S(2)}, u32[]{:S(2)}) collective-permute-start(bf16[320,896]{1,0:T(8,128)(2,1)S(1)} %compact.1.own), channel_id=1, source_target_pairs={{0,2},{1,3},{2,4},{3,5},{4,6},{5,7},{6,0},{7,1},{8,10},{9,11},{10,... | collective-permute-start | bytes 1720328 | tf_op jit(solution)/shard_map/ppermute | solution.py:65
  51.4 1.5 collective-permute-start.4
  52.9 11.4 %collective-permute-done.3.right = bf16[320,896]{1,0:T(8,128)(2,1)S(1)} collective-permute-done((bf16[320,896]{1,0:T(8,128)(2,1)S(1)}, bf16[320,896]{1,0:T(8,128)(2,1)S(1)}, u32[]{:S(2)}, u32[]{:S(2)}) %collective-permute-start.3) | collective-permute-done | bytes 573472 | tf_op jit(solution)/shard_map/ppermute | solution.py:65
  65.2 2.7 %collective-permute-start.6 = (bf16[160,896]{1,0:T(8,128)(2,1)S(1)}, bf16[160,896]{1,0:T(8,128)(2,1)S(1)}, u32[]{:S(2)}, u32[]{:S(2)}) collective-permute-start(bf16[160,896]{1,0:T(8,128)(2,1)S(1)} %slice.9), channel_id=1, source_target_pairs={{0,6},{1,7},{2,0},{3,1},{4,2},{5,3},{6,4},{7,5},{8,14},{9,15},{10,... | collective-permute-start | bytes 860168 | tf_op jit(solution)/shard_map/ppermute | solution.py:65
  67.9 4.1 %load.1 = (bf16[240,3584]{1,0:T(8,128)(2,1)S(1)}, bf16[240,3584]{1,0:T(8,128)(2,1)S(1)}, bf16[240,3584]{1,0:T(8,128)(2,1)S(1)}, bf16[240,3584]{1,0:T(8,128)(2,1)...) custom-call(bf16[240,3584]{1,0:T(8,128)(2,1)} %bitcast.14, bf16[240,3584]{1,0:T(8,128)(2,1)} %bitcast.16, ...), custom_call_target="tpu_custom_call" | custom-call | bytes 10000000 | tf_op jit(solution)/shard_map/load/pallas_call | solution.py:441
  72.3 5.7 %expert.1 = (bf16[160,896]{1,0:T(8,128)(2,1)S(1)}, bf16[160,896]{1,0:T(8,128)(2,1)S(1)}, bf16[160,896]{1,0:T(8,128)(2,1)S(1)}, bf16[160,896]{1,0:T(8,128)(2,1)S(1)}) custom-call(s32[3]{0:T(128)S(1)} %pad_add_fusion.me, bf16[320,896]{1,0:T(8,128)(2,1)S(1)} %compact.1.own, bf16[320,896]{1,0:T(8,128)(2,1)S(1)} %collective-permute-done.3.right, ...), custom_call_target="tpu_custom_call" | custom-call | flops 2752512000 | bytes 18000000 | tf_op jit(solution)/shard_map/expert/pallas_call | solution.py:449
  77.9 1.4 collective-permute-start.10
  79.4 2.2 %collective-permute-start.11 = (bf16[160,896]{1,0:T(8,128)(2,1)S(1)}, bf16[160,896]{1,0:T(8,128)(2,1)S(1)}, u32[]{:S(2)}, u32[]{:S(2)}) collective-permute-start(bf16[160,896]{1,0:T(8,128)(2,1)S(1)} %get-tuple-element.75), channel_id=1, source_target_pairs={{0,6},{1,7},{2,0},{3,1},{4,2},{5,3},{6,4},{7,5},{8,14},{9,15},{10,... | collective-permute-start | bytes 860168 | tf_op jit(solution)/shard_map/ppermute | solution.py:65
  83.0 6.2 %collective-permute-done.10.second = bf16[160,896]{1,0:T(8,128)(2,1)S(1)} collective-permute-done((bf16[160,896]{1,0:T(8,128)(2,1)S(1)}, bf16[160,896]{1,0:T(8,128)(2,1)S(1)}, u32[]{:S(2)}, u32[]{:S(2)}) %collective-permute-start.10) | collective-permute-done | bytes 286752 | tf_op jit(solution)/shard_map/ppermute | solution.py:65
  89.2 1.5 collective-permute-done.11.third
  90.7 1.8 %collective-permute-done.12.fourth = bf16[160,896]{1,0:T(8,128)(2,1)S(1)} collective-permute-done((bf16[160,896]{1,0:T(8,128)(2,1)S(1)}, bf16[160,896]{1,0:T(8,128)(2,1)S(1)}, u32[]{:S(2)}, u32[]{:S(2)}) %collective-permute-start.12) | collective-permute-done | bytes 286752 | tf_op jit(solution)/shard_map/ppermute | solution.py:65
  93.4 5.3 %collective-permute-done.13.came = bf16[160,512]{1,0:T(8,128)(2,1)S(1)} collective-permute-done((bf16[160,512]{1,0:T(8,128)(2,1)S(1)}, bf16[160,512]{1,0:T(8,128)(2,1)S(1)}, u32[]{:S(2)}, u32[]{:S(2)}) %collective-permute-start.13) | collective-permute-done | bytes 163872 | tf_op jit(solution)/shard_map/ppermute | solution.py:65
  99.6 9.3 %all-to-all-start.1 = ((bf16[16,16,512]{2,1,0:T(8,128)(2,1)}), bf16[16,16,512]{2,1,0:T(8,128)(2,1)S(1)}, u32[]{:S(2)}, u32[]{:S(2)}) async-start(bf16[16,16,512]{2,1,0:T(8,128)(2,1)} %bitcast.8), calls=%async_computation.1 | async-start | bytes 524288 | tf_op jit(solution)/shard_map/all_to_all | solution.py:461
  109.9 1.9 %copy-done = bf16[2048,768]{1,0:T(8,128)(2,1)S(1)} copy-done((bf16[2048,768]{1,0:T(8,128)(2,1)S(1)}, bf16[2048,768]{1,0:T(8,128)(2,1)}, u32[]{:S(2)}) %copy-start) | copy-done | bytes 3145752
  111.8 2.7 %stats.1 = (f32[8,128]{1,0:T(8,128)S(1)}, f32[2,128,128]{2,1,0:T(8,128)S(1)}) custom-call(s32[3]{0:T(128)S(1)} %pad_add_fusion.me, bf16[128,256]{1,0:T(8,128)(2,1)S(1)} %copy-done.4, bf16[2048,768]{1,0:T(8,128)(2,1)S(1)} %copy-done), custom_call_target="tpu_custom_call" | custom-call | flops 268435456 | bytes 4000000 | tf_op jit(solution)/shard_map/stats/pallas_call | solution.py:463
  114.5 5.4 %all-to-all-done.1 = bf16[16,16,512]{2,1,0:T(8,128)(2,1)S(1)} async-done(((bf16[16,16,512]{2,1,0:T(8,128)(2,1)}), bf16[16,16,512]{2,1,0:T(8,128)(2,1)S(1)}, u32[]{:S(2)}, u32[]{:S(2)}) %all-to-all-start.1) | async-done | bytes 262176 | tf_op jit(solution)/shard_map/all_to_all | solution.py:461
  122.1 13.6 %all_to_all.20.mine = bf16[8,128,256]{2,1,0:T(8,128)(2,1)S(1)} all-to-all(bf16[8,128,256]{2,1,0:T(8,128)(2,1)S(1)} %broadcast_in_dim.2), channel_id=1, replica_groups=mesh['ctx'=16,'tp'=2,'ep'=8] {'ep'}, dimensions={0} | all-to-all | bytes 1048576 | tf_op jit(solution)/shard_map/all_to_all | solution.py:482
  135.7 1.9 %collective-permute-done.16.other = bf16[8,128,256]{2,1,0:T(8,128)(2,1)S(1)} collective-permute-done((bf16[8,128,256]{2,1,0:T(8,128)(2,1)S(1)}, bf16[8,128,256]{2,1,0:T(8,128)(2,1)S(1)}, u32[]{:S(2)}, u32[]{:S(2)}) %collective-permute-start.16) | collective-permute-done | bytes 524320 | tf_op jit(solution)/shard_map/ppermute | solution.py:60
  137.6 3.4 %norm.1 = (bf16[128,3584]{1,0:T(8,128)(2,1)}, bf16[4,144,256]{2,1,0:T(8,128)(2,1)S(1)}) custom-call(s32[3]{0:T(128)S(1)} %pad_add_fusion.me, bf16[128,3584]{1,0:T(8,128)(2,1)S(1)} %copy-done.3, bf16[128,3584]{1,0:T(8,128)(2,1)S(1)} %copy-done.2, f32[3584]{0:T(1024)S(1)} %copy-done.6, bf16[8,128,256]{2,1,0:T(8,128)(2,1)S(1)} %all_to_all.20.mine, ...), custom_call_target="tpu_custom_call" | custom-call | flops 469762048 | bytes 6000000 | tf_op jit(solution)/shard_map/norm/pallas_call | solution.py:483
  141.1 15.4 %all_to_all.21.grads.refs_0_ = bf16[4,144,256]{2,1,0:T(8,128)(2,1)S(1)} all-to-all(bf16[4,144,256]{2,1,0:T(8,128)(2,1)S(1)} %get-tuple-element.91), channel_id=1, replica_groups={{0,64,128,192},{16,80,144,208},{32,96,160,224},{48,112,176,240},{1,65,1..., dimensions={0} | all-to-all | bytes 589824 | tf_op jit(solution)/shard_map/all_to_all | solution.py:493
  156.5 2.4 %collective-permute-start.19 = (bf16[4,144,256]{2,1,0:T(8,128)(2,1)S(1)}, bf16[4,144,256]{2,1,0:T(8,128)(2,1)S(1)}, u32[]{:S(2)}, u32[]{:S(2)}) collective-permute-start(bf16[4,144,256]{2,1,0:T(8,128)(2,1)S(1)} %all_to_all.21.grads.refs_0_), channel_id=1, source_target_pairs={{0,32},{16,48},{32,0},{48,16},{64,96},{80,112},{96,64},{112,80},{1... | collective-permute-start | bytes 884744 | tf_op jit(solution)/shard_map/ppermute | solution.py:69
  162.2 1.9 %queries.3 = bf16[128,256]{1,0:T(8,128)(2,1)} custom-call(s32[3]{0:T(128)S(1)} %pad_add_fusion.me, bf16[128,256]{1,0:T(8,128)(2,1)S(1)} %copy-done.4, bf16[2048,768]{1,0:T(8,128)(2,1)S(1)} %copy-done.1, bf16[4,144,256]{2,1,0:T(8,128)(2,1)S(1)} %all_to_all.21.grads.refs_0_), custom_call_target="tpu_custom_call" | custom-call | flops 201326592 | bytes 4000000 | tf_op jit(solution)/shard_map/queries/pallas_call | solution.py:494
  164.1 3.6 %collective-permute-done.19.refs_0_ = bf16[4,144,256]{2,1,0:T(8,128)(2,1)S(1)} collective-permute-done((bf16[4,144,256]{2,1,0:T(8,128)(2,1)S(1)}, bf16[4,144,256]{2,1,0:T(8,128)(2,1)S(1)}, u32[]{:S(2)}, u32[]{:S(2)}) %collective-permute-start.19) | collective-permute-done | bytes 294944 | tf_op jit(solution)/shard_map/ppermute | solution.py:69
  170.9 2.4 %keys.7 = (bf16[128,256]{1,0:T(8,128)(2,1)}, bf16[128,256]{1,0:T(8,128)(2,1)}) custom-call(s32[3]{0:T(128)S(1)} %pad_add_fusion.me, bf16[2048,768]{1,0:T(8,128)(2,1)S(1)} %copy-done.1, bf16[4,144,256]{2,1,0:T(8,128)(2,1)S(1)} %collective-permute-done.17.refs_0_, bf16[4,144,256]{2,1,0:T(8,128)(2,1)S(1)} %collective-permute-done.18.refs_1_, ...), custom_call_target="tpu_custom_call" | custom-call | flops 268435456 | bytes 4000000 | tf_op jit(solution)/shard_map/keys/pallas_call | solution.py:506
  (55 shorter events, 18.6 us)
Async XLA Ops:
  7.2 102.7 %all-gather.2.cloned.1.call-start = ((), (), s32[]{:S(2)}) async-start(), calls=%async_computation.4 | async-start | bytes 3342336 | tf_op jit(solution)/shard_map/all_gather | solution.py:420
  7.3 0.7 copy-start.5
  8.0 0.7 copy-start.7
  8.7 0.7 copy-start.8
  13.5 35.5 %all-to-all-start = ((bf16[16,24,896]{2,1,0:T(8,128)(2,1)}), bf16[16,24,896]{2,1,0:T(8,128)(2,1)S(1)}, u32[]{:S(2)}, u32[]{:S(2)}) async-start(bf16[16,24,896]{2,1,0:T(8,128)(2,1)} %get-tuple-element.52), calls=%async_computation | async-start | bytes 1376256 | tf_op jit(solution)/shard_map/all_to_all | solution.py:421
  23.7 44.2 %collective-permute-start.7 = (bf16[240,3584]{1,0:T(8,128)(2,1)}, bf16[240,3584]{1,0:T(8,128)(2,1)}, u32[]{:S(2)}, u32[]{:S(2)}) collective-permute-start(bf16[240,3584]{1,0:T(8,128)(2,1)} %bitcast.13), channel_id=1, source_target_pairs={{0,8},{8,0},{1,9},{9,1},{2,10},{10,2},{3,11},{11,3},{4,12},{12,4},... | collective-permute-start | bytes 5160968 | tf_op jit(solution)/shard_map/ppermute | solution.py:60
  23.8 44.1 %collective-permute-start.8 = (bf16[240,3584]{1,0:T(8,128)(2,1)}, bf16[240,3584]{1,0:T(8,128)(2,1)}, u32[]{:S(2)}, u32[]{:S(2)}) collective-permute-start(bf16[240,3584]{1,0:T(8,128)(2,1)} %bitcast.15), channel_id=1, source_target_pairs={{0,8},{8,0},{1,9},{9,1},{2,10},{10,2},{3,11},{11,3},{4,12},{12,4},... | collective-permute-start | bytes 5160968 | tf_op jit(solution)/shard_map/ppermute | solution.py:60
  24.3 43.6 %collective-permute-start.9 = (bf16[240,3584]{1,0:T(8,128)(2,1)}, bf16[240,3584]{1,0:T(8,128)(2,1)}, u32[]{:S(2)}, u32[]{:S(2)}) collective-permute-start(bf16[240,3584]{1,0:T(8,128)(2,1)} %bitcast.17), channel_id=1, source_target_pairs={{0,8},{8,0},{1,9},{9,1},{2,10},{10,2},{3,11},{11,3},{4,12},{12,4},... | collective-permute-start | bytes 5160968 | tf_op jit(solution)/shard_map/ppermute | solution.py:60
  29.5 9.3 %collective-permute-start = (bf16[128,896]{1,0:T(8,128)(2,1)S(1)}, bf16[128,896]{1,0:T(8,128)(2,1)S(1)}, u32[]{:S(2)}, u32[]{:S(2)}) collective-permute-start(bf16[128,896]{1,0:T(8,128)(2,1)S(1)} %get-tuple-element.55), channel_id=1, source_target_pairs={{0,2},{1,3},{2,4},{3,5},{4,6},{5,7},{6,0},{7,1},{8,10},{9,11},{10,... | collective-permute-start | bytes 688136 | tf_op jit(solution)/shard_map/ppermute | solution.py:65
  31.2 9.6 %collective-permute-start.1 = (bf16[128,896]{1,0:T(8,128)(2,1)S(1)}, bf16[128,896]{1,0:T(8,128)(2,1)S(1)}, u32[]{:S(2)}, u32[]{:S(2)}) collective-permute-start(bf16[128,896]{1,0:T(8,128)(2,1)S(1)} %get-tuple-element.56), channel_id=1, source_target_pairs={{0,6},{1,7},{2,0},{3,1},{4,2},{5,3},{6,4},{7,5},{8,14},{9,15},{10,... | collective-permute-start | bytes 688136 | tf_op jit(solution)/shard_map/ppermute | solution.py:65
  38.8 8.8 %collective-permute-start.2 = (bf16[128,896]{1,0:T(8,128)(2,1)S(1)}, bf16[128,896]{1,0:T(8,128)(2,1)S(1)}, u32[]{:S(2)}, u32[]{:S(2)}) collective-permute-start(bf16[128,896]{1,0:T(8,128)(2,1)S(1)} %get-tuple-element.57), channel_id=1, source_target_pairs={{0,4},{1,5},{2,6},{3,7},{4,0},{5,1},{6,2},{7,3},{8,12},{9,13},{10,... | collective-permute-start | bytes 688136 | tf_op jit(solution)/shard_map/ppermute | solution.py:65
  49.5 14.8 %collective-permute-start.3 = (bf16[320,896]{1,0:T(8,128)(2,1)S(1)}, bf16[320,896]{1,0:T(8,128)(2,1)S(1)}, u32[]{:S(2)}, u32[]{:S(2)}) collective-permute-start(bf16[320,896]{1,0:T(8,128)(2,1)S(1)} %compact.1.own), channel_id=1, source_target_pairs={{0,2},{1,3},{2,4},{3,5},{4,6},{5,7},{6,0},{7,1},{8,10},{9,11},{10,... | collective-permute-start | bytes 1720328 | tf_op jit(solution)/shard_map/ppermute | solution.py:65
  51.4 13.8 %collective-permute-start.4 = (bf16[320,896]{1,0:T(8,128)(2,1)S(1)}, bf16[320,896]{1,0:T(8,128)(2,1)S(1)}, u32[]{:S(2)}, u32[]{:S(2)}) collective-permute-start(bf16[320,896]{1,0:T(8,128)(2,1)S(1)} %compact.1.own), channel_id=1, source_target_pairs={{0,6},{1,7},{2,0},{3,1},{4,2},{5,3},{6,4},{7,5},{8,14},{9,15},{10,... | collective-permute-start | bytes 1720328 | tf_op jit(solution)/shard_map/ppermute | solution.py:65
  64.3 7.9 %collective-permute-start.5 = (bf16[160,896]{1,0:T(8,128)(2,1)S(1)}, bf16[160,896]{1,0:T(8,128)(2,1)S(1)}, u32[]{:S(2)}, u32[]{:S(2)}) collective-permute-start(bf16[160,896]{1,0:T(8,128)(2,1)S(1)} %slice.8), channel_id=1, source_target_pairs={{0,2},{1,3},{2,4},{3,5},{4,6},{5,7},{6,0},{7,1},{8,10},{9,11},{10,... | collective-permute-start | bytes 860168 | tf_op jit(solution)/shard_map/ppermute | solution.py:65
  65.2 7.0 %collective-permute-start.6 = (bf16[160,896]{1,0:T(8,128)(2,1)S(1)}, bf16[160,896]{1,0:T(8,128)(2,1)S(1)}, u32[]{:S(2)}, u32[]{:S(2)}) collective-permute-start(bf16[160,896]{1,0:T(8,128)(2,1)S(1)} %slice.9), channel_id=1, source_target_pairs={{0,6},{1,7},{2,0},{3,1},{4,2},{5,3},{6,4},{7,5},{8,14},{9,15},{10,... | collective-permute-start | bytes 860168 | tf_op jit(solution)/shard_map/ppermute | solution.py:65
  77.9 32.0 %copy-start.4 = (bf16[128,256]{1,0:T(8,128)(2,1)S(1)}, bf16[128,256]{1,0:T(8,128)(2,1)}, u32[]{:S(2)}) copy-start(bf16[128,256]{1,0:T(8,128)(2,1)} %own_q.1) | copy-start | bytes 196612
  77.9 11.3 %collective-permute-start.10 = (bf16[160,896]{1,0:T(8,128)(2,1)S(1)}, bf16[160,896]{1,0:T(8,128)(2,1)S(1)}, u32[]{:S(2)}, u32[]{:S(2)}) collective-permute-start(bf16[160,896]{1,0:T(8,128)(2,1)S(1)} %get-tuple-element.74), channel_id=1, source_target_pairs={{0,2},{1,3},{2,4},{3,5},{4,6},{5,7},{6,0},{7,1},{8,10},{9,11},{10,... | collective-permute-start | bytes 860168 | tf_op jit(solution)/shard_map/ppermute | solution.py:65
  79.4 11.3 %collective-permute-start.11 = (bf16[160,896]{1,0:T(8,128)(2,1)S(1)}, bf16[160,896]{1,0:T(8,128)(2,1)S(1)}, u32[]{:S(2)}, u32[]{:S(2)}) collective-permute-start(bf16[160,896]{1,0:T(8,128)(2,1)S(1)} %get-tuple-element.75), channel_id=1, source_target_pairs={{0,6},{1,7},{2,0},{3,1},{4,2},{5,3},{6,4},{7,5},{8,14},{9,15},{10,... | collective-permute-start | bytes 860168 | tf_op jit(solution)/shard_map/ppermute | solution.py:65
  81.6 10.9 %collective-permute-start.12 = (bf16[160,896]{1,0:T(8,128)(2,1)S(1)}, bf16[160,896]{1,0:T(8,128)(2,1)S(1)}, u32[]{:S(2)}, u32[]{:S(2)}) collective-permute-start(bf16[160,896]{1,0:T(8,128)(2,1)S(1)} %get-tuple-element.76), channel_id=1, source_target_pairs={{0,4},{1,5},{2,6},{3,7},{4,0},{5,1},{6,2},{7,3},{8,12},{9,13},{10,... | collective-permute-start | bytes 860168 | tf_op jit(solution)/shard_map/ppermute | solution.py:65
  93.3 5.4 %collective-permute-start.13 = (bf16[160,512]{1,0:T(8,128)(2,1)S(1)}, bf16[160,512]{1,0:T(8,128)(2,1)S(1)}, u32[]{:S(2)}, u32[]{:S(2)}) collective-permute-start(bf16[160,512]{1,0:T(8,128)(2,1)S(1)} %get-tuple-element.78), channel_id=1, source_target_pairs={{0,1},{1,0},{2,3},{3,2},{4,5},{5,4},{6,7},{7,6},{8,9},{9,8},{10,11... | collective-permute-start | bytes 491528 | tf_op jit(solution)/shard_map/ppermute | solution.py:65
  99.6 20.3 %all-to-all-start.1 = ((bf16[16,16,512]{2,1,0:T(8,128)(2,1)}), bf16[16,16,512]{2,1,0:T(8,128)(2,1)S(1)}, u32[]{:S(2)}, u32[]{:S(2)}) async-start(bf16[16,16,512]{2,1,0:T(8,128)(2,1)} %bitcast.8), calls=%async_computation.1 | async-start | bytes 524288 | tf_op jit(solution)/shard_map/all_to_all | solution.py:461
  108.9 5.6 %collective-permute-start.14 = (bf16[128,512]{1,0:T(8,128)(2,1)S(1)}, bf16[128,512]{1,0:T(8,128)(2,1)S(1)}, u32[]{:S(2)}, u32[]{:S(2)}) collective-permute-start(bf16[128,512]{1,0:T(8,128)(2,1)S(1)} %get-tuple-element.82), channel_id=1, source_target_pairs={{0,1},{1,0},{2,3},{3,2},{4,5},{5,4},{6,7},{7,6},{8,9},{9,8},{10,11... | collective-permute-start | bytes 393224 | tf_op jit(solution)/shard_map/ppermute | solution.py:65
  109.9 1.9 %copy-start = (bf16[2048,768]{1,0:T(8,128)(2,1)S(1)}, bf16[2048,768]{1,0:T(8,128)(2,1)}, u32[]{:S(2)}) copy-start(bf16[2048,768]{1,0:T(8,128)(2,1)} %all-gather.2.cloned.1.call-done.gathered) | copy-start | bytes 9437188
  114.5 23.1 %copy-start.2 = (bf16[128,3584]{1,0:T(8,128)(2,1)S(1)}, bf16[128,3584]{1,0:T(8,128)(2,1)}, u32[]{:S(2)}) copy-start(bf16[128,3584]{1,0:T(8,128)(2,1)} %grad_out.5) | copy-start | bytes 2752516
  114.5 23.1 %copy-start.3 = (bf16[128,3584]{1,0:T(8,128)(2,1)S(1)}, bf16[128,3584]{1,0:T(8,128)(2,1)}, u32[]{:S(2)}) copy-start(bf16[128,3584]{1,0:T(8,128)(2,1)} %hidden.3) | copy-start | bytes 2752516
  114.5 23.1 %copy-start.6 = (f32[3584]{0:T(1024)S(1)}, f32[3584]{0:T(1024)}, u32[]{:S(2)}) copy-start(f32[3584]{0:T(1024)} %gain.3) | copy-start | bytes 43012
  120.7 1.3 collective-permute-start.15
  135.7 25.2 %copy-start.1 = (bf16[2048,768]{1,0:T(8,128)(2,1)S(1)}, bf16[2048,768]{1,0:T(8,128)(2,1)}, u32[]{:S(2)}) copy-start(bf16[2048,768]{1,0:T(8,128)(2,1)} %all-gather.2.cloned.1.call-done.gathered) | copy-start | bytes 9437188
  135.7 1.9 %collective-permute-start.16 = (bf16[8,128,256]{2,1,0:T(8,128)(2,1)S(1)}, bf16[8,128,256]{2,1,0:T(8,128)(2,1)S(1)}, u32[]{:S(2)}, u32[]{:S(2)}) collective-permute-start(bf16[8,128,256]{2,1,0:T(8,128)(2,1)S(1)} %all_to_all.20.mine), channel_id=1, source_target_pairs={{0,8},{8,0},{1,9},{9,1},{2,10},{10,2},{3,11},{11,3},{4,12},{12,4},... | collective-permute-start | bytes 1572872 | tf_op jit(solution)/shard_map/ppermute | solution.py:60
  156.5 11.3 %collective-permute-start.19 = (bf16[4,144,256]{2,1,0:T(8,128)(2,1)S(1)}, bf16[4,144,256]{2,1,0:T(8,128)(2,1)S(1)}, u32[]{:S(2)}, u32[]{:S(2)}) collective-permute-start(bf16[4,144,256]{2,1,0:T(8,128)(2,1)S(1)} %all_to_all.21.grads.refs_0_), channel_id=1, source_target_pairs={{0,32},{16,48},{32,0},{48,16},{64,96},{80,112},{96,64},{112,80},{1... | collective-permute-start | bytes 884744 | tf_op jit(solution)/shard_map/ppermute | solution.py:69
  158.9 11.5 %collective-permute-start.17 = (bf16[4,144,256]{2,1,0:T(8,128)(2,1)S(1)}, bf16[4,144,256]{2,1,0:T(8,128)(2,1)S(1)}, u32[]{:S(2)}, u32[]{:S(2)}) collective-permute-start(bf16[4,144,256]{2,1,0:T(8,128)(2,1)S(1)} %all_to_all.21.grads.refs_0_), channel_id=1, source_target_pairs={{0,48},{16,0},{32,16},{48,32},{64,112},{80,64},{96,80},{112,96},{1... | collective-permute-start | bytes 884744 | tf_op jit(solution)/shard_map/ppermute | solution.py:69
  160.1 10.8 %collective-permute-start.18 = (bf16[4,144,256]{2,1,0:T(8,128)(2,1)S(1)}, bf16[4,144,256]{2,1,0:T(8,128)(2,1)S(1)}, u32[]{:S(2)}, u32[]{:S(2)}) collective-permute-start(bf16[4,144,256]{2,1,0:T(8,128)(2,1)S(1)} %all_to_all.21.grads.refs_0_), channel_id=1, source_target_pairs={{0,16},{16,32},{32,48},{48,0},{64,80},{80,96},{96,112},{112,64},{1... | collective-permute-start | bytes 884744 | tf_op jit(solution)/shard_map/ppermute | solution.py:69
Sparse Core Ops, SparseCore 0:
  13.7 74.6 all-gather.1

commit v5 on v4

--- a/solution.py
+++ b/solution.py
@@ -71,8 +71,10 @@
 
 def sum_over_y(me, parts, name):
     size = shape(parts[0].shape[0], CHUNK)
+    order = ((2, 2), (1, 1), (3, -1)) if name == "dense_sum" else ((1, 1), (3, -1), (2, 2))
+    moved = [to_ep(parts[n], dy, 0) for n, dy in order]
     return call(sum_kernel, (size, size), [SMEM] + [VMEM] * 4, name=name)(
-        me, parts[0], to_ep(parts[1], 1, 0), to_ep(parts[3], -1, 0), to_ep(parts[2], 2, 0)
+        me, parts[0], *moved
     )
 
 

time: 181 us -> 181 us (level)
    ppermute x12, waiting for transfers between devices: 39.3 us -> 37.2 us  [to_ep(): return lax.ppermute(x, 'ep', pairs)]
  transfers between devices with their start and end apart: 23 -> 23, of which waited for: 15 -> 16; matrix products, arithmetic and copies ran while one was open for 0% -> 0% of each run, Pallas kernels for 14% -> 14%
where the time goes in v5:
time: 181 us; the launch traced here: 180 us
  waiting for transfers between devices  52.7 us (29%)
  starting transfers between devices  44.8 us (25%)
  Pallas kernels  35.5 us (20%)
  blocking collectives  29 us (16%)
  between operations  14.2 us (8%)
  local copies, waits for them, and re-layouts  4.08 us (2%)
    ppermute x12, waiting for transfers between devices, to_ep(): return lax.ppermute(x, 'ep', pairs)  37.2 us
    ppermute x12, starting transfers between devices, to_ep(): return lax.ppermute(x, 'ep', pairs)  19.8 us
    all_to_all x1, blocking collectives, body(): lax.all_to_all(message, 'ctx', split_axis=0, concat_axis=0, tiled=True, a...  15.4 us
    all_to_all x1, blocking collectives, body(): total = lax.all_to_all(total, 'ep', split_axis=0, concat_axis=0, tiled=True)  13.6 us
    all_to_all x1, starting transfers between devices, body(): came = lax.all_to_all(send, 'ctx', split_axis=0, concat_axis=0, tiled=True)  10.1 us
    all_to_all x1, starting transfers between devices, body(): lax.all_to_all(back.reshape(16, 16, CHUNK), 'ctx', split_axis=0, concat_a...  9.53 us
    pallas_call x1, Pallas kernels, body(): call(expert_kernel, (shape(160, PIECE),) * 4, [SMEM] + [VMEM] * 11, scrat...  5.66 us
    ppermute x3, waiting for transfers between devices, to_ctx(): lax.ppermute(x, 'ctx', [(z * 4 + q, z * 4 + (q + dx) % 4) for z in range(...  5.5 us
  transfers between devices with their start and end apart: 23, of which 16 were waited for; matrix products, arithmetic and copies ran while one was open for 0% of the time, Pallas kernels for 14%

profile of v5, /device:TPU:32, one launch (start us, length us, event | category | flops | bytes accessed | tf_op | source)
XLA Modules:
  0.0 180.3 jit_solution(17582896171530519953)
XLA Ops:
  9.4 4.1 %prepare.1 = (bf16[128,3584]{1,0:T(8,128)(2,1)S(1)}, bf16[16,24,896]{2,1,0:T(8,128)(2,1)}, bf16[256,128]{1,0:T(8,128)(2,1)S(1)}, bf16[128,768]{1,0:T(8,128)(2,1)}) custom-call(s32[3]{0:T(128)S(1)} %pad_add_fusion.me, bf16[128,3584]{1,0:T(8,128)(2,1)} %hidden.3, bf16[128,3584]{1,0:T(8,128)(2,1)} %grad_out.5, f32[3584]{0:T(1024)S(1)} %copy-done.5, ...), custom_call_target="tpu_custom_call" | custom-call | flops 100000000 | bytes 4000000 | tf_op jit(solution)/shard_map/prepare/pallas_call | solution.py:412
  13.5 10.1 %all-to-all-start = ((bf16[16,24,896]{2,1,0:T(8,128)(2,1)}), bf16[16,24,896]{2,1,0:T(8,128)(2,1)S(1)}, u32[]{:S(2)}, u32[]{:S(2)}) async-start(bf16[16,24,896]{2,1,0:T(8,128)(2,1)} %get-tuple-element.52), calls=%async_computation | async-start | bytes 1376256 | tf_op jit(solution)/shard_map/all_to_all | solution.py:423
  24.4 5.1 %dense.1 = (bf16[128,896]{1,0:T(8,128)(2,1)S(1)}, bf16[128,896]{1,0:T(8,128)(2,1)S(1)}, bf16[128,896]{1,0:T(8,128)(2,1)S(1)}, bf16[128,896]{1,0:T(8,128)(2,1)S(1)}) custom-call(s32[3]{0:T(128)S(1)} %pad_add_fusion.me, bf16[128,3584]{1,0:T(8,128)(2,1)S(1)} %get-tuple-element.53.mixed, bf16[128,3584]{1,0:T(8,128)(2,1)} %grad_out.5, bf16[152,3584]{1,0:T(8,128)(2,1)} %gate_in.1, ...), custom_call_target="tpu_custom_call" | custom-call | flops 697303040 | bytes 6000000 | tf_op jit(solution)/shard_map/dense/pallas_call | solution.py:425
  29.5 3.3 %collective-permute-start = (bf16[128,896]{1,0:T(8,128)(2,1)S(1)}, bf16[128,896]{1,0:T(8,128)(2,1)S(1)}, u32[]{:S(2)}, u32[]{:S(2)}) collective-permute-start(bf16[128,896]{1,0:T(8,128)(2,1)S(1)} %get-tuple-element.55), channel_id=1, source_target_pairs={{0,4},{1,5},{2,6},{3,7},{4,0},{5,1},{6,2},{7,3},{8,12},{9,13},{10,... | collective-permute-start | bytes 688136 | tf_op jit(solution)/shard_map/ppermute | solution.py:65
  33.5 6.1 %collective-permute-done.second = bf16[128,896]{1,0:T(8,128)(2,1)S(1)} collective-permute-done((bf16[128,896]{1,0:T(8,128)(2,1)S(1)}, bf16[128,896]{1,0:T(8,128)(2,1)S(1)}, u32[]{:S(2)}, u32[]{:S(2)}) %collective-permute-start) | collective-permute-done | bytes 229408 | tf_op jit(solution)/shard_map/ppermute | solution.py:65
  39.5 2.5 %collective-permute-start.2 = (bf16[128,896]{1,0:T(8,128)(2,1)S(1)}, bf16[128,896]{1,0:T(8,128)(2,1)S(1)}, u32[]{:S(2)}, u32[]{:S(2)}) collective-permute-start(bf16[128,896]{1,0:T(8,128)(2,1)S(1)} %get-tuple-element.57), channel_id=1, source_target_pairs={{0,6},{1,7},{2,0},{3,1},{4,2},{5,3},{6,4},{7,5},{8,14},{9,15},{10,... | collective-permute-start | bytes 688136 | tf_op jit(solution)/shard_map/ppermute | solution.py:65
  42.1 1.9 %collective-permute-done.1.third = bf16[128,896]{1,0:T(8,128)(2,1)S(1)} collective-permute-done((bf16[128,896]{1,0:T(8,128)(2,1)S(1)}, bf16[128,896]{1,0:T(8,128)(2,1)S(1)}, u32[]{:S(2)}, u32[]{:S(2)}) %collective-permute-start.1) | collective-permute-done | bytes 229408 | tf_op jit(solution)/shard_map/ppermute | solution.py:65
  44.0 2.9 %collective-permute-done.2.fourth = bf16[128,896]{1,0:T(8,128)(2,1)S(1)} collective-permute-done((bf16[128,896]{1,0:T(8,128)(2,1)S(1)}, bf16[128,896]{1,0:T(8,128)(2,1)S(1)}, u32[]{:S(2)}, u32[]{:S(2)}) %collective-permute-start.2) | collective-permute-done | bytes 229408 | tf_op jit(solution)/shard_map/ppermute | solution.py:65
  47.5 1.5 all-to-all-done.came
  49.5 1.8 %collective-permute-start.3 = (bf16[320,896]{1,0:T(8,128)(2,1)S(1)}, bf16[320,896]{1,0:T(8,128)(2,1)S(1)}, u32[]{:S(2)}, u32[]{:S(2)}) collective-permute-start(bf16[320,896]{1,0:T(8,128)(2,1)S(1)} %compact.1.own), channel_id=1, source_target_pairs={{0,2},{1,3},{2,4},{3,5},{4,6},{5,7},{6,0},{7,1},{8,10},{9,11},{10,... | collective-permute-start | bytes 1720328 | tf_op jit(solution)/shard_map/ppermute | solution.py:65
  51.4 1.5 collective-permute-start.4
  52.9 11.4 %collective-permute-done.3.right = bf16[320,896]{1,0:T(8,128)(2,1)S(1)} collective-permute-done((bf16[320,896]{1,0:T(8,128)(2,1)S(1)}, bf16[320,896]{1,0:T(8,128)(2,1)S(1)}, u32[]{:S(2)}, u32[]{:S(2)}) %collective-permute-start.3) | collective-permute-done | bytes 573472 | tf_op jit(solution)/shard_map/ppermute | solution.py:65
  65.2 2.7 %collective-permute-start.6 = (bf16[160,896]{1,0:T(8,128)(2,1)S(1)}, bf16[160,896]{1,0:T(8,128)(2,1)S(1)}, u32[]{:S(2)}, u32[]{:S(2)}) collective-permute-start(bf16[160,896]{1,0:T(8,128)(2,1)S(1)} %slice.9), channel_id=1, source_target_pairs={{0,6},{1,7},{2,0},{3,1},{4,2},{5,3},{6,4},{7,5},{8,14},{9,15},{10,... | collective-permute-start | bytes 860168 | tf_op jit(solution)/shard_map/ppermute | solution.py:65
  67.9 4.1 %load.1 = (bf16[240,3584]{1,0:T(8,128)(2,1)S(1)}, bf16[240,3584]{1,0:T(8,128)(2,1)S(1)}, bf16[240,3584]{1,0:T(8,128)(2,1)S(1)}, bf16[240,3584]{1,0:T(8,128)(2,1)...) custom-call(bf16[240,3584]{1,0:T(8,128)(2,1)} %bitcast.14, bf16[240,3584]{1,0:T(8,128)(2,1)} %bitcast.16, ...), custom_call_target="tpu_custom_call" | custom-call | bytes 10000000 | tf_op jit(solution)/shard_map/load/pallas_call | solution.py:443
  72.3 5.7 %expert.1 = (bf16[160,896]{1,0:T(8,128)(2,1)S(1)}, bf16[160,896]{1,0:T(8,128)(2,1)S(1)}, bf16[160,896]{1,0:T(8,128)(2,1)S(1)}, bf16[160,896]{1,0:T(8,128)(2,1)S(1)}) custom-call(s32[3]{0:T(128)S(1)} %pad_add_fusion.me, bf16[320,896]{1,0:T(8,128)(2,1)S(1)} %compact.1.own, bf16[320,896]{1,0:T(8,128)(2,1)S(1)} %collective-permute-done.3.right, ...), custom_call_target="tpu_custom_call" | custom-call | flops 2752512000 | bytes 18000000 | tf_op jit(solution)/shard_map/expert/pallas_call | solution.py:451
  79.4 2.2 %collective-permute-start.11 = (bf16[160,896]{1,0:T(8,128)(2,1)S(1)}, bf16[160,896]{1,0:T(8,128)(2,1)S(1)}, u32[]{:S(2)}, u32[]{:S(2)}) collective-permute-start(bf16[160,896]{1,0:T(8,128)(2,1)S(1)} %get-tuple-element.75), channel_id=1, source_target_pairs={{0,6},{1,7},{2,0},{3,1},{4,2},{5,3},{6,4},{7,5},{8,14},{9,15},{10,... | collective-permute-start | bytes 860168 | tf_op jit(solution)/shard_map/ppermute | solution.py:65
  83.0 6.2 %collective-permute-done.10.second = bf16[160,896]{1,0:T(8,128)(2,1)S(1)} collective-permute-done((bf16[160,896]{1,0:T(8,128)(2,1)S(1)}, bf16[160,896]{1,0:T(8,128)(2,1)S(1)}, u32[]{:S(2)}, u32[]{:S(2)}) %collective-permute-start.10) | collective-permute-done | bytes 286752 | tf_op jit(solution)/shard_map/ppermute | solution.py:65
  89.2 1.5 collective-permute-done.11.third
  90.7 1.8 %collective-permute-done.12.fourth = bf16[160,896]{1,0:T(8,128)(2,1)S(1)} collective-permute-done((bf16[160,896]{1,0:T(8,128)(2,1)S(1)}, bf16[160,896]{1,0:T(8,128)(2,1)S(1)}, u32[]{:S(2)}, u32[]{:S(2)}) %collective-permute-start.12) | collective-permute-done | bytes 286752 | tf_op jit(solution)/shard_map/ppermute | solution.py:65
  93.5 5.1 %collective-permute-done.13.came = bf16[160,512]{1,0:T(8,128)(2,1)S(1)} collective-permute-done((bf16[160,512]{1,0:T(8,128)(2,1)S(1)}, bf16[160,512]{1,0:T(8,128)(2,1)S(1)}, u32[]{:S(2)}, u32[]{:S(2)}) %collective-permute-start.13) | collective-permute-done | bytes 163872 | tf_op jit(solution)/shard_map/ppermute | solution.py:65
  99.6 9.5 %all-to-all-start.1 = ((bf16[16,16,512]{2,1,0:T(8,128)(2,1)}), bf16[16,16,512]{2,1,0:T(8,128)(2,1)S(1)}, u32[]{:S(2)}, u32[]{:S(2)}) async-start(bf16[16,16,512]{2,1,0:T(8,128)(2,1)} %bitcast.8), calls=%async_computation.1 | async-start | bytes 524288 | tf_op jit(solution)/shard_map/all_to_all | solution.py:463
  110.2 1.9 %copy-done = bf16[2048,768]{1,0:T(8,128)(2,1)S(1)} copy-done((bf16[2048,768]{1,0:T(8,128)(2,1)S(1)}, bf16[2048,768]{1,0:T(8,128)(2,1)}, u32[]{:S(2)}) %copy-start) | copy-done | bytes 3145752
  112.1 2.7 %stats.1 = (f32[8,128]{1,0:T(8,128)S(1)}, f32[2,128,128]{2,1,0:T(8,128)S(1)}) custom-call(s32[3]{0:T(128)S(1)} %pad_add_fusion.me, bf16[128,256]{1,0:T(8,128)(2,1)S(1)} %copy-done.4, bf16[2048,768]{1,0:T(8,128)(2,1)S(1)} %copy-done), custom_call_target="tpu_custom_call" | custom-call | flops 268435456 | bytes 4000000 | tf_op jit(solution)/shard_map/stats/pallas_call | solution.py:465
  114.9 5.3 %all-to-all-done.1 = bf16[16,16,512]{2,1,0:T(8,128)(2,1)S(1)} async-done(((bf16[16,16,512]{2,1,0:T(8,128)(2,1)}), bf16[16,16,512]{2,1,0:T(8,128)(2,1)S(1)}, u32[]{:S(2)}, u32[]{:S(2)}) %all-to-all-start.1) | async-done | bytes 262176 | tf_op jit(solution)/shard_map/all_to_all | solution.py:463
  122.4 13.6 %all_to_all.20.mine = bf16[8,128,256]{2,1,0:T(8,128)(2,1)S(1)} all-to-all(bf16[8,128,256]{2,1,0:T(8,128)(2,1)S(1)} %broadcast_in_dim.2), channel_id=1, replica_groups=mesh['ctx'=16,'tp'=2,'ep'=8] {'ep'}, dimensions={0} | all-to-all | bytes 1048576 | tf_op jit(solution)/shard_map/all_to_all | solution.py:484
  136.0 1.9 %collective-permute-done.16.other = bf16[8,128,256]{2,1,0:T(8,128)(2,1)S(1)} collective-permute-done((bf16[8,128,256]{2,1,0:T(8,128)(2,1)S(1)}, bf16[8,128,256]{2,1,0:T(8,128)(2,1)S(1)}, u32[]{:S(2)}, u32[]{:S(2)}) %collective-permute-start.16) | collective-permute-done | bytes 524320 | tf_op jit(solution)/shard_map/ppermute | solution.py:60
  137.9 3.4 %norm.1 = (bf16[128,3584]{1,0:T(8,128)(2,1)}, bf16[4,144,256]{2,1,0:T(8,128)(2,1)S(1)}) custom-call(s32[3]{0:T(128)S(1)} %pad_add_fusion.me, bf16[128,3584]{1,0:T(8,128)(2,1)S(1)} %copy-done.3, bf16[128,3584]{1,0:T(8,128)(2,1)S(1)} %copy-done.2, f32[3584]{0:T(1024)S(1)} %copy-done.6, bf16[8,128,256]{2,1,0:T(8,128)(2,1)S(1)} %all_to_all.20.mine, ...), custom_call_target="tpu_custom_call" | custom-call | flops 469762048 | bytes 6000000 | tf_op jit(solution)/shard_map/norm/pallas_call | solution.py:485
  141.3 15.4 %all_to_all.21.grads.refs_0_ = bf16[4,144,256]{2,1,0:T(8,128)(2,1)S(1)} all-to-all(bf16[4,144,256]{2,1,0:T(8,128)(2,1)S(1)} %get-tuple-element.91), channel_id=1, replica_groups={{0,64,128,192},{16,80,144,208},{32,96,160,224},{48,112,176,240},{1,65,1..., dimensions={0} | all-to-all | bytes 589824 | tf_op jit(solution)/shard_map/all_to_all | solution.py:495
  156.7 2.5 %collective-permute-start.19 = (bf16[4,144,256]{2,1,0:T(8,128)(2,1)S(1)}, bf16[4,144,256]{2,1,0:T(8,128)(2,1)S(1)}, u32[]{:S(2)}, u32[]{:S(2)}) collective-permute-start(bf16[4,144,256]{2,1,0:T(8,128)(2,1)S(1)} %all_to_all.21.grads.refs_0_), channel_id=1, source_target_pairs={{0,32},{16,48},{32,0},{48,16},{64,96},{80,112},{96,64},{112,80},{1... | collective-permute-start | bytes 884744 | tf_op jit(solution)/shard_map/ppermute | solution.py:69
  162.4 1.9 %queries.3 = bf16[128,256]{1,0:T(8,128)(2,1)} custom-call(s32[3]{0:T(128)S(1)} %pad_add_fusion.me, bf16[128,256]{1,0:T(8,128)(2,1)S(1)} %copy-done.4, bf16[2048,768]{1,0:T(8,128)(2,1)S(1)} %copy-done.1, bf16[4,144,256]{2,1,0:T(8,128)(2,1)S(1)} %all_to_all.21.grads.refs_0_), custom_call_target="tpu_custom_call" | custom-call | flops 201326592 | bytes 4000000 | tf_op jit(solution)/shard_map/queries/pallas_call | solution.py:496
  164.4 3.6 %collective-permute-done.19.refs_0_ = bf16[4,144,256]{2,1,0:T(8,128)(2,1)S(1)} collective-permute-done((bf16[4,144,256]{2,1,0:T(8,128)(2,1)S(1)}, bf16[4,144,256]{2,1,0:T(8,128)(2,1)S(1)}, u32[]{:S(2)}, u32[]{:S(2)}) %collective-permute-start.19) | collective-permute-done | bytes 294944 | tf_op jit(solution)/shard_map/ppermute | solution.py:69
  171.1 2.4 %keys.7 = (bf16[128,256]{1,0:T(8,128)(2,1)}, bf16[128,256]{1,0:T(8,128)(2,1)}) custom-call(s32[3]{0:T(128)S(1)} %pad_add_fusion.me, bf16[2048,768]{1,0:T(8,128)(2,1)S(1)} %copy-done.1, bf16[4,144,256]{2,1,0:T(8,128)(2,1)S(1)} %collective-permute-done.17.refs_0_, bf16[4,144,256]{2,1,0:T(8,128)(2,1)S(1)} %collective-permute-done.18.refs_1_, ...), custom_call_target="tpu_custom_call" | custom-call | flops 268435456 | bytes 4000000 | tf_op jit(solution)/shard_map/keys/pallas_call | solution.py:508
  (55 shorter events, 20.3 us)
Async XLA Ops:
  7.2 103.1 %all-gather.2.cloned.1.call-start = ((), (), s32[]{:S(2)}) async-start(), calls=%async_computation.4 | async-start | bytes 3342336 | tf_op jit(solution)/shard_map/all_gather | solution.py:422
  7.3 0.7 copy-start.5
  8.0 0.7 copy-start.7
  8.7 0.7 copy-start.8
  13.5 35.5 %all-to-all-start = ((bf16[16,24,896]{2,1,0:T(8,128)(2,1)}), bf16[16,24,896]{2,1,0:T(8,128)(2,1)S(1)}, u32[]{:S(2)}, u32[]{:S(2)}) async-start(bf16[16,24,896]{2,1,0:T(8,128)(2,1)} %get-tuple-element.52), calls=%async_computation | async-start | bytes 1376256 | tf_op jit(solution)/shard_map/all_to_all | solution.py:423
  23.7 44.2 %collective-permute-start.7 = (bf16[240,3584]{1,0:T(8,128)(2,1)}, bf16[240,3584]{1,0:T(8,128)(2,1)}, u32[]{:S(2)}, u32[]{:S(2)}) collective-permute-start(bf16[240,3584]{1,0:T(8,128)(2,1)} %bitcast.13), channel_id=1, source_target_pairs={{0,8},{8,0},{1,9},{9,1},{2,10},{10,2},{3,11},{11,3},{4,12},{12,4},... | collective-permute-start | bytes 5160968 | tf_op jit(solution)/shard_map/ppermute | solution.py:60
  23.8 44.1 %collective-permute-start.8 = (bf16[240,3584]{1,0:T(8,128)(2,1)}, bf16[240,3584]{1,0:T(8,128)(2,1)}, u32[]{:S(2)}, u32[]{:S(2)}) collective-permute-start(bf16[240,3584]{1,0:T(8,128)(2,1)} %bitcast.15), channel_id=1, source_target_pairs={{0,8},{8,0},{1,9},{9,1},{2,10},{10,2},{3,11},{11,3},{4,12},{12,4},... | collective-permute-start | bytes 5160968 | tf_op jit(solution)/shard_map/ppermute | solution.py:60
  24.3 43.6 %collective-permute-start.9 = (bf16[240,3584]{1,0:T(8,128)(2,1)}, bf16[240,3584]{1,0:T(8,128)(2,1)}, u32[]{:S(2)}, u32[]{:S(2)}) collective-permute-start(bf16[240,3584]{1,0:T(8,128)(2,1)} %bitcast.17), channel_id=1, source_target_pairs={{0,8},{8,0},{1,9},{9,1},{2,10},{10,2},{3,11},{11,3},{4,12},{12,4},... | collective-permute-start | bytes 5160968 | tf_op jit(solution)/shard_map/ppermute | solution.py:60
  29.5 10.0 %collective-permute-start = (bf16[128,896]{1,0:T(8,128)(2,1)S(1)}, bf16[128,896]{1,0:T(8,128)(2,1)S(1)}, u32[]{:S(2)}, u32[]{:S(2)}) collective-permute-start(bf16[128,896]{1,0:T(8,128)(2,1)S(1)} %get-tuple-element.55), channel_id=1, source_target_pairs={{0,4},{1,5},{2,6},{3,7},{4,0},{5,1},{6,2},{7,3},{8,12},{9,13},{10,... | collective-permute-start | bytes 688136 | tf_op jit(solution)/shard_map/ppermute | solution.py:65
  32.8 11.2 %collective-permute-start.1 = (bf16[128,896]{1,0:T(8,128)(2,1)S(1)}, bf16[128,896]{1,0:T(8,128)(2,1)S(1)}, u32[]{:S(2)}, u32[]{:S(2)}) collective-permute-start(bf16[128,896]{1,0:T(8,128)(2,1)S(1)} %get-tuple-element.56), channel_id=1, source_target_pairs={{0,2},{1,3},{2,4},{3,5},{4,6},{5,7},{6,0},{7,1},{8,10},{9,11},{10,... | collective-permute-start | bytes 688136 | tf_op jit(solution)/shard_map/ppermute | solution.py:65
  39.5 7.3 %collective-permute-start.2 = (bf16[128,896]{1,0:T(8,128)(2,1)S(1)}, bf16[128,896]{1,0:T(8,128)(2,1)S(1)}, u32[]{:S(2)}, u32[]{:S(2)}) collective-permute-start(bf16[128,896]{1,0:T(8,128)(2,1)S(1)} %get-tuple-element.57), channel_id=1, source_target_pairs={{0,6},{1,7},{2,0},{3,1},{4,2},{5,3},{6,4},{7,5},{8,14},{9,15},{10,... | collective-permute-start | bytes 688136 | tf_op jit(solution)/shard_map/ppermute | solution.py:65
  49.5 14.8 %collective-permute-start.3 = (bf16[320,896]{1,0:T(8,128)(2,1)S(1)}, bf16[320,896]{1,0:T(8,128)(2,1)S(1)}, u32[]{:S(2)}, u32[]{:S(2)}) collective-permute-start(bf16[320,896]{1,0:T(8,128)(2,1)S(1)} %compact.1.own), channel_id=1, source_target_pairs={{0,2},{1,3},{2,4},{3,5},{4,6},{5,7},{6,0},{7,1},{8,10},{9,11},{10,... | collective-permute-start | bytes 1720328 | tf_op jit(solution)/shard_map/ppermute | solution.py:65
  51.4 13.8 %collective-permute-start.4 = (bf16[320,896]{1,0:T(8,128)(2,1)S(1)}, bf16[320,896]{1,0:T(8,128)(2,1)S(1)}, u32[]{:S(2)}, u32[]{:S(2)}) collective-permute-start(bf16[320,896]{1,0:T(8,128)(2,1)S(1)} %compact.1.own), channel_id=1, source_target_pairs={{0,6},{1,7},{2,0},{3,1},{4,2},{5,3},{6,4},{7,5},{8,14},{9,15},{10,... | collective-permute-start | bytes 1720328 | tf_op jit(solution)/shard_map/ppermute | solution.py:65
  64.3 7.9 %collective-permute-start.5 = (bf16[160,896]{1,0:T(8,128)(2,1)S(1)}, bf16[160,896]{1,0:T(8,128)(2,1)S(1)}, u32[]{:S(2)}, u32[]{:S(2)}) collective-permute-start(bf16[160,896]{1,0:T(8,128)(2,1)S(1)} %slice.8), channel_id=1, source_target_pairs={{0,2},{1,3},{2,4},{3,5},{4,6},{5,7},{6,0},{7,1},{8,10},{9,11},{10,... | collective-permute-start | bytes 860168 | tf_op jit(solution)/shard_map/ppermute | solution.py:65
  65.2 7.0 %collective-permute-start.6 = (bf16[160,896]{1,0:T(8,128)(2,1)S(1)}, bf16[160,896]{1,0:T(8,128)(2,1)S(1)}, u32[]{:S(2)}, u32[]{:S(2)}) collective-permute-start(bf16[160,896]{1,0:T(8,128)(2,1)S(1)} %slice.9), channel_id=1, source_target_pairs={{0,6},{1,7},{2,0},{3,1},{4,2},{5,3},{6,4},{7,5},{8,14},{9,15},{10,... | collective-permute-start | bytes 860168 | tf_op jit(solution)/shard_map/ppermute | solution.py:65
  77.9 32.3 %copy-start.4 = (bf16[128,256]{1,0:T(8,128)(2,1)S(1)}, bf16[128,256]{1,0:T(8,128)(2,1)}, u32[]{:S(2)}) copy-start(bf16[128,256]{1,0:T(8,128)(2,1)} %own_q.1) | copy-start | bytes 196612
  77.9 11.3 %collective-permute-start.10 = (bf16[160,896]{1,0:T(8,128)(2,1)S(1)}, bf16[160,896]{1,0:T(8,128)(2,1)S(1)}, u32[]{:S(2)}, u32[]{:S(2)}) collective-permute-start(bf16[160,896]{1,0:T(8,128)(2,1)S(1)} %get-tuple-element.74), channel_id=1, source_target_pairs={{0,2},{1,3},{2,4},{3,5},{4,6},{5,7},{6,0},{7,1},{8,10},{9,11},{10,... | collective-permute-start | bytes 860168 | tf_op jit(solution)/shard_map/ppermute | solution.py:65
  79.4 11.3 %collective-permute-start.11 = (bf16[160,896]{1,0:T(8,128)(2,1)S(1)}, bf16[160,896]{1,0:T(8,128)(2,1)S(1)}, u32[]{:S(2)}, u32[]{:S(2)}) collective-permute-start(bf16[160,896]{1,0:T(8,128)(2,1)S(1)} %get-tuple-element.75), channel_id=1, source_target_pairs={{0,6},{1,7},{2,0},{3,1},{4,2},{5,3},{6,4},{7,5},{8,14},{9,15},{10,... | collective-permute-start | bytes 860168 | tf_op jit(solution)/shard_map/ppermute | solution.py:65
  81.6 10.9 %collective-permute-start.12 = (bf16[160,896]{1,0:T(8,128)(2,1)S(1)}, bf16[160,896]{1,0:T(8,128)(2,1)S(1)}, u32[]{:S(2)}, u32[]{:S(2)}) collective-permute-start(bf16[160,896]{1,0:T(8,128)(2,1)S(1)} %get-tuple-element.76), channel_id=1, source_target_pairs={{0,4},{1,5},{2,6},{3,7},{4,0},{5,1},{6,2},{7,3},{8,12},{9,13},{10,... | collective-permute-start | bytes 860168 | tf_op jit(solution)/shard_map/ppermute | solution.py:65
  93.3 5.4 %collective-permute-start.13 = (bf16[160,512]{1,0:T(8,128)(2,1)S(1)}, bf16[160,512]{1,0:T(8,128)(2,1)S(1)}, u32[]{:S(2)}, u32[]{:S(2)}) collective-permute-start(bf16[160,512]{1,0:T(8,128)(2,1)S(1)} %get-tuple-element.78), channel_id=1, source_target_pairs={{0,1},{1,0},{2,3},{3,2},{4,5},{5,4},{6,7},{7,6},{8,9},{9,8},{10,11... | collective-permute-start | bytes 491528 | tf_op jit(solution)/shard_map/ppermute | solution.py:65
  99.6 20.6 %all-to-all-start.1 = ((bf16[16,16,512]{2,1,0:T(8,128)(2,1)}), bf16[16,16,512]{2,1,0:T(8,128)(2,1)S(1)}, u32[]{:S(2)}, u32[]{:S(2)}) async-start(bf16[16,16,512]{2,1,0:T(8,128)(2,1)} %bitcast.8), calls=%async_computation.1 | async-start | bytes 524288 | tf_op jit(solution)/shard_map/all_to_all | solution.py:463
  109.2 5.7 %collective-permute-start.14 = (bf16[128,512]{1,0:T(8,128)(2,1)S(1)}, bf16[128,512]{1,0:T(8,128)(2,1)S(1)}, u32[]{:S(2)}, u32[]{:S(2)}) collective-permute-start(bf16[128,512]{1,0:T(8,128)(2,1)S(1)} %get-tuple-element.82), channel_id=1, source_target_pairs={{0,1},{1,0},{2,3},{3,2},{4,5},{5,4},{6,7},{7,6},{8,9},{9,8},{10,11... | collective-permute-start | bytes 393224 | tf_op jit(solution)/shard_map/ppermute | solution.py:65
  110.2 1.9 %copy-start = (bf16[2048,768]{1,0:T(8,128)(2,1)S(1)}, bf16[2048,768]{1,0:T(8,128)(2,1)}, u32[]{:S(2)}) copy-start(bf16[2048,768]{1,0:T(8,128)(2,1)} %all-gather.2.cloned.1.call-done.gathered) | copy-start | bytes 9437188
  114.8 23.1 %copy-start.2 = (bf16[128,3584]{1,0:T(8,128)(2,1)S(1)}, bf16[128,3584]{1,0:T(8,128)(2,1)}, u32[]{:S(2)}) copy-start(bf16[128,3584]{1,0:T(8,128)(2,1)} %grad_out.5) | copy-start | bytes 2752516
  114.9 23.1 %copy-start.3 = (bf16[128,3584]{1,0:T(8,128)(2,1)S(1)}, bf16[128,3584]{1,0:T(8,128)(2,1)}, u32[]{:S(2)}) copy-start(bf16[128,3584]{1,0:T(8,128)(2,1)} %hidden.3) | copy-start | bytes 2752516
  114.9 23.1 %copy-start.6 = (f32[3584]{0:T(1024)S(1)}, f32[3584]{0:T(1024)}, u32[]{:S(2)}) copy-start(f32[3584]{0:T(1024)} %gain.3) | copy-start | bytes 43012
  120.9 1.3 collective-permute-start.15
  136.0 25.2 %copy-start.1 = (bf16[2048,768]{1,0:T(8,128)(2,1)S(1)}, bf16[2048,768]{1,0:T(8,128)(2,1)}, u32[]{:S(2)}) copy-start(bf16[2048,768]{1,0:T(8,128)(2,1)} %all-gather.2.cloned.1.call-done.gathered) | copy-start | bytes 9437188
  136.0 1.9 %collective-permute-start.16 = (bf16[8,128,256]{2,1,0:T(8,128)(2,1)S(1)}, bf16[8,128,256]{2,1,0:T(8,128)(2,1)S(1)}, u32[]{:S(2)}, u32[]{:S(2)}) collective-permute-start(bf16[8,128,256]{2,1,0:T(8,128)(2,1)S(1)} %all_to_all.20.mine), channel_id=1, source_target_pairs={{0,8},{8,0},{1,9},{9,1},{2,10},{10,2},{3,11},{11,3},{4,12},{12,4},... | collective-permute-start | bytes 1572872 | tf_op jit(solution)/shard_map/ppermute | solution.py:60
  156.7 11.3 %collective-permute-start.19 = (bf16[4,144,256]{2,1,0:T(8,128)(2,1)S(1)}, bf16[4,144,256]{2,1,0:T(8,128)(2,1)S(1)}, u32[]{:S(2)}, u32[]{:S(2)}) collective-permute-start(bf16[4,144,256]{2,1,0:T(8,128)(2,1)S(1)} %all_to_all.21.grads.refs_0_), channel_id=1, source_target_pairs={{0,32},{16,48},{32,0},{48,16},{64,96},{80,112},{96,64},{112,80},{1... | collective-permute-start | bytes 884744 | tf_op jit(solution)/shard_map/ppermute | solution.py:69
  159.2 11.5 %collective-permute-start.17 = (bf16[4,144,256]{2,1,0:T(8,128)(2,1)S(1)}, bf16[4,144,256]{2,1,0:T(8,128)(2,1)S(1)}, u32[]{:S(2)}, u32[]{:S(2)}) collective-permute-start(bf16[4,144,256]{2,1,0:T(8,128)(2,1)S(1)} %all_to_all.21.grads.refs_0_), channel_id=1, source_target_pairs={{0,48},{16,0},{32,16},{48,32},{64,112},{80,64},{96,80},{112,96},{1... | collective-permute-start | bytes 884744 | tf_op jit(solution)/shard_map/ppermute | solution.py:69
  160.3 10.8 %collective-permute-start.18 = (bf16[4,144,256]{2,1,0:T(8,128)(2,1)S(1)}, bf16[4,144,256]{2,1,0:T(8,128)(2,1)S(1)}, u32[]{:S(2)}, u32[]{:S(2)}) collective-permute-start(bf16[4,144,256]{2,1,0:T(8,128)(2,1)S(1)} %all_to_all.21.grads.refs_0_), channel_id=1, source_target_pairs={{0,16},{16,32},{32,48},{48,0},{64,80},{80,96},{96,112},{112,64},{1... | collective-permute-start | bytes 884744 | tf_op jit(solution)/shard_map/ppermute | solution.py:69
Sparse Core Ops, SparseCore 0:
  13.7 74.6 all-gather.1
